TPU v7x, 128 devices: a whole 4x4x4 slice. The times are simulated.
128 devices in a mesh: exp: 8 (over x_lo, z), ten: 16 (over y, x_hi, core).
Axes of the slice: x: 4 (x_hi: 2, x_lo: 2; x = x_hi * 2 + x_lo), y: 4, z: 4, core: 2. Of those that a mesh axis runs over, the one named last changes fastest.
Arguments:
- master_gate_up: float32 [8, 2, 1536, 4096], P('exp', None, None, 'ten'), may hold values from -0.09375 to 0.09375
- grad_gate_up: float32 [8, 2, 1536, 4096], P('exp', None, None, 'ten'), may hold values from -24 to 24
- first_gate_up: float32 [8, 2, 1536, 4096], P('exp', None, None, 'ten'), may hold values from -3 to 3
- second_gate_up: float32 [8, 2, 1536, 4096], P('exp', None, None, 'ten'), may hold values from 1 to 16
- master_down: float32 [8, 1536, 4096], P('exp', None, 'ten'), may hold values from -0.15625 to 0.15625
- grad_down: float32 [8, 1536, 4096], P('exp', None, 'ten'), may hold values from -24 to 24
- first_down: float32 [8, 1536, 4096], P('exp', None, 'ten'), may hold values from -3 to 3
- second_down: float32 [8, 1536, 4096], P('exp', None, 'ten'), may hold values from 1 to 16
- tokens: bfloat16 [4096, 4096], P(('exp', 'ten')), may hold values from -6 to 6
- route_ids: int32 [4096, 2], P(('exp', 'ten')), may hold values from 0 to 7, all different within a row; in each aligned block of 32 rows (0 to 31, 32 to 63, ...) at most 12 rows name the same one
- route_weights: float32 [4096, 2], P(('exp', 'ten')), may hold values from 0.2 to 1
Outputs:
- new_master_gate_up: float32 [8, 2, 1536, 4096], P('exp', None, None, 'ten')
- new_master_down: float32 [8, 1536, 4096], P('exp', None, 'ten')
- rollout_gate_up: bfloat16 [8, 2, 1536, 4096], P('exp', None, 'ten')
- rollout_down: bfloat16 [8, 1536, 4096], P('exp', 'ten')
- moe_out: bfloat16 [4096, 4096], P(('exp', 'ten'))
Inputs may be any that keep to these rules, and one draw needn't show every extreme that they name: `route_ids`: within one device's block of 32 rows no expert is named by more than 12 entries, a bound that some block reaches; a row names 2 different experts.
All inputs are finite; a program needn't handle non-finite values.
Results may differ from a plain program's by a relative error of at most 0.0033.
The roundings to bfloat16 on the way count: a program that leaves them out, or rounds other values in their place, can miss the bound.
Values may be sent and summed in bfloat16 or wider, within the bound.
No kernel may reach another device: no remote copies, remote signals or barrier semaphores. Data moves between devices by JAX's collectives and lax.ppermute only.
A program may use at most 192 MiB of HBM per device.

v0:
```python
import jax
import jax.numpy as jnp
from jax import lax
from jax.sharding import PartitionSpec as P

beta_first = 0.9
beta_second = 0.95
learn_rate = 0.01
weight_decay = 0.1
adam_epsilon = 1e-08
bias_first = 1.0 - 0.9**50
bias_second = 1.0 - 0.95**50


def adamw_update(master, grads, first, second):
    moment_one = beta_first * first + (1.0 - beta_first) * grads
    moment_two = beta_second * second + (1.0 - beta_second) * grads * grads
    scaled = moment_one / bias_first / (jnp.sqrt(moment_two / bias_second) + adam_epsilon)
    return master - learn_rate * (scaled + weight_decay * master)


def body(
    master_gate_up,
    grad_gate_up,
    first_gate_up,
    second_gate_up,
    master_down,
    grad_down,
    first_down,
    second_down,
    tokens,
    route_ids,
    route_weights,
):
    new_master_gate_up = adamw_update(master_gate_up, grad_gate_up, first_gate_up, second_gate_up)
    new_master_down = adamw_update(master_down, grad_down, first_down, second_down)
    send_gate_up = new_master_gate_up.astype(jnp.bfloat16)
    hidden_units = send_gate_up.shape[2]
    local_width = send_gate_up.shape[3]
    local_down = new_master_down.astype(jnp.bfloat16)
    send_down = local_down.reshape(1, 1, hidden_units, local_width)
    rollout_gate_up, down_four = (
        lax.all_to_all(send_gate_up, "ten", split_axis=2, concat_axis=3, tiled=True),
        lax.all_to_all(send_down, "ten", split_axis=2, concat_axis=3, tiled=True),
    )
    rollout_down = down_four.reshape(1, down_four.shape[2], down_four.shape[3])
    owners = lax.axis_size("exp")
    rows_here = tokens.shape[0]
    width = tokens.shape[1]
    top_count = route_ids.shape[1]
    capacity = 3 * rows_here * top_count // (2 * owners)
    flat_ids = route_ids.reshape(-1)
    onehot = (flat_ids[:, None] == jnp.arange(owners, dtype=jnp.int32)[None, :]).astype(jnp.int32)
    earlier = jnp.cumsum(onehot, axis=0) - onehot
    position = jnp.sum(earlier * onehot, axis=1)
    slot_index = flat_ids * capacity + position
    selector = slot_index[:, None] == jnp.arange(owners * capacity, dtype=jnp.int32)[None, :]
    placing = jnp.sum(
        selector.reshape(rows_here, top_count, owners * capacity).astype(jnp.float32), axis=1
    )
    dispatch = jnp.dot(placing.T.astype(jnp.bfloat16), tokens, preferred_element_type=jnp.float32)
    dispatch = dispatch.astype(jnp.bfloat16).reshape(owners, capacity, width)
    received = lax.all_to_all(dispatch, "exp", split_axis=0, concat_axis=0, tiled=True).reshape(
        owners * capacity, width
    )
    gate_weights = rollout_gate_up[0, 0]
    up_weights = rollout_gate_up[0, 1]
    contract = (((1,), (1,)), ((), ()))
    piece = lax.all_gather(received, "ten", axis=0, tiled=True)
    gate = lax.dot_general(piece, gate_weights, contract, preferred_element_type=jnp.float32)
    up = lax.dot_general(piece, up_weights, contract, preferred_element_type=jnp.float32)
    hidden = (jax.nn.silu(gate) * up).astype(jnp.bfloat16)
    expert_out = lax.psum_scatter(
        jnp.dot(hidden, rollout_down[0], preferred_element_type=jnp.float32),
        "ten",
        scatter_dimension=0,
        tiled=True,
    ).astype(jnp.bfloat16)
    returned = expert_out.reshape(owners, capacity, width)
    back = lax.all_to_all(returned, "exp", split_axis=0, concat_axis=0, tiled=True).reshape(
        owners * capacity, width
    )
    weighted = selector.astype(jnp.float32) * route_weights.reshape(-1)[:, None]
    combining = jnp.sum(weighted.reshape(rows_here, top_count, owners * capacity), axis=1)
    moe_out = jnp.dot(combining, back.astype(jnp.float32), precision=lax.Precision.HIGHEST).astype(
        jnp.bfloat16
    )
    return (new_master_gate_up, new_master_down, rollout_gate_up, rollout_down, moe_out)


def solution(mesh):
    return jax.shard_map(
        body,
        mesh=mesh,
        in_specs=(
            P("exp", None, None, "ten"),
            P("exp", None, None, "ten"),
            P("exp", None, None, "ten"),
            P("exp", None, None, "ten"),
            P("exp", None, "ten"),
            P("exp", None, "ten"),
            P("exp", None, "ten"),
            P("exp", None, "ten"),
            P(("exp", "ten"), None),
            P(("exp", "ten"), None),
            P(("exp", "ten"), None),
        ),
        out_specs=(
            P("exp", None, None, "ten"),
            P("exp", None, "ten"),
            P("exp", None, "ten", None),
            P("exp", "ten", None),
            P(("exp", "ten"), None),
        ),
        check_vma=False,
    )
```

profile of v0, /device:TPU:0, one launch (start us, length us, event | category | flops | bytes accessed | tf_op | source)
XLA Modules:
  0.0 389.4 jit_solution(10869380531667194808)
XLA Ops:
  7.2 0.0 copy-start
  7.2 0.0 all-gather.2.cloned.1.call-start
  7.2 0.8 copy.93
  8.0 0.1 eq.30
  8.1 0.1 fusion.21
  8.2 0.1 reduce_window_sum.11
  8.3 0.2 select_reduce_fusion.1
  8.5 0.1 reduce_sum.30
  8.6 0.1 copy.94
  8.7 0.7 multiply_add_fusion
  9.4 0.8 convert_reduce_fusion
  10.2 0.4 convolution_convert_fusion
  10.5 0.2 reshape.66
  10.7 21.9 %all_to_all.43 = bf16[8,12,4096]{2,1,0:T(8,128)(2,1)S(1)} all-to-all(bf16[8,12,4096]{2,1,0:T(8,128)(2,1)S(1)} %reshape.66), channel_id=1, replica_groups=mesh['exp'=8,'ten'=16] {'exp'}, dimensions={0} | all-to-all | bytes 1572864 | tf_op jit(solution)/shard_map/all_to_all | solution.py:63
  32.6 1.1 reshape.67
  33.7 0.0 all-gather.2.cloned.1.call-update
  33.7 5.2 %convert_bitcast_fusion = (bf16[1,1,1536,256]{3,2,1,0:T(8,128)(2,1)S(1)}, f32[1,1536,256]{2,1,0:T(8,128)}) fusion(f32[1,1536,256]{2,1,0:T(8,128)} %param.15, f32[1,1536,256]{2,1,0:T(8,128)} %param.16, f32[1,1536,256]{2,1,0:T(8,128)} %param.18, f32[1,1536,256]{2,1,0:T(8,128)} %param.17), kind=kLoop, calls=%fused_computation.24 | loop fusion | flops 6291456 | bytes 8650752 | tf_op jit(solution)/shard_map/reshape | solution.py:41
  38.9 8.8 %copy.100 = bf16[1,1,1536,256]{3,1,0,2:T(2,128)(2,1)S(1)} copy(bf16[1,1,1536,256]{3,2,1,0:T(8,128)(2,1)S(1)} %get-tuple-element.27) | data formatting | bytes 1572864 | tf_op jit(solution)/shard_map/reshape | solution.py:41
  47.7 0.5 broadcast.46
  48.2 8.1 %reduce = bf16[1536,256]{1,0:T(8,128)(2,1)S(1)} reduce(bf16[1536,1,1,256]{3,2,1,0:T(2,128)(2,1)S(1)} %bitcast.38, bf16[]{:T(256)} %broadcast.46), dimensions={1,2}, to_apply=%bitcast.34.reduce_sub_computation | reduce | bytes 1572866
  56.3 1.1 reshape.70
  57.4 6.7 %all-to-all-start.1 = ((bf16[16,2,12288]{2,1,0:T(2,128)(2,1)}), bf16[16,2,12288]{2,1,0:T(2,128)(2,1)S(1)}, u32[]{:S(2)}, u32[]{:S(2)}) async-start(bf16[16,2,12288]{2,1,0:T(2,128)(2,1)} %reshape.70), calls=%async_computation.1 | async-start | bytes 1572864 | tf_op jit(solution)/shard_map/all_to_all | solution.py:44
  64.1 7.0 %fusion.24 = (bf16[1,2,1536,256]{3,2,1,0:T(8,128)(2,1)S(1)}, f32[1,2,1536,256]{3,2,1,0:T(8,128)}) fusion(f32[1,2,1536,256]{3,2,1,0:T(8,128)} %param.11, f32[1,2,1536,256]{3,2,1,0:T(8,128)} %param.12, f32[1,2,1536,256]{3,2,1,0:T(8,128)} %param.14, f32[1,2,1536,256]{3,2,1,0:T(8,128)} %param.13), kind=kLoop, calls=%fused_computation.40 | loop fusion | flops 12582912 | bytes 17301504 | tf_op jit(solution)/shard_map/convert_element_type | solution.py:37
  71.1 10.7 %copy.89 = bf16[1,2,1536,256]{3,1,0,2:T(2,128)(2,1)} copy(bf16[1,2,1536,256]{3,2,1,0:T(8,128)(2,1)S(1)} %get-tuple-element.29) | data formatting | bytes 3145728 | tf_op jit(solution)/shard_map/convert_element_type | solution.py:37
  81.8 0.0 all-to-all-done.1
  81.8 7.2 %all-to-all-start = ((bf16[1,2,1536,256]{3,1,0,2:T(2,128)(2,1)}), bf16[1,2,1536,256]{3,1,0,2:T(2,128)(2,1)S(1)}, u32[]{:S(2)}, u32[]{:S(2)}) async-start(bf16[1,2,1536,256]{3,1,0,2:T(2,128)(2,1)} %copy.89), calls=%async_computation | async-start | bytes 3145728 | tf_op jit(solution)/shard_map/all_to_all | solution.py:43
  89.0 0.2 reduce-scatter.2.cloned.1.call-start
  89.2 2.1 reshape.71
  91.3 1.5 copy.96
  92.8 0.1 copy.97
  92.9 36.9 %all-to-all-done = bf16[1,2,1536,256]{3,1,0,2:T(2,128)(2,1)S(1)} async-done(((bf16[1,2,1536,256]{3,1,0,2:T(2,128)(2,1)}), bf16[1,2,1536,256]{3,1,0,2:T(2,128)(2,1)S(1)}, u32[]{:S(2)}, u32[]{:S(2)}) %all-to-all-start) | async-done | bytes 1572896 | tf_op jit(solution)/shard_map/all_to_all | solution.py:43
  129.8 2.0 copy.90
  131.8 2.6 all_to_all.33
  134.4 0.0 copy-start.2
  134.4 8.1 %all-gather.2.cloned.1.call-done = bf16[1536,4096]{1,0:T(8,128)(2,1)} async-done(((bf16[96,4096]{1,0:T(8,128)(2,1)}), bf16[1536,4096]{1,0:T(8,128)(2,1)}) %all-gather.2.cloned.1.call-update) | async-done | bytes 12582928 | tf_op jit(solution)/shard_map/all_gather | solution.py:69
  142.5 9.4 %fusion.14 = f32[1536,96]{0,1:T(8,128)} fusion(bf16[1536,4096]{1,0:T(8,128)(2,1)} %all-gather.2.cloned.1.call-done, bf16[1,2,96,4096]{3,2,1,0:T(8,128)(2,1)S(1)} %all_to_all.33), kind=kOutput, calls=%fused_computation.23 | convolution fusion | flops 1207959552 | bytes 13959168 | tf_op jit(solution)/shard_map/dot_general | solution.py:70
  151.9 20.5 %fusion.7 = f32[1536,4096]{1,0:T(8,128)} fusion(bf16[96,4096]{1,0:T(8,128)(2,1)S(1)} %bitcast.40, bf16[1536,4096]{1,0:T(8,128)(2,1)} %all-gather.2.cloned.1.call-done, bf16[1,2,96,4096]{3,2,1,0:T(8,128)(2,1)S(1)} %all_to_all.33, f32[1536,96]{0,1:T(8,128)} %fusion.14), kind=kOutput, calls=%fused_computation.13 | convolution fusion | flops 2416803840 | bytes 39911424 | tf_op jit(solution)/shard_map/dot_general | solution.py:74
  172.4 0.0 reduce-scatter.2.cloned.1.call-update
  172.4 187.5 %reduce-scatter.2.cloned.1.call-done = f32[96,4096]{1,0:T(8,128)} async-done(((f32[1536,4096]{1,0:T(8,128)}), f32[96,4096]{1,0:T(8,128)}) %reduce-scatter.2.cloned.1.call-update) | async-done | bytes 1572880 | tf_op jit(solution)/shard_map/reduce_scatter | solution.py:73
  359.9 1.5 convert_element_type.37
  361.4 1.2 reshape.68
  362.5 4.4 %all-to-all-start.3 = ((bf16[8,12,4096]{2,1,0:T(8,128)(2,1)}), bf16[8,12,4096]{2,1,0:T(8,128)(2,1)S(1)}, u32[]{:S(2)}, u32[]{:S(2)}) async-start(bf16[8,12,4096]{2,1,0:T(8,128)(2,1)} %reshape.68), calls=%async_computation.4 | async-start | bytes 2097152 | tf_op jit(solution)/shard_map/all_to_all | solution.py:80
  367.0 0.4 copy.92
  367.4 0.0 copy-start.1
  367.4 1.2 reshape.65
  368.7 12.6 %all-to-all-done.3 = bf16[8,12,4096]{2,1,0:T(8,128)(2,1)S(1)} async-done(((bf16[8,12,4096]{2,1,0:T(8,128)(2,1)}), bf16[8,12,4096]{2,1,0:T(8,128)(2,1)S(1)}, u32[]{:S(2)}, u32[]{:S(2)}) %all-to-all-start.3) | async-done | bytes 786464 | tf_op jit(solution)/shard_map/all_to_all | solution.py:80
  381.2 0.2 reshape.69
  381.4 1.1 convolution_convert_fusion.1
  (3 shorter events, 0.0 us)
Async XLA Ops:
  7.2 3.0 copy-start
  7.2 135.4 %all-gather.2.cloned.1.call-start = ((), (), s32[]{:S(2)}) async-start(), calls=%async_computation.5 | async-start | bytes 13369344 | tf_op jit(solution)/shard_map/all_gather | solution.py:69
  57.4 24.4 %all-to-all-start.1 = ((bf16[16,2,12288]{2,1,0:T(2,128)(2,1)}), bf16[16,2,12288]{2,1,0:T(2,128)(2,1)S(1)}, u32[]{:S(2)}, u32[]{:S(2)}) async-start(bf16[16,2,12288]{2,1,0:T(2,128)(2,1)} %reshape.70), calls=%async_computation.1 | async-start | bytes 1572864 | tf_op jit(solution)/shard_map/all_to_all | solution.py:44
  81.8 48.0 %all-to-all-start = ((bf16[1,2,1536,256]{3,1,0,2:T(2,128)(2,1)}), bf16[1,2,1536,256]{3,1,0,2:T(2,128)(2,1)S(1)}, u32[]{:S(2)}, u32[]{:S(2)}) async-start(bf16[1,2,1536,256]{3,1,0,2:T(2,128)(2,1)} %copy.89), calls=%async_computation | async-start | bytes 3145728 | tf_op jit(solution)/shard_map/all_to_all | solution.py:43
  89.0 270.9 %reduce-scatter.2.cloned.1.call-start = ((), (), s32[]{:S(2)}) async-start(), calls=%async_computation.6 | async-start | bytes 26738688 | tf_op jit(solution)/shard_map/reduce_scatter | solution.py:73
  134.4 17.5 %copy-start.2 = (bf16[1,2,96,4096]{3,2,1,0:T(8,128)(2,1)}, bf16[1,2,96,4096]{3,2,1,0:T(8,128)(2,1)S(1)}, u32[]{:S(2)}) copy-start(bf16[1,2,96,4096]{3,2,1,0:T(8,128)(2,1)S(1)} %all_to_all.33) | copy-start | bytes 4718596
  362.5 18.7 %all-to-all-start.3 = ((bf16[8,12,4096]{2,1,0:T(8,128)(2,1)}), bf16[8,12,4096]{2,1,0:T(8,128)(2,1)S(1)}, u32[]{:S(2)}, u32[]{:S(2)}) async-start(bf16[8,12,4096]{2,1,0:T(8,128)(2,1)} %reshape.68), calls=%async_computation.4 | async-start | bytes 2097152 | tf_op jit(solution)/shard_map/all_to_all | solution.py:80
  367.4 15.2 %copy-start.1 = (bf16[32,4096]{1,0:T(8,128)(2,1)S(1)}, bf16[32,4096]{1,0:T(8,128)(2,1)}, u32[]{:S(2)}) copy-start(bf16[32,4096]{1,0:T(8,128)(2,1)} %param.19) | copy-start | bytes 786436
Sparse Core Ops, SparseCore 0:
  33.9 108.6 all-gather.1
  172.5 187.3 reduce-scatter.1
where the time goes:
time: 390 us; the launch traced here: 389 us
  waiting for transfers between devices  245 us (63%)
  local copies, waits for them, and re-layouts  34.6 us (9%)
  matrix products  31.4 us (8%)
  other arithmetic  23.6 us (6%)
  blocking collectives  21.9 us (6%)
  starting transfers between devices  18.6 us (5%)
  between operations  14.2 us (4%)
    reduce_scatter x1, waiting for transfers between devices, body(): lax.psum_scatter(jnp.dot(hidden, rollout_down[0], preferred_element_type=...  187 us
    all_to_all x1, waiting for transfers between devices, body(): lax.all_to_all(send_gate_up, 'ten', split_axis=2, concat_axis=3, tiled=True)  36.9 us
    all_to_all x1, blocking collectives, body(): lax.all_to_all(dispatch, 'exp', split_axis=0, concat_axis=0, tiled=True)  21.9 us
    dot_general x1, matrix products, body(): jnp.dot(hidden, rollout_down[0], preferred_element_type=jnp.float32)  20.5 us
    all_to_all x1, waiting for transfers between devices, body(): lax.all_to_all(returned, 'exp', split_axis=0, concat_axis=0, tiled=True)  12.6 us
    convert_element_type x1, local copies, waits for them, and re-layouts, body(): send_gate_up = new_master_gate_up.astype(jnp.bfloat16)  10.7 us
    dot_general x1, matrix products, body(): lax.dot_general(piece, gate_weights, contract, preferred_element_type=jnp...  9.37 us
    reshape x1, local copies, waits for them, and re-layouts, body(): send_down = local_down.reshape(1, 1, hidden_units, local_width)  8.75 us
  transfers between devices with their start and end apart: 5, of which 4 were waited for; matrix products, arithmetic and copies ran while one was open for 12% of the time, Pallas kernels for 0%

commit v1 on v0

v1 whole, which is shorter than its diff:
```python
import functools

import jax
import jax.numpy as jnp
from jax import lax
from jax.experimental import pallas as pl
from jax.experimental.pallas import tpu as pltpu
from jax.sharding import PartitionSpec as P

beta_first = 0.9
beta_second = 0.95
learn_rate = 0.01
weight_decay = 0.1
adam_epsilon = 1e-08
bias_first = 1.0 - 0.9**50
bias_second = 1.0 - 0.95**50

F32 = jnp.float32
BF16 = jnp.bfloat16
VMEM = pl.BlockSpec(memory_space=pltpu.VMEM)
SMEM = pl.BlockSpec(memory_space=pltpu.SMEM)
ANY = pl.BlockSpec(memory_space=pl.ANY)
NT = (((1,), (1,)), ((), ()))

SHIFTS = (0, -1, 1, 2)
SLOTS = 12
PAIR = 2 * SLOTS


def adamw_update(master, grads, first, second):
    moment_one = beta_first * first + (1.0 - beta_first) * grads
    moment_two = beta_second * second + (1.0 - beta_second) * grads * grads
    scaled = moment_one * (1.0 / bias_first)
    scaled = scaled / (jnp.sqrt(moment_two * (1.0 / bias_second)) + adam_epsilon)
    return master - learn_rate * (scaled + weight_decay * master)


def params(mib=32):
    return pltpu.CompilerParams(vmem_limit_bytes=mib << 20)


def cost(flops, nbytes):
    return pl.CostEstimate(flops=int(flops), bytes_accessed=int(nbytes), transcendentals=0)


def move(array, target):
    pairs = []
    for i in range(128):
        xl, z, y, xh, core = i // 64, i // 16 % 4, i // 4 % 4, i // 2 % 2, i % 2
        a, b, c, d, f = target(xl, z, y, xh, core)
        pairs.append((i, ((a * 4 + b % 4) * 4 + c % 4) * 4 + d * 2 + f))
    return lax.ppermute(array, ("exp", "ten"), pairs)


def move_y(array, shift):
    return move(array, lambda xl, z, y, xh, core: (xl, z, y + shift, xh, core))


def move_xh(array):
    return move(array, lambda xl, z, y, xh, core: (xl, z, y, 1 - xh, core))


def move_core(array):
    return move(array, lambda xl, z, y, xh, core: (xl, z, y, xh, 1 - core))


def move_out(array, k):
    return move(array, lambda xl, z, y, xh, core: (core, z + k, y, xh, xl))


def move_home(array, k):
    return move(array, lambda xl, z, y, xh, core: (core, z - k, y, xh, xl))


def staged(arrays):
    return lax.optimization_barrier(arrays)


def after(arrays, others):
    return lax.optimization_barrier((arrays, others))[0]


def adam_kernel(count, parts, rows, blocks_ref, *refs):
    ins, rest = refs[:4], refs[4:]
    new_ref, pieces = rest[-(count + 5)], rest[-(count + 4) : -4]
    held_ref, made_ref, in_sem, out_sem = rest[-4:]
    steps = [(i, part) for i in range(count) for part in range(parts)]

    def at(ref, step):
        i, part = steps[step]
        return ref.at[0, part, pl.ds(pl.multiple_of(blocks_ref[i] * rows, rows), rows)]

    copies = [
        [
            pltpu.make_async_copy(at(ref, step), held_ref.at[step, j], in_sem.at[step, j])
            for j, ref in enumerate(ins)
        ]
        for step in range(len(steps))
    ]
    for step in copies:
        for copy in step:
            copy.start()
    outs = []
    for step, (i, part) in enumerate(steps):
        for copy in copies[step]:
            copy.wait()

        def some(r, carry, step=step, i=i, part=part):
            at_rows = pl.ds(pl.multiple_of(r * 32, 32), 32)
            new = adamw_update(*(held_ref[step, j, at_rows] for j in range(4)))
            made_ref[step, at_rows] = new
            pieces[i][part, at_rows] = new.astype(BF16)
            return carry

        lax.fori_loop(0, rows // 32, some, 0)
        out = pltpu.make_async_copy(made_ref.at[step], at(new_ref, step), out_sem.at[step])
        out.start()
        outs.append(out)
    for out in outs:
        out.wait()


def adam(blocks, arrays, target, rows):
    count, parts = blocks.shape[0], arrays[0].shape[1]
    given = [] if target is None else [target]
    return pl.pallas_call(
        functools.partial(adam_kernel, count, parts, rows),
        in_specs=[SMEM] + [ANY] * (4 + len(given)),
        out_specs=[ANY] + [VMEM] * count,
        out_shape=[jax.ShapeDtypeStruct(arrays[0].shape, F32)]
        + [jax.ShapeDtypeStruct((parts, rows, 256), BF16)] * count,
        scratch_shapes=[
            pltpu.VMEM((count * parts, 4, rows, 256), F32),
            pltpu.VMEM((count * parts, rows, 256), F32),
            pltpu.SemaphoreType.DMA((count * parts, 4)),
            pltpu.SemaphoreType.DMA((count * parts,)),
        ],
        input_output_aliases={5: 0} if given else {},
        cost_estimate=cost(0, count * parts * rows * 256 * 22),
        compiler_params=params(56),
        name="adam",
    )(blocks, *arrays, *given)


def slot_parts(slot):
    k = (slot >= PAIR).astype(jnp.int32) + (slot >= 2 * PAIR) + (slot >= 3 * PAIR)
    rest = slot - PAIR * k
    half = (rest >= SLOTS).astype(jnp.int32)
    return k, half, rest - SLOTS * half


def routing(where_ref, meta):
    rows = meta.shape[0]
    expert = lax.broadcasted_iota(jnp.int32, (rows, 128), 1).astype(F32)
    first = meta[:, 0:1] == expert
    second = meta[:, 1:2] == expert
    named = jnp.where(first | second, 1.0, 0.0)
    row = lax.broadcasted_iota(jnp.int32, (rows, rows), 0)
    column = lax.broadcasted_iota(jnp.int32, (rows, rows), 1)
    before = jnp.where(column < row, 1.0, 0.0)
    place = jnp.dot(before.astype(BF16), named.astype(BF16), preferred_element_type=F32)
    place = jnp.where(named > 0.0, place, 99.0)
    weight = jnp.where(first, meta[:, 2:3], 0.0) + jnp.where(second, meta[:, 3:4], 0.0)
    return place, weight


def expert_of_slot(where_ref):
    slot = lax.broadcasted_iota(jnp.int32, (96, 128), 0)
    expert = lax.broadcasted_iota(jnp.int32, (96, 128), 1)
    k, _, _ = slot_parts(slot)
    z = where_ref[4] + k
    z = jnp.where(z >= 4, z - 4, z)
    return jnp.where(expert == where_ref[2] * 4 + z, 1.0, 0.0).astype(BF16)


def dispatch_kernel(where_ref, own_ref, other_ref, own_meta_ref, other_meta_ref, *outs):
    at_expert = expert_of_slot(where_ref)
    slot = lax.broadcasted_iota(jnp.int32, (96, 32), 0)
    _, half, place_of_slot = slot_parts(slot)
    total = None
    for side, (rows_ref, meta_ref) in enumerate(
        ((own_ref, own_meta_ref), (other_ref, other_meta_ref))
    ):
        place, _ = routing(where_ref, meta_ref[...])
        found = lax.dot_general(at_expert, place.astype(BF16), NT, preferred_element_type=F32)
        hit = (found == place_of_slot.astype(F32)) & (half == side)
        placing = jnp.where(hit, 1.0, 0.0).astype(BF16)
        part = jnp.dot(placing, rows_ref[...], preferred_element_type=F32)
        total = part if total is None else total + part
    for k in range(4):
        outs[k][...] = total[k * PAIR : (k + 1) * PAIR].astype(BF16)


def dispatch(where, own, other, own_meta, other_meta):
    return pl.pallas_call(
        dispatch_kernel,
        in_specs=[SMEM] + [VMEM] * 4,
        out_specs=[VMEM] * 4,
        out_shape=[jax.ShapeDtypeStruct((PAIR, 4096), BF16)] * 4,
        cost_estimate=cost(2 * 96 * 64 * 4096, 4 << 20),
        compiler_params=params(),
        name="dispatch",
    )(where, own, other, own_meta, other_meta)


def combine_kernel(where_ref, own_meta_ref, other_meta_ref, *rest):
    backs, (own_ref, other_ref) = rest[:4], rest[4:]
    at_expert = expert_of_slot(where_ref)
    slot = lax.broadcasted_iota(jnp.int32, (32, 96), 1)
    _, half, place_of_slot = slot_parts(slot)
    parts = []
    for side, meta_ref in enumerate((own_meta_ref, other_meta_ref)):
        place, weight = routing(where_ref, meta_ref[...])
        found = lax.dot_general(place.astype(BF16), at_expert, NT, preferred_element_type=F32)
        hit = (found == place_of_slot.astype(F32)) & (half == side)
        left = weight
        for _ in range(3):
            piece = left.astype(BF16)
            left = left - piece.astype(F32)
            spread = lax.dot_general(piece, at_expert, NT, preferred_element_type=F32)
            parts.append(jnp.where(hit, spread, 0.0))
    mixing = jnp.concatenate(parts, axis=0).astype(BF16)
    for g, shift in enumerate(SHIFTS):
        lanes = pl.ds(g * 1024, 1024)
        back = jnp.concatenate([b[:, lanes].astype(F32) for b in backs], axis=0).astype(BF16)
        mixed = jnp.dot(mixing, back, preferred_element_type=F32)
        columns = pl.ds(pl.multiple_of(wrap(where_ref[0] - shift) * 1024, 1024), 1024)
        own_ref[:, columns] = mixed[0:32] + mixed[32:64] + mixed[64:96]
        other_ref[:, columns] = mixed[96:128] + mixed[128:160] + mixed[160:192]


def combine(where, own_meta, other_meta, backs):
    return pl.pallas_call(
        combine_kernel,
        in_specs=[SMEM] + [VMEM] * 6,
        out_specs=[VMEM] * 2,
        out_shape=[jax.ShapeDtypeStruct((32, 4096), F32)] * 2,
        cost_estimate=cost(2 * 192 * 96 * 4096, 2 << 20),
        compiler_params=params(),
        name="combine",
    )(where, own_meta, other_meta, *backs)


def wrap(y):
    y = jnp.where(y >= 4, y - 4, y)
    return jnp.where(y < 0, y + 4, y)


def first_kernel(where_ref, *refs):
    rows, pieces = refs[:8], refs[8:24]
    hidden_ref, rollout_ref, x_ref, w_ref, acc_ref, x_sem, w_sem, out_sem = refs[24:]
    y, xh, core = where_ref[0], where_ref[1], where_ref[2]
    x_copies = [
        pltpu.make_async_copy(rows[i], x_ref.at[pl.ds(i * 48, 48)], x_sem.at[i]) for i in range(8)
    ]
    w_copies = []
    for i in range(16):
        group, s = i // 4, i % 4
        from_y = wrap(y + SHIFTS[s])
        from_xh = xh if group % 2 == 0 else 1 - xh
        from_core = core if group < 2 else 1 - core
        columns = pl.ds(pl.multiple_of((from_y * 4 + from_xh * 2 + from_core) * 256, 256), 256)
        w_copies.append(pltpu.make_async_copy(pieces[i], w_ref.at[:, :, columns], w_sem.at[i]))
    for copy in x_copies:
        copy.start()
    for s in range(4):
        for group in range(4):
            w_copies[group * 4 + s].start()
    for copy in x_copies:
        copy.wait()
    for s in range(4):
        for group in range(4):
            w_copies[group * 4 + s].wait()
        columns = pl.ds(pl.multiple_of(wrap(y + SHIFTS[s]) * 1024, 1024), 1024)
        for g in range(2):
            product = lax.dot_general(
                x_ref[:, columns], w_ref[g, :, columns], NT, preferred_element_type=F32
            )
            if s == 0:
                acc_ref[g] = product
            else:
                acc_ref[g] += product
    out = pltpu.make_async_copy(
        w_ref.at[:, pl.ds(pl.multiple_of((xh * 2 + core) * 96, 96), 96), :],
        rollout_ref.at[0],
        out_sem,
    )
    out.start()
    gate, up = acc_ref[0], acc_ref[1]
    hidden_ref[...] = (gate / (1.0 + jnp.exp(-gate)) * up).astype(BF16)
    out.wait()


def first_matmul(where, rows, pieces):
    return pl.pallas_call(
        first_kernel,
        in_specs=[SMEM] + [ANY] * 24,
        out_specs=[VMEM, ANY],
        out_shape=[
            jax.ShapeDtypeStruct((384, 384), BF16),
            jax.ShapeDtypeStruct((1, 2, 96, 4096), BF16),
        ],
        scratch_shapes=[
            pltpu.VMEM((384, 4096), BF16),
            pltpu.VMEM((2, 384, 4096), BF16),
            pltpu.VMEM((2, 384, 384), F32),
            pltpu.SemaphoreType.DMA((8,)),
            pltpu.SemaphoreType.DMA((16,)),
            pltpu.SemaphoreType.DMA,
        ],
        cost_estimate=cost(2 * 384 * 768 * 4096, 11 << 20),
        compiler_params=params(),
        name="first_matmul",
    )(where, *rows, *pieces)


def second_kernel(where_ref, *refs):
    hidden, downs = refs[:4], refs[4:8]
    outs, slices = refs[8:12], refs[12:16]
    h_ref, d_ref, h_sem, d_sem, out_sem = refs[16:]
    y, xh, core = where_ref[0], where_ref[1], where_ref[2]
    copies = []
    for i in range(4):
        from_xh = xh if i % 2 == 0 else 1 - xh
        from_core = core if i < 2 else 1 - core
        columns = pl.ds(pl.multiple_of((from_xh * 2 + from_core) * 256, 256), 256)
        copies.append(pltpu.make_async_copy(downs[i], d_ref.at[:, columns], d_sem.at[i]))
    h_copies = []
    for d, shift in enumerate(SHIFTS):
        columns = pl.ds(pl.multiple_of(wrap(y + shift) * 384, 128), 384)
        for g, origin in enumerate(SHIFTS):
            there = [(s - origin + shift) % 4 for s in SHIFTS].index(0)
            h_copies.append(
                pltpu.make_async_copy(
                    hidden[d].at[pl.ds(there * 96, 96)],
                    h_ref.at[pl.ds(g * 96, 96), columns],
                    h_sem.at[d * 4 + g],
                )
            )
    for copy in copies + h_copies:
        copy.start()
    for copy in copies:
        copy.wait()
    sends = []
    for j, shift in enumerate(SHIFTS):
        first = pl.multiple_of((wrap(y + shift) * 4 + xh * 2 + core) * 96, 96)
        send = pltpu.make_async_copy(d_ref.at[pl.ds(first, 96)], slices[j], out_sem.at[j])
        send.start()
        sends.append(send)
    for copy in h_copies:
        copy.wait()
    for half in range(2):
        lanes = pl.ds(half * 512, 512)
        product = jnp.dot(h_ref[...], d_ref[:, lanes], preferred_element_type=F32).astype(BF16)
        for g in range(4):
            outs[g][:, lanes] = product[g * 96 : (g + 1) * 96]
    for send in sends:
        send.wait()


def second_matmul(where, hidden, downs):
    return pl.pallas_call(
        second_kernel,
        in_specs=[SMEM] + [ANY] * 8,
        out_specs=[VMEM] * 4 + [ANY] * 4,
        out_shape=[jax.ShapeDtypeStruct((96, 1024), BF16)] * 8,
        scratch_shapes=[
            pltpu.VMEM((384, 1536), BF16),
            pltpu.VMEM((1536, 1024), BF16),
            pltpu.SemaphoreType.DMA((16,)),
            pltpu.SemaphoreType.DMA((4,)),
            pltpu.SemaphoreType.DMA((4,)),
        ],
        cost_estimate=cost(2 * 384 * 1536 * 1024, 6 << 20),
        compiler_params=params(),
        name="second_matmul",
    )(where, *hidden, *downs)


def regroup_kernel(*refs):
    parts, outs = refs[:4], refs[4:]
    for g in range(4):
        wide = parts[g][...].astype(F32)
        for k in range(4):
            outs[k][:, g * 1024 : (g + 1) * 1024] = wide[k * PAIR : (k + 1) * PAIR].astype(BF16)


def regroup(parts):
    return pl.pallas_call(
        regroup_kernel,
        in_specs=[VMEM] * 4,
        out_specs=[VMEM] * 4,
        out_shape=[jax.ShapeDtypeStruct((PAIR, 4096), BF16)] * 4,
        cost_estimate=cost(0, 2 << 20),
        compiler_params=params(),
        name="regroup",
    )(*parts)


def place_kernel(where_ref, *refs):
    parts, out_ref, sem = refs[:4], refs[4], refs[5]
    copies = []
    for j, shift in enumerate(SHIFTS):
        columns = pl.ds(pl.multiple_of(wrap(where_ref[0] - shift) * 1024, 1024), 1024)
        copies.append(pltpu.make_async_copy(parts[j], out_ref.at[0, :, columns], sem.at[j]))
    for copy in copies:
        copy.start()
    for copy in copies:
        copy.wait()


def place_down(where, parts):
    return pl.pallas_call(
        place_kernel,
        in_specs=[SMEM] + [ANY] * 4,
        out_specs=ANY,
        out_shape=jax.ShapeDtypeStruct((1, 96, 4096), BF16),
        scratch_shapes=[pltpu.SemaphoreType.DMA((4,))],
        cost_estimate=cost(0, 2 << 20),
        compiler_params=params(),
        name="place_down",
    )(where, *parts)


def body(
    master_gate_up,
    grad_gate_up,
    first_gate_up,
    second_gate_up,
    master_down,
    grad_down,
    first_down,
    second_down,
    tokens,
    route_ids,
    route_weights,
):
    exp, ten = lax.axis_index("exp"), lax.axis_index("ten")
    y, xh, core, z = ten // 4, ten // 2 % 2, ten % 2, exp % 4
    where = jnp.stack([y, xh, core, exp // 4, z]).astype(jnp.int32)

    meta = jnp.concatenate([route_ids.astype(F32), route_weights], axis=1)
    other_tokens, other_meta = move_core(tokens), move_core(meta)

    gate_up = (master_gate_up, grad_gate_up, first_gate_up, second_gate_up)
    near = jnp.stack([(y + 1) % 4, (y + 3) % 4]).astype(jnp.int32)
    far = jnp.stack([y, (y + 2) % 4]).astype(jnp.int32)
    partial, to_next, to_last = adam(near, gate_up, None, 384)
    from_last, from_next = move_y(to_next, 1), move_y(to_last, -1)
    chunks = dispatch(where, tokens, other_tokens, meta, other_meta)
    arrived = [move_out(chunk, k) for k, chunk in enumerate(chunks)]
    partial = after(partial, chunks)
    new_master_gate_up, stays, to_far = adam(far, gate_up, partial, 384)
    down_arrays = tuple(a[:, None] for a in (master_down, grad_down, first_down, second_down))
    down_arrays = after(down_arrays, stays)
    new_master_down, down = adam(jnp.zeros((1,), jnp.int32), down_arrays, None, 1536)
    new_master_down, down = new_master_down[:, 0], down[0]

    stays_across = move_xh(stays)
    stays, from_last, from_next, stays_across, to_far, down = staged(
        (stays, from_last, from_next, stays_across, to_far, down)
    )
    from_far, last_across = move_y(to_far, 2), move_xh(from_last)
    crossed = {0: move_core(stays)}
    from_far, last_across, from_next, arrived, crossed[0], stays_across, from_last = staged(
        (from_far, last_across, from_next, arrived, crossed[0], stays_across, from_last)
    )
    head, tail = jnp.concatenate(arrived[:2], axis=0), jnp.concatenate(arrived[2:], axis=0)
    last_head, next_tail, next_across = move_y(head, 1), move_y(tail, -1), move_xh(from_next)
    crossed[4] = move_core(stays_across)
    crossed[1] = move_core(after(from_last, crossed[4]))
    last_head, next_tail, next_across, head, tail, from_far, crossed[1], last_across = staged(
        (last_head, next_tail, next_across, head, tail, from_far, crossed[1], last_across)
    )
    last_tail, next_head = move_y(tail, 1), move_y(head, -1)
    far_head, far_tail = move_y(last_head, 1), move_y(next_tail, -1)
    far_across = move_xh(from_far)
    rows = [head, tail, last_head, last_tail, next_head, next_tail, far_head, far_tail]
    pieces = [stays, from_last, from_next, from_far, stays_across, last_across, next_across, far_across]
    crossed[2] = move_core(from_next)
    crossed[5] = move_core(after(last_across, crossed[2]))
    crossed[6] = move_core(after(next_across, crossed[5]))
    crossed[3] = move_core(after(from_far, crossed[6]))
    crossed[7] = move_core(far_across)
    down_across = move_xh(after(down, far_across))
    hidden, rollout_gate_up = first_matmul(where, rows, pieces + [crossed[i] for i in range(8)])

    hiddens = [hidden, move_y(hidden, 1), move_y(hidden, -1), move_y(hidden, 2)]
    downs = [down, down_across]
    downs = downs + [move_core(piece) for piece in downs]
    result = second_matmul(where, hiddens, downs)
    outs, slices = result[:4], result[4:]
    parts = [outs[0]] + [move_y(part, shift) for part, shift in zip(outs[1:], SHIFTS[1:])]
    backs = [move_home(chunk, k) for k, chunk in enumerate(regroup(parts))]
    slices = [slices[0]] + [move_y(part, shift) for part, shift in zip(slices[1:], SHIFTS[1:])]
    rollout_down = place_down(where, slices)
    backs, rollout_down = staged((backs, rollout_down))
    own, other = combine(where, meta, other_meta, backs)
    moe_out = (own + move_core(other)).astype(BF16)
    return (new_master_gate_up, new_master_down, rollout_gate_up, rollout_down, moe_out)


def solution(mesh):
    wide, tall, rows = P("exp", None, None, "ten"), P("exp", None, "ten"), P(("exp", "ten"), None)
    return jax.shard_map(
        body,
        mesh=mesh,
        in_specs=(wide,) * 4 + (tall,) * 4 + (rows,) * 3,
        out_specs=(wide, tall, P("exp", None, "ten", None), P("exp", "ten", None), rows),
        check_vma=False,
    )
```

time: 390 us -> 172 us (0.44)
  waiting for transfers between devices: 245 us -> 90.4 us
  Pallas kernels: 0 us -> 34.6 us
  local copies, waits for them, and re-layouts: 34.6 us -> 0.25 us
  matrix products: 31.4 us -> 0 us
  starting transfers between devices: 18.6 us -> 40.9 us
  blocking collectives: 21.9 us -> 0 us
  other arithmetic: 23.6 us -> 3.29 us
  between operations: 14.2 us -> 0.86 us
    reduce_scatter x1 -> x0, waiting for transfers between devices: 187 us -> none  [body(): lax.psum_scatter(jnp.dot(hidden, rollout_down[0], preferred_element_type=...]
    ppermute x0 -> x44, waiting for transfers between devices: none -> 90.4 us  [move(): return lax.ppermute(array, ('exp', 'ten'), pairs)]
    all_to_all x3 -> x0, waiting for transfers between devices: 49.4 us -> none  [the longest x1 36.9 us: body(): lax.all_to_all(send_gate_up, 'ten', split_axis=2, concat_axis=3, tiled=True)]
    ppermute x0 -> x44, starting transfers between devices: none -> 40.9 us  [move(): return lax.ppermute(array, ('exp', 'ten'), pairs)]
    pallas_call x0 -> x9, Pallas kernels: none -> 34.6 us  [the longest x3 18.7 us: adam(): pl.pallas_call(functools.partial(adam_kernel, count, parts, rows), in_spe...]
    dot_general x4 -> x0, matrix products: 31.4 us -> none  [the longest x1 20.5 us: body(): jnp.dot(hidden, rollout_down[0], preferred_element_type=jnp.float32)]
    all_to_all x1 -> x0, blocking collectives: 21.9 us -> none  [body(): lax.all_to_all(dispatch, 'exp', split_axis=0, concat_axis=0, tiled=True)]
    all_to_all x3 -> x0, starting transfers between devices: 18.4 us -> none  [the longest x1 7.21 us: body(): lax.all_to_all(send_gate_up, 'ten', split_axis=2, concat_axis=3, tiled=True)]
  transfers between devices with their start and end apart: 5 -> 44, of which waited for: 4 -> 20; matrix products, arithmetic and copies ran while one was open for 12% -> 2% of each run, Pallas kernels for 0% -> 17%
where the time goes in v1:
time: 172 us; the launch traced here: 170 us
  waiting for transfers between devices  90.4 us (53%)
  starting transfers between devices  40.9 us (24%)
  Pallas kernels  34.6 us (20%)
  other arithmetic  3.29 us (2%)
    ppermute x44, waiting for transfers between devices, move(): return lax.ppermute(array, ('exp', 'ten'), pairs)  90.4 us
    ppermute x44, starting transfers between devices, move(): return lax.ppermute(array, ('exp', 'ten'), pairs)  40.9 us
    pallas_call x3, Pallas kernels, adam(): pl.pallas_call(functools.partial(adam_kernel, count, parts, rows), in_spe...  18.7 us
    pallas_call x1, Pallas kernels, first_matmul(): pl.pallas_call(first_kernel, in_specs=[SMEM] + [ANY] * 24, out_specs=[VME...  7.43 us
    pallas_call x1, Pallas kernels, second_matmul(): pl.pallas_call(second_kernel, in_specs=[SMEM] + [ANY] * 8, out_specs=[VME...  4.01 us
  transfers between devices with their start and end apart: 44, of which 20 were waited for; matrix products, arithmetic and copies ran while one was open for 2% of the time, Pallas kernels for 17%

profile of v1, /device:TPU:0, one launch (start us, length us, event | category | flops | bytes accessed | tf_op | source)
XLA Modules:
  0.0 170.3 jit_solution(13550999354007472643)
XLA Ops:
  0.7 0.7 convert_element_type.6
  1.4 0.7 pad_maximum_fusion
  3.3 5.9 %adam.3 = (f32[1,2,1536,256]{3,2,1,0:T(8,128)}, bf16[2,384,256]{2,1,0:T(8,128)(2,1)}, bf16[2,384,256]{2,1,0:T(8,128)(2,1)}) custom-call(s32[2]{0:T(128)} %pad_add_fusion.1.blocks_ref, f32[1,2,1536,256]{3,2,1,0:T(8,128)} %refs_0_.3, f32[1,2,1536,256]{3,2,1,0:T(8,128)} %refs_1_.3, f32[1,2,1536,256]{3,2,1,0:T(8,128)} %refs_2_.3, f32[1,2,1536,256]{3,2,1,0:T(8,128)} %refs_3_.3), custom_call_target="tpu_custom_call" | custom-call | bytes 8650752 | tf_op jit(solution)/shard_map/adam/pallas_call | solution.py:126
  9.2 1.7 %collective-permute-start.2 = (bf16[2,384,256]{2,1,0:T(8,128)(2,1)}, bf16[2,384,256]{2,1,0:T(8,128)(2,1)S(1)}, u32[]{:S(2)}, u32[]{:S(2)}) collective-permute-start(bf16[2,384,256]{2,1,0:T(8,128)(2,1)} %get-tuple-element.85), channel_id=1, source_target_pairs={{0,4},{1,5},{2,6},{3,7},{4,8},{5,9},{6,10},{7,11},{8,12},{9,13},{1... | collective-permute-start | bytes 1179656 | tf_op jit(solution)/shard_map/ppermute | solution.py:52
  10.9 1.6 collective-permute-start.3
  13.2 1.4 dispatch.1
  14.6 5.9 %adam.4 = (f32[1,2,1536,256]{3,2,1,0:T(8,128)}, bf16[2,384,256]{2,1,0:T(8,128)(2,1)}, bf16[2,384,256]{2,1,0:T(8,128)(2,1)}) custom-call(s32[2]{0:T(128)} %pad_add_fusion.blocks_ref, f32[1,2,1536,256]{3,2,1,0:T(8,128)} %refs_0_.3, f32[1,2,1536,256]{3,2,1,0:T(8,128)} %refs_1_.3, f32[1,2,1536,256]{3,2,1,0:T(8,128)} %refs_2_.3, ...), custom_call_target="tpu_custom_call", output_to_operand_aliasing={{0}: (5, {})} | custom-call | bytes 8650752 | tf_op jit(solution)/shard_map/adam/pallas_call | solution.py:126
  20.5 3.2 %collective-permute-start.4 = (bf16[2,384,256]{2,1,0:T(8,128)(2,1)}, bf16[2,384,256]{2,1,0:T(8,128)(2,1)S(1)}, u32[]{:S(2)}, u32[]{:S(2)}) collective-permute-start(bf16[2,384,256]{2,1,0:T(8,128)(2,1)} %get-tuple-element.92.refs_8_), channel_id=1, source_target_pairs={{0,2},{1,3},{2,0},{3,1},{4,6},{5,7},{6,4},{7,5},{8,10},{9,11},{10,... | collective-permute-start | bytes 1179656 | tf_op jit(solution)/shard_map/ppermute | solution.py:52
  23.7 0.7 collective-permute-start.7
  24.3 2.0 %collective-permute-start.8 = (bf16[24,4096]{1,0:T(8,128)(2,1)S(1)}, bf16[24,4096]{1,0:T(8,128)(2,1)S(1)}, u32[]{:S(2)}, u32[]{:S(2)}) collective-permute-start(bf16[24,4096]{1,0:T(8,128)(2,1)S(1)} %get-tuple-element.74), channel_id=1, source_target_pairs={{0,16},{1,80},{2,18},{3,82},{4,20},{5,84},{6,22},{7,86},{8,24},{9,... | collective-permute-start | bytes 589832 | tf_op jit(solution)/shard_map/ppermute | solution.py:52
  26.3 6.9 %adam.5 = (f32[1,1,1536,256]{3,2,1,0:T(8,128)}, bf16[1,1536,256]{2,1,0:T(8,128)(2,1)}) custom-call(s32[1]{0:T(128)} %constant.77.clone.1.blocks_ref, f32[1,1,1536,256]{3,2,1,0:T(8,128)} %bitcast.17, f32[1,1,1536,256]{3,2,1,0:T(8,128)} %bitcast.18, f32[1,1,1536,256]{3,2,1,0:T(8,128)} %bitcast.19, f32[1,1,1536,256]{3,2,1,0:T(8,128)} %bitcast.20), custom_call_target="tpu_custom_call" | custom-call | bytes 8650752 | tf_op jit(solution)/shard_map/adam/pallas_call | solution.py:126
  33.2 1.1 collective-permute-done.4.refs_12_
  34.3 2.1 %collective-permute-start.5 = (bf16[2,384,256]{2,1,0:T(8,128)(2,1)S(1)}, bf16[2,384,256]{2,1,0:T(8,128)(2,1)S(1)}, u32[]{:S(2)}, u32[]{:S(2)}) collective-permute-start(bf16[2,384,256]{2,1,0:T(8,128)(2,1)S(1)} %copy-done.3), channel_id=1, source_target_pairs={{0,8},{1,9},{2,10},{3,11},{4,12},{5,13},{6,14},{7,15},{8,0},{9,1},... | collective-permute-start | bytes 1179656 | tf_op jit(solution)/shard_map/ppermute | solution.py:52
  36.4 3.0 %collective-permute-start.6 = (bf16[2,384,256]{2,1,0:T(8,128)(2,1)S(1)}, bf16[2,384,256]{2,1,0:T(8,128)(2,1)S(1)}, u32[]{:S(2)}, u32[]{:S(2)}) collective-permute-start(bf16[2,384,256]{2,1,0:T(8,128)(2,1)S(1)} %collective-permute-done.2.refs_9_), channel_id=1, source_target_pairs={{0,2},{1,3},{2,0},{3,1},{4,6},{5,7},{6,4},{7,5},{8,10},{9,11},{10,... | collective-permute-start | bytes 1179656 | tf_op jit(solution)/shard_map/ppermute | solution.py:52
  39.4 4.0 %collective-permute-start.9 = (bf16[24,4096]{1,0:T(8,128)(2,1)S(1)}, bf16[24,4096]{1,0:T(8,128)(2,1)S(1)}, u32[]{:S(2)}, u32[]{:S(2)}) collective-permute-start(bf16[24,4096]{1,0:T(8,128)(2,1)S(1)} %get-tuple-element.75), channel_id=1, source_target_pairs={{0,32},{1,96},{2,34},{3,98},{4,36},{5,100},{6,38},{7,102},{8,40},{... | collective-permute-start | bytes 589832 | tf_op jit(solution)/shard_map/ppermute | solution.py:52
  43.4 0.7 collective-permute-start.10
  44.1 4.6 %collective-permute-done.9 = bf16[24,4096]{1,0:T(8,128)(2,1)S(1)} collective-permute-done((bf16[24,4096]{1,0:T(8,128)(2,1)S(1)}, bf16[24,4096]{1,0:T(8,128)(2,1)S(1)}, u32[]{:S(2)}, u32[]{:S(2)}) %collective-permute-start.9) | collective-permute-done | bytes 196640 | tf_op jit(solution)/shard_map/ppermute | solution.py:52
  48.7 5.7 %collective-permute-done.10 = bf16[24,4096]{1,0:T(8,128)(2,1)S(1)} collective-permute-done((bf16[24,4096]{1,0:T(8,128)(2,1)S(1)}, bf16[24,4096]{1,0:T(8,128)(2,1)S(1)}, u32[]{:S(2)}, u32[]{:S(2)}) %collective-permute-start.10) | collective-permute-done | bytes 196640 | tf_op jit(solution)/shard_map/ppermute | solution.py:52
  54.5 1.5 collective-permute-start.13
  58.2 4.7 %collective-permute-done.13.refs_5_ = bf16[48,4096]{1,0:T(8,128)(2,1)S(1)} collective-permute-done((bf16[48,4096]{1,0:T(8,128)(2,1)S(1)}, bf16[48,4096]{1,0:T(8,128)(2,1)S(1)}, u32[]{:S(2)}, u32[]{:S(2)}) %collective-permute-start.13) | collective-permute-done | bytes 393248 | tf_op jit(solution)/shard_map/ppermute | solution.py:52
  63.0 5.9 %collective-permute-done.12.refs_2_ = bf16[48,4096]{1,0:T(8,128)(2,1)S(1)} collective-permute-done((bf16[48,4096]{1,0:T(8,128)(2,1)S(1)}, bf16[48,4096]{1,0:T(8,128)(2,1)S(1)}, u32[]{:S(2)}, u32[]{:S(2)}) %collective-permute-start.12) | collective-permute-done | bytes 393248 | tf_op jit(solution)/shard_map/ppermute | solution.py:52
  69.9 11.4 %collective-permute-done.21.refs_15_ = bf16[2,384,256]{2,1,0:T(8,128)(2,1)S(1)} collective-permute-done((bf16[2,384,256]{2,1,0:T(8,128)(2,1)S(1)}, bf16[2,384,256]{2,1,0:T(8,128)(2,1)S(1)}, u32[]{:S(2)}, u32[]{:S(2)}) %collective-permute-start.21) | collective-permute-done | bytes 393248 | tf_op jit(solution)/shard_map/ppermute | solution.py:52
  81.9 2.7 %collective-permute-start.18 = (bf16[48,4096]{1,0:T(8,128)(2,1)S(1)}, bf16[48,4096]{1,0:T(8,128)(2,1)S(1)}, u32[]{:S(2)}, u32[]{:S(2)}) collective-permute-start(bf16[48,4096]{1,0:T(8,128)(2,1)S(1)} %constant_dynamic-update-slice_fusion.refs_0_), channel_id=1, source_target_pairs={{0,12},{1,13},{2,14},{3,15},{4,0},{5,1},{6,2},{7,3},{8,4},{9,5},{1... | collective-permute-start | bytes 1179656 | tf_op jit(solution)/shard_map/ppermute | solution.py:52
  84.6 3.2 %collective-permute-start.20 = (bf16[48,4096]{1,0:T(8,128)(2,1)S(1)}, bf16[48,4096]{1,0:T(8,128)(2,1)S(1)}, u32[]{:S(2)}, u32[]{:S(2)}) collective-permute-start(bf16[48,4096]{1,0:T(8,128)(2,1)S(1)} %collective-permute-done.13.refs_5_), channel_id=1, source_target_pairs={{0,12},{1,13},{2,14},{3,15},{4,0},{5,1},{6,2},{7,3},{8,4},{9,5},{1... | collective-permute-start | bytes 1179656 | tf_op jit(solution)/shard_map/ppermute | solution.py:52
  87.8 6.2 %collective-permute-done.18.refs_4_ = bf16[48,4096]{1,0:T(8,128)(2,1)S(1)} collective-permute-done((bf16[48,4096]{1,0:T(8,128)(2,1)S(1)}, bf16[48,4096]{1,0:T(8,128)(2,1)S(1)}, u32[]{:S(2)}, u32[]{:S(2)}) %collective-permute-start.18) | collective-permute-done | bytes 393248 | tf_op jit(solution)/shard_map/ppermute | solution.py:52
  94.0 3.7 %collective-permute-done.17.refs_3_ = bf16[48,4096]{1,0:T(8,128)(2,1)S(1)} collective-permute-done((bf16[48,4096]{1,0:T(8,128)(2,1)S(1)}, bf16[48,4096]{1,0:T(8,128)(2,1)S(1)}, u32[]{:S(2)}, u32[]{:S(2)}) %collective-permute-start.17) | collective-permute-done | bytes 393248 | tf_op jit(solution)/shard_map/ppermute | solution.py:52
  97.7 7.7 %collective-permute-done.19.refs_6_ = bf16[48,4096]{1,0:T(8,128)(2,1)S(1)} collective-permute-done((bf16[48,4096]{1,0:T(8,128)(2,1)S(1)}, bf16[48,4096]{1,0:T(8,128)(2,1)S(1)}, u32[]{:S(2)}, u32[]{:S(2)}) %collective-permute-start.19) | collective-permute-done | bytes 393248 | tf_op jit(solution)/shard_map/ppermute | solution.py:52
  106.0 7.4 %first_matmul.1 = (bf16[384,384]{1,0:T(8,128)(2,1)S(1)}, bf16[1,2,96,4096]{3,2,1,0:T(8,128)(2,1)}) custom-call(s32[5]{0:T(128)S(1)} %stack.44.where_ref, bf16[48,4096]{1,0:T(8,128)(2,1)S(1)} %constant_dynamic-update-slice_fusion.refs_0_, bf16[48,4096]{1,0:T(8,128)(2,1)S(1)} %constant_dynamic-update-slice_fusion.2.refs_1_, ...), custom_call_target="tpu_custom_call" | custom-call | flops 2415919104 | bytes 11534336 | tf_op jit(solution)/shard_map/first_matmul/pallas_call | solution.py:295
  113.5 1.7 %collective-permute-start.28 = (bf16[384,384]{1,0:T(8,128)(2,1)S(1)}, bf16[384,384]{1,0:T(8,128)(2,1)S(1)}, u32[]{:S(2)}, u32[]{:S(2)}) collective-permute-start(bf16[384,384]{1,0:T(8,128)(2,1)S(1)} %get-tuple-element.117.refs_0_), channel_id=1, source_target_pairs={{0,12},{1,13},{2,14},{3,15},{4,0},{5,1},{6,2},{7,3},{8,4},{9,5},{1... | collective-permute-start | bytes 884744 | tf_op jit(solution)/shard_map/ppermute | solution.py:52
  115.6 9.3 %collective-permute-done.29.refs_3_ = bf16[384,384]{1,0:T(8,128)(2,1)S(1)} collective-permute-done((bf16[384,384]{1,0:T(8,128)(2,1)S(1)}, bf16[384,384]{1,0:T(8,128)(2,1)S(1)}, u32[]{:S(2)}, u32[]{:S(2)}) %collective-permute-start.29) | collective-permute-done | bytes 294944 | tf_op jit(solution)/shard_map/ppermute | solution.py:52
  124.9 2.3 %collective-permute-done.28.refs_2_ = bf16[384,384]{1,0:T(8,128)(2,1)S(1)} collective-permute-done((bf16[384,384]{1,0:T(8,128)(2,1)S(1)}, bf16[384,384]{1,0:T(8,128)(2,1)S(1)}, u32[]{:S(2)}, u32[]{:S(2)}) %collective-permute-start.28) | collective-permute-done | bytes 294944 | tf_op jit(solution)/shard_map/ppermute | solution.py:52
  127.2 3.1 %collective-permute-done.27.refs_1_ = bf16[384,384]{1,0:T(8,128)(2,1)S(1)} collective-permute-done((bf16[384,384]{1,0:T(8,128)(2,1)S(1)}, bf16[384,384]{1,0:T(8,128)(2,1)S(1)}, u32[]{:S(2)}, u32[]{:S(2)}) %collective-permute-start.27) | collective-permute-done | bytes 294944 | tf_op jit(solution)/shard_map/ppermute | solution.py:52
  130.2 4.0 %second_matmul.1 = (bf16[96,1024]{1,0:T(8,128)(2,1)S(1)}, bf16[96,1024]{1,0:T(8,128)(2,1)S(1)}, bf16[96,1024]{1,0:T(8,128)(2,1)S(1)}, bf16[96,1024]{1,0:T(8,128)...) custom-call(s32[5]{0:T(128)S(1)} %stack.44.where_ref, ...), custom_call_target="tpu_custom_call" | custom-call | flops 1207959552 | bytes 6291456 | tf_op jit(solution)/shard_map/second_matmul/pallas_call | solution.py:362
  134.3 0.7 collective-permute-start.33
  134.9 1.4 collective-permute-start.34
  136.6 2.4 %collective-permute-start.40 = (bf16[96,1024]{1,0:T(8,128)(2,1)S(1)}, bf16[96,1024]{1,0:T(8,128)(2,1)S(1)}, u32[]{:S(2)}, u32[]{:S(2)}) collective-permute-start(bf16[96,1024]{1,0:T(8,128)(2,1)S(1)} %get-tuple-element.129), channel_id=1, source_target_pairs={{0,12},{1,13},{2,14},{3,15},{4,0},{5,1},{6,2},{7,3},{8,4},{9,5},{1... | collective-permute-start | bytes 589832 | tf_op jit(solution)/shard_map/ppermute | solution.py:52
  139.0 3.1 %collective-permute-done.33.refs_1_ = bf16[96,1024]{1,0:T(8,128)(2,1)S(1)} collective-permute-done((bf16[96,1024]{1,0:T(8,128)(2,1)S(1)}, bf16[96,1024]{1,0:T(8,128)(2,1)S(1)}, u32[]{:S(2)}, u32[]{:S(2)}) %collective-permute-start.33) | collective-permute-done | bytes 196640 | tf_op jit(solution)/shard_map/ppermute | solution.py:52
  142.1 5.9 %collective-permute-done.34.refs_2_ = bf16[96,1024]{1,0:T(8,128)(2,1)S(1)} collective-permute-done((bf16[96,1024]{1,0:T(8,128)(2,1)S(1)}, bf16[96,1024]{1,0:T(8,128)(2,1)S(1)}, u32[]{:S(2)}, u32[]{:S(2)}) %collective-permute-start.34) | collective-permute-done | bytes 196640 | tf_op jit(solution)/shard_map/ppermute | solution.py:52
  148.1 0.7 collective-permute-start.36
  148.8 2.3 %collective-permute-start.37 = (bf16[24,4096]{1,0:T(8,128)(2,1)S(1)}, bf16[24,4096]{1,0:T(8,128)(2,1)S(1)}, u32[]{:S(2)}, u32[]{:S(2)}) collective-permute-start(bf16[24,4096]{1,0:T(8,128)(2,1)S(1)} %get-tuple-element.125), channel_id=1, source_target_pairs={{0,48},{1,112},{2,50},{3,114},{4,52},{5,116},{6,54},{7,118},{8,56}... | collective-permute-start | bytes 589832 | tf_op jit(solution)/shard_map/ppermute | solution.py:52
  151.1 0.7 collective-permute-start.38
  151.8 3.3 %collective-permute-done.41.refs_2_ = bf16[96,1024]{1,0:T(8,128)(2,1)S(1)} collective-permute-done((bf16[96,1024]{1,0:T(8,128)(2,1)S(1)}, bf16[96,1024]{1,0:T(8,128)(2,1)S(1)}, u32[]{:S(2)}, u32[]{:S(2)}) %collective-permute-start.41) | collective-permute-done | bytes 196640 | tf_op jit(solution)/shard_map/ppermute | solution.py:52
  155.1 1.5 place_down.1
  156.6 1.6 collective-permute-done.38.rest_2_
  158.2 7.7 %collective-permute-done.39.rest_3_ = bf16[24,4096]{1,0:T(8,128)(2,1)S(1)} collective-permute-done((bf16[24,4096]{1,0:T(8,128)(2,1)S(1)}, bf16[24,4096]{1,0:T(8,128)(2,1)S(1)}, u32[]{:S(2)}, u32[]{:S(2)}) %collective-permute-start.39) | collective-permute-done | bytes 196640 | tf_op jit(solution)/shard_map/ppermute | solution.py:52
  166.0 1.5 combine.1
  167.6 1.9 %collective-permute-done.43 = f32[32,4096]{1,0:T(8,128)S(1)} collective-permute-done((f32[32,4096]{1,0:T(8,128)S(1)}, f32[32,4096]{1,0:T(8,128)S(1)}, u32[]{:S(2)}, u32[]{:S(2)}) %collective-permute-start.43) | collective-permute-done | bytes 524320 | tf_op jit(solution)/shard_map/ppermute | solution.py:52
  169.5 0.8 add_convert_fusion
  (68 shorter events, 7.3 us)
Async XLA Ops:
  0.6 12.6 %collective-permute-start = (bf16[32,4096]{1,0:T(8,128)(2,1)}, bf16[32,4096]{1,0:T(8,128)(2,1)S(1)}, u32[]{:S(2)}, u32[]{:S(2)}) collective-permute-start(bf16[32,4096]{1,0:T(8,128)(2,1)} %own_ref.1), channel_id=1, source_target_pairs={{0,1},{1,0},{2,3},{3,2},{4,5},{5,4},{6,7},{7,6},{8,9},{9,8},{10,11... | collective-permute-start | bytes 786440 | tf_op jit(solution)/shard_map/ppermute | solution.py:52
  2.2 11.0 %collective-permute-start.1 = (f32[32,4]{1,0:T(8,128)S(1)}, f32[32,4]{1,0:T(8,128)S(1)}, u32[]{:S(2)}, u32[]{:S(2)}) collective-permute-start(f32[32,4]{1,0:T(8,128)S(1)} %copy.20.own_meta_ref), channel_id=1, source_target_pairs={{0,1},{1,0},{2,3},{3,2},{4,5},{5,4},{6,7},{7,6},{8,9},{9,8},{10,11... | collective-permute-start | bytes 1544 | tf_op jit(solution)/shard_map/ppermute | solution.py:52
  3.3 9.9 %copy-start.1 = (bf16[32,4096]{1,0:T(8,128)(2,1)S(1)}, bf16[32,4096]{1,0:T(8,128)(2,1)}, u32[]{:S(2)}) copy-start(bf16[32,4096]{1,0:T(8,128)(2,1)} %own_ref.1) | copy-start | bytes 786436
  9.2 24.0 %collective-permute-start.2 = (bf16[2,384,256]{2,1,0:T(8,128)(2,1)}, bf16[2,384,256]{2,1,0:T(8,128)(2,1)S(1)}, u32[]{:S(2)}, u32[]{:S(2)}) collective-permute-start(bf16[2,384,256]{2,1,0:T(8,128)(2,1)} %get-tuple-element.85), channel_id=1, source_target_pairs={{0,4},{1,5},{2,6},{3,7},{4,8},{5,9},{6,10},{7,11},{8,12},{9,13},{1... | collective-permute-start | bytes 1179656 | tf_op jit(solution)/shard_map/ppermute | solution.py:52
  10.9 22.3 %collective-permute-start.3 = (bf16[2,384,256]{2,1,0:T(8,128)(2,1)}, bf16[2,384,256]{2,1,0:T(8,128)(2,1)S(1)}, u32[]{:S(2)}, u32[]{:S(2)}) collective-permute-start(bf16[2,384,256]{2,1,0:T(8,128)(2,1)} %get-tuple-element.86), channel_id=1, source_target_pairs={{0,12},{1,13},{2,14},{3,15},{4,0},{5,1},{6,2},{7,3},{8,4},{9,5},{1... | collective-permute-start | bytes 1179656 | tf_op jit(solution)/shard_map/ppermute | solution.py:52
  20.5 13.8 %collective-permute-start.4 = (bf16[2,384,256]{2,1,0:T(8,128)(2,1)}, bf16[2,384,256]{2,1,0:T(8,128)(2,1)S(1)}, u32[]{:S(2)}, u32[]{:S(2)}) collective-permute-start(bf16[2,384,256]{2,1,0:T(8,128)(2,1)} %get-tuple-element.92.refs_8_), channel_id=1, source_target_pairs={{0,2},{1,3},{2,0},{3,1},{4,6},{5,7},{6,4},{7,5},{8,10},{9,11},{10,... | collective-permute-start | bytes 1179656 | tf_op jit(solution)/shard_map/ppermute | solution.py:52
  23.7 15.8 %collective-permute-start.7 = (bf16[24,4096]{1,0:T(8,128)(2,1)S(1)}, bf16[24,4096]{1,0:T(8,128)(2,1)S(1)}, u32[]{:S(2)}, u32[]{:S(2)}) collective-permute-start(bf16[24,4096]{1,0:T(8,128)(2,1)S(1)} %get-tuple-element.73), channel_id=1, source_target_pairs={{0,0},{1,64},{2,2},{3,66},{4,4},{5,68},{6,6},{7,70},{8,8},{9,72},{... | collective-permute-start | bytes 589832 | tf_op jit(solution)/shard_map/ppermute | solution.py:52
  24.3 19.1 %collective-permute-start.8 = (bf16[24,4096]{1,0:T(8,128)(2,1)S(1)}, bf16[24,4096]{1,0:T(8,128)(2,1)S(1)}, u32[]{:S(2)}, u32[]{:S(2)}) collective-permute-start(bf16[24,4096]{1,0:T(8,128)(2,1)S(1)} %get-tuple-element.74), channel_id=1, source_target_pairs={{0,16},{1,80},{2,18},{3,82},{4,20},{5,84},{6,22},{7,86},{8,24},{9,... | collective-permute-start | bytes 589832 | tf_op jit(solution)/shard_map/ppermute | solution.py:52
  26.3 8.0 %copy-start.3 = (bf16[2,384,256]{2,1,0:T(8,128)(2,1)S(1)}, bf16[2,384,256]{2,1,0:T(8,128)(2,1)}, u32[]{:S(2)}) copy-start(bf16[2,384,256]{2,1,0:T(8,128)(2,1)} %get-tuple-element.89) | copy-start | bytes 1179652
  26.3 13.1 %copy-start = (bf16[2,384,256]{2,1,0:T(8,128)(2,1)S(1)}, bf16[2,384,256]{2,1,0:T(8,128)(2,1)}, u32[]{:S(2)}) copy-start(bf16[2,384,256]{2,1,0:T(8,128)(2,1)} %get-tuple-element.92.refs_8_) | copy-start | bytes 1179652
  34.3 20.1 %collective-permute-start.5 = (bf16[2,384,256]{2,1,0:T(8,128)(2,1)S(1)}, bf16[2,384,256]{2,1,0:T(8,128)(2,1)S(1)}, u32[]{:S(2)}, u32[]{:S(2)}) collective-permute-start(bf16[2,384,256]{2,1,0:T(8,128)(2,1)S(1)} %copy-done.3), channel_id=1, source_target_pairs={{0,8},{1,9},{2,10},{3,11},{4,12},{5,13},{6,14},{7,15},{8,0},{9,1},... | collective-permute-start | bytes 1179656 | tf_op jit(solution)/shard_map/ppermute | solution.py:52
  36.4 18.0 %collective-permute-start.6 = (bf16[2,384,256]{2,1,0:T(8,128)(2,1)S(1)}, bf16[2,384,256]{2,1,0:T(8,128)(2,1)S(1)}, u32[]{:S(2)}, u32[]{:S(2)}) collective-permute-start(bf16[2,384,256]{2,1,0:T(8,128)(2,1)S(1)} %collective-permute-done.2.refs_9_), channel_id=1, source_target_pairs={{0,2},{1,3},{2,0},{3,1},{4,6},{5,7},{6,4},{7,5},{8,10},{9,11},{10,... | collective-permute-start | bytes 1179656 | tf_op jit(solution)/shard_map/ppermute | solution.py:52
  39.4 15.0 %collective-permute-start.11 = (bf16[2,384,256]{2,1,0:T(8,128)(2,1)S(1)}, bf16[2,384,256]{2,1,0:T(8,128)(2,1)S(1)}, u32[]{:S(2)}, u32[]{:S(2)}) collective-permute-start(bf16[2,384,256]{2,1,0:T(8,128)(2,1)S(1)} %copy-done), channel_id=1, source_target_pairs={{0,1},{1,0},{2,3},{3,2},{4,5},{5,4},{6,7},{7,6},{8,9},{9,8},{10,11... | collective-permute-start | bytes 1179656 | tf_op jit(solution)/shard_map/ppermute | solution.py:52
  39.4 9.2 %collective-permute-start.9 = (bf16[24,4096]{1,0:T(8,128)(2,1)S(1)}, bf16[24,4096]{1,0:T(8,128)(2,1)S(1)}, u32[]{:S(2)}, u32[]{:S(2)}) collective-permute-start(bf16[24,4096]{1,0:T(8,128)(2,1)S(1)} %get-tuple-element.75), channel_id=1, source_target_pairs={{0,32},{1,96},{2,34},{3,98},{4,36},{5,100},{6,38},{7,102},{8,40},{... | collective-permute-start | bytes 589832 | tf_op jit(solution)/shard_map/ppermute | solution.py:52
  43.4 11.0 %collective-permute-start.10 = (bf16[24,4096]{1,0:T(8,128)(2,1)S(1)}, bf16[24,4096]{1,0:T(8,128)(2,1)S(1)}, u32[]{:S(2)}, u32[]{:S(2)}) collective-permute-start(bf16[24,4096]{1,0:T(8,128)(2,1)S(1)} %get-tuple-element.76), channel_id=1, source_target_pairs={{0,48},{1,112},{2,50},{3,114},{4,52},{5,116},{6,54},{7,118},{8,56}... | collective-permute-start | bytes 589832 | tf_op jit(solution)/shard_map/ppermute | solution.py:52
  54.5 8.5 %collective-permute-start.13 = (bf16[48,4096]{1,0:T(8,128)(2,1)S(1)}, bf16[48,4096]{1,0:T(8,128)(2,1)S(1)}, u32[]{:S(2)}, u32[]{:S(2)}) collective-permute-start(bf16[48,4096]{1,0:T(8,128)(2,1)S(1)} %constant_dynamic-update-slice_fusion.2.refs_1_), channel_id=1, source_target_pairs={{0,12},{1,13},{2,14},{3,15},{4,0},{5,1},{6,2},{7,3},{8,4},{9,5},{1... | collective-permute-start | bytes 1179656 | tf_op jit(solution)/shard_map/ppermute | solution.py:52
  56.0 1.7 %collective-permute-start.15 = (bf16[2,384,256]{2,1,0:T(8,128)(2,1)S(1)}, bf16[2,384,256]{2,1,0:T(8,128)(2,1)S(1)}, u32[]{:S(2)}, u32[]{:S(2)}) collective-permute-start(bf16[2,384,256]{2,1,0:T(8,128)(2,1)S(1)} %collective-permute-done.4.refs_12_), channel_id=1, source_target_pairs={{0,1},{1,0},{2,3},{3,2},{4,5},{5,4},{6,7},{7,6},{8,9},{9,8},{10,11... | collective-permute-start | bytes 1179656 | tf_op jit(solution)/shard_map/ppermute | solution.py:52
  56.0 74.2 %copy-start.2 = (bf16[1,1536,256]{2,1,0:T(8,128)(2,1)S(1)}, bf16[1,1536,256]{2,1,0:T(8,128)(2,1)}, u32[]{:S(2)}) copy-start(bf16[1,1536,256]{2,1,0:T(8,128)(2,1)} %get-tuple-element.88) | copy-start | bytes 2359300
  56.0 12.8 %collective-permute-start.12 = (bf16[48,4096]{1,0:T(8,128)(2,1)S(1)}, bf16[48,4096]{1,0:T(8,128)(2,1)S(1)}, u32[]{:S(2)}, u32[]{:S(2)}) collective-permute-start(bf16[48,4096]{1,0:T(8,128)(2,1)S(1)} %constant_dynamic-update-slice_fusion.refs_0_), channel_id=1, source_target_pairs={{0,4},{1,5},{2,6},{3,7},{4,8},{5,9},{6,10},{7,11},{8,12},{9,13},{1... | collective-permute-start | bytes 1179656 | tf_op jit(solution)/shard_map/ppermute | solution.py:52
  56.7 12.8 %collective-permute-start.14 = (bf16[2,384,256]{2,1,0:T(8,128)(2,1)S(1)}, bf16[2,384,256]{2,1,0:T(8,128)(2,1)S(1)}, u32[]{:S(2)}, u32[]{:S(2)}) collective-permute-start(bf16[2,384,256]{2,1,0:T(8,128)(2,1)S(1)} %collective-permute-done.3.refs_10_), channel_id=1, source_target_pairs={{0,2},{1,3},{2,0},{3,1},{4,6},{5,7},{6,4},{7,5},{8,10},{9,11},{10,... | collective-permute-start | bytes 1179656 | tf_op jit(solution)/shard_map/ppermute | solution.py:52
  57.7 11.7 %collective-permute-start.16 = (bf16[2,384,256]{2,1,0:T(8,128)(2,1)S(1)}, bf16[2,384,256]{2,1,0:T(8,128)(2,1)S(1)}, u32[]{:S(2)}, u32[]{:S(2)}) collective-permute-start(bf16[2,384,256]{2,1,0:T(8,128)(2,1)S(1)} %collective-permute-done.2.refs_9_), channel_id=1, source_target_pairs={{0,1},{1,0},{2,3},{3,2},{4,5},{5,4},{6,7},{7,6},{8,9},{9,8},{10,11... | collective-permute-start | bytes 1179656 | tf_op jit(solution)/shard_map/ppermute | solution.py:52
  57.9 12.1 %collective-permute-start.22 = (bf16[2,384,256]{2,1,0:T(8,128)(2,1)S(1)}, bf16[2,384,256]{2,1,0:T(8,128)(2,1)S(1)}, u32[]{:S(2)}, u32[]{:S(2)}) collective-permute-start(bf16[2,384,256]{2,1,0:T(8,128)(2,1)S(1)} %collective-permute-done.3.refs_10_), channel_id=1, source_target_pairs={{0,1},{1,0},{2,3},{3,2},{4,5},{5,4},{6,7},{7,6},{8,9},{9,8},{10,11... | collective-permute-start | bytes 1179656 | tf_op jit(solution)/shard_map/ppermute | solution.py:52
  69.4 11.9 %collective-permute-start.21 = (bf16[2,384,256]{2,1,0:T(8,128)(2,1)S(1)}, bf16[2,384,256]{2,1,0:T(8,128)(2,1)S(1)}, u32[]{:S(2)}, u32[]{:S(2)}) collective-permute-start(bf16[2,384,256]{2,1,0:T(8,128)(2,1)S(1)} %collective-permute-done.5.refs_11_), channel_id=1, source_target_pairs={{0,2},{1,3},{2,0},{3,1},{4,6},{5,7},{6,4},{7,5},{8,10},{9,11},{10,... | collective-permute-start | bytes 1179656 | tf_op jit(solution)/shard_map/ppermute | solution.py:52
  69.9 11.9 %collective-permute-start.23 = (bf16[2,384,256]{2,1,0:T(8,128)(2,1)S(1)}, bf16[2,384,256]{2,1,0:T(8,128)(2,1)S(1)}, u32[]{:S(2)}, u32[]{:S(2)}) collective-permute-start(bf16[2,384,256]{2,1,0:T(8,128)(2,1)S(1)} %collective-permute-done.6.refs_13_), channel_id=1, source_target_pairs={{0,1},{1,0},{2,3},{3,2},{4,5},{5,4},{6,7},{7,6},{8,9},{9,8},{10,11... | collective-permute-start | bytes 1179656 | tf_op jit(solution)/shard_map/ppermute | solution.py:52
  81.4 24.1 %collective-permute-start.30 = (bf16[1536,256]{1,0:T(8,128)(2,1)}, bf16[1536,256]{1,0:T(8,128)(2,1)S(1)}, u32[]{:S(2)}, u32[]{:S(2)}) collective-permute-start(bf16[1536,256]{1,0:T(8,128)(2,1)} %bitcast.14), channel_id=1, source_target_pairs={{0,2},{1,3},{2,0},{3,1},{4,6},{5,7},{6,4},{7,5},{8,10},{9,11},{10,... | collective-permute-start | bytes 2359304 | tf_op jit(solution)/shard_map/ppermute | solution.py:52
  81.9 2.7 %collective-permute-start.24 = (bf16[2,384,256]{2,1,0:T(8,128)(2,1)S(1)}, bf16[2,384,256]{2,1,0:T(8,128)(2,1)S(1)}, u32[]{:S(2)}, u32[]{:S(2)}) collective-permute-start(bf16[2,384,256]{2,1,0:T(8,128)(2,1)S(1)} %collective-permute-done.14.refs_14_), channel_id=1, source_target_pairs={{0,1},{1,0},{2,3},{3,2},{4,5},{5,4},{6,7},{7,6},{8,9},{9,8},{10,11... | collective-permute-start | bytes 1179656 | tf_op jit(solution)/shard_map/ppermute | solution.py:52
  81.9 12.1 %collective-permute-start.18 = (bf16[48,4096]{1,0:T(8,128)(2,1)S(1)}, bf16[48,4096]{1,0:T(8,128)(2,1)S(1)}, u32[]{:S(2)}, u32[]{:S(2)}) collective-permute-start(bf16[48,4096]{1,0:T(8,128)(2,1)S(1)} %constant_dynamic-update-slice_fusion.refs_0_), channel_id=1, source_target_pairs={{0,12},{1,13},{2,14},{3,15},{4,0},{5,1},{6,2},{7,3},{8,4},{9,5},{1... | collective-permute-start | bytes 1179656 | tf_op jit(solution)/shard_map/ppermute | solution.py:52
  84.5 13.2 %collective-permute-start.17 = (bf16[48,4096]{1,0:T(8,128)(2,1)S(1)}, bf16[48,4096]{1,0:T(8,128)(2,1)S(1)}, u32[]{:S(2)}, u32[]{:S(2)}) collective-permute-start(bf16[48,4096]{1,0:T(8,128)(2,1)S(1)} %constant_dynamic-update-slice_fusion.2.refs_1_), channel_id=1, source_target_pairs={{0,4},{1,5},{2,6},{3,7},{4,8},{5,9},{6,10},{7,11},{8,12},{9,13},{1... | collective-permute-start | bytes 1179656 | tf_op jit(solution)/shard_map/ppermute | solution.py:52
  84.6 20.9 %collective-permute-start.19 = (bf16[48,4096]{1,0:T(8,128)(2,1)S(1)}, bf16[48,4096]{1,0:T(8,128)(2,1)S(1)}, u32[]{:S(2)}, u32[]{:S(2)}) collective-permute-start(bf16[48,4096]{1,0:T(8,128)(2,1)S(1)} %collective-permute-done.12.refs_2_), channel_id=1, source_target_pairs={{0,4},{1,5},{2,6},{3,7},{4,8},{5,9},{6,10},{7,11},{8,12},{9,13},{1... | collective-permute-start | bytes 1179656 | tf_op jit(solution)/shard_map/ppermute | solution.py:52
  84.6 21.4 %collective-permute-start.20 = (bf16[48,4096]{1,0:T(8,128)(2,1)S(1)}, bf16[48,4096]{1,0:T(8,128)(2,1)S(1)}, u32[]{:S(2)}, u32[]{:S(2)}) collective-permute-start(bf16[48,4096]{1,0:T(8,128)(2,1)S(1)} %collective-permute-done.13.refs_5_), channel_id=1, source_target_pairs={{0,12},{1,13},{2,14},{3,15},{4,0},{5,1},{6,2},{7,3},{8,4},{9,5},{1... | collective-permute-start | bytes 1179656 | tf_op jit(solution)/shard_map/ppermute | solution.py:52
  94.0 12.0 %collective-permute-start.26 = (bf16[2,384,256]{2,1,0:T(8,128)(2,1)S(1)}, bf16[2,384,256]{2,1,0:T(8,128)(2,1)S(1)}, u32[]{:S(2)}, u32[]{:S(2)}) collective-permute-start(bf16[2,384,256]{2,1,0:T(8,128)(2,1)S(1)} %collective-permute-done.21.refs_15_), channel_id=1, source_target_pairs={{0,1},{1,0},{2,3},{3,2},{4,5},{5,4},{6,7},{7,6},{8,9},{9,8},{10,11... | collective-permute-start | bytes 1179656 | tf_op jit(solution)/shard_map/ppermute | solution.py:52
  97.7 8.2 %collective-permute-start.25 = (bf16[2,384,256]{2,1,0:T(8,128)(2,1)S(1)}, bf16[2,384,256]{2,1,0:T(8,128)(2,1)S(1)}, u32[]{:S(2)}, u32[]{:S(2)}) collective-permute-start(bf16[2,384,256]{2,1,0:T(8,128)(2,1)S(1)} %collective-permute-done.5.refs_11_), channel_id=1, source_target_pairs={{0,1},{1,0},{2,3},{3,2},{4,5},{5,4},{6,7},{7,6},{8,9},{9,8},{10,11... | collective-permute-start | bytes 1179656 | tf_op jit(solution)/shard_map/ppermute | solution.py:52
  105.4 10.2 %collective-permute-start.31 = (bf16[1536,256]{1,0:T(8,128)(2,1)}, bf16[1536,256]{1,0:T(8,128)(2,1)S(1)}, u32[]{:S(2)}, u32[]{:S(2)}) collective-permute-start(bf16[1536,256]{1,0:T(8,128)(2,1)} %bitcast.15), channel_id=1, source_target_pairs={{0,1},{1,0},{2,3},{3,2},{4,5},{5,4},{6,7},{7,6},{8,9},{9,8},{10,11... | collective-permute-start | bytes 2359304 | tf_op jit(solution)/shard_map/ppermute | solution.py:52
  105.4 24.8 %collective-permute-start.32 = (bf16[1536,256]{1,0:T(8,128)(2,1)S(1)}, bf16[1536,256]{1,0:T(8,128)(2,1)S(1)}, u32[]{:S(2)}, u32[]{:S(2)}) collective-permute-start(bf16[1536,256]{1,0:T(8,128)(2,1)S(1)} %collective-permute-done.30.refs_5_), channel_id=1, source_target_pairs={{0,1},{1,0},{2,3},{3,2},{4,5},{5,4},{6,7},{7,6},{8,9},{9,8},{10,11... | collective-permute-start | bytes 2359304 | tf_op jit(solution)/shard_map/ppermute | solution.py:52
  113.4 11.5 %collective-permute-start.29 = (bf16[384,384]{1,0:T(8,128)(2,1)S(1)}, bf16[384,384]{1,0:T(8,128)(2,1)S(1)}, u32[]{:S(2)}, u32[]{:S(2)}) collective-permute-start(bf16[384,384]{1,0:T(8,128)(2,1)S(1)} %get-tuple-element.117.refs_0_), channel_id=1, source_target_pairs={{0,8},{1,9},{2,10},{3,11},{4,12},{5,13},{6,14},{7,15},{8,0},{9,1},... | collective-permute-start | bytes 884744 | tf_op jit(solution)/shard_map/ppermute | solution.py:52
  113.5 13.7 %collective-permute-start.28 = (bf16[384,384]{1,0:T(8,128)(2,1)S(1)}, bf16[384,384]{1,0:T(8,128)(2,1)S(1)}, u32[]{:S(2)}, u32[]{:S(2)}) collective-permute-start(bf16[384,384]{1,0:T(8,128)(2,1)S(1)} %get-tuple-element.117.refs_0_), channel_id=1, source_target_pairs={{0,12},{1,13},{2,14},{3,15},{4,0},{5,1},{6,2},{7,3},{8,4},{9,5},{1... | collective-permute-start | bytes 884744 | tf_op jit(solution)/shard_map/ppermute | solution.py:52
  115.2 15.0 %collective-permute-start.27 = (bf16[384,384]{1,0:T(8,128)(2,1)S(1)}, bf16[384,384]{1,0:T(8,128)(2,1)S(1)}, u32[]{:S(2)}, u32[]{:S(2)}) collective-permute-start(bf16[384,384]{1,0:T(8,128)(2,1)S(1)} %get-tuple-element.117.refs_0_), channel_id=1, source_target_pairs={{0,4},{1,5},{2,6},{3,7},{4,8},{5,9},{6,10},{7,11},{8,12},{9,13},{1... | collective-permute-start | bytes 884744 | tf_op jit(solution)/shard_map/ppermute | solution.py:52
  134.3 7.8 %collective-permute-start.33 = (bf16[96,1024]{1,0:T(8,128)(2,1)S(1)}, bf16[96,1024]{1,0:T(8,128)(2,1)S(1)}, u32[]{:S(2)}, u32[]{:S(2)}) collective-permute-start(bf16[96,1024]{1,0:T(8,128)(2,1)S(1)} %get-tuple-element.121), channel_id=1, source_target_pairs={{0,12},{1,13},{2,14},{3,15},{4,0},{5,1},{6,2},{7,3},{8,4},{9,5},{1... | collective-permute-start | bytes 589832 | tf_op jit(solution)/shard_map/ppermute | solution.py:52
  134.9 13.1 %collective-permute-start.34 = (bf16[96,1024]{1,0:T(8,128)(2,1)S(1)}, bf16[96,1024]{1,0:T(8,128)(2,1)S(1)}, u32[]{:S(2)}, u32[]{:S(2)}) collective-permute-start(bf16[96,1024]{1,0:T(8,128)(2,1)S(1)} %get-tuple-element.122), channel_id=1, source_target_pairs={{0,4},{1,5},{2,6},{3,7},{4,8},{5,9},{6,10},{7,11},{8,12},{9,13},{1... | collective-permute-start | bytes 589832 | tf_op jit(solution)/shard_map/ppermute | solution.py:52
  136.3 11.7 %collective-permute-start.35 = (bf16[96,1024]{1,0:T(8,128)(2,1)S(1)}, bf16[96,1024]{1,0:T(8,128)(2,1)S(1)}, u32[]{:S(2)}, u32[]{:S(2)}) collective-permute-start(bf16[96,1024]{1,0:T(8,128)(2,1)S(1)} %get-tuple-element.123), channel_id=1, source_target_pairs={{0,8},{1,9},{2,10},{3,11},{4,12},{5,13},{6,14},{7,15},{8,0},{9,1},... | collective-permute-start | bytes 589832 | tf_op jit(solution)/shard_map/ppermute | solution.py:52
  136.6 14.4 %collective-permute-start.40 = (bf16[96,1024]{1,0:T(8,128)(2,1)S(1)}, bf16[96,1024]{1,0:T(8,128)(2,1)S(1)}, u32[]{:S(2)}, u32[]{:S(2)}) collective-permute-start(bf16[96,1024]{1,0:T(8,128)(2,1)S(1)} %get-tuple-element.129), channel_id=1, source_target_pairs={{0,12},{1,13},{2,14},{3,15},{4,0},{5,1},{6,2},{7,3},{8,4},{9,5},{1... | collective-permute-start | bytes 589832 | tf_op jit(solution)/shard_map/ppermute | solution.py:52
  139.0 16.1 %collective-permute-start.41 = (bf16[96,1024]{1,0:T(8,128)(2,1)S(1)}, bf16[96,1024]{1,0:T(8,128)(2,1)S(1)}, u32[]{:S(2)}, u32[]{:S(2)}) collective-permute-start(bf16[96,1024]{1,0:T(8,128)(2,1)S(1)} %get-tuple-element.130), channel_id=1, source_target_pairs={{0,4},{1,5},{2,6},{3,7},{4,8},{5,9},{6,10},{7,11},{8,12},{9,13},{1... | collective-permute-start | bytes 589832 | tf_op jit(solution)/shard_map/ppermute | solution.py:52
  142.1 13.0 %collective-permute-start.42 = (bf16[96,1024]{1,0:T(8,128)(2,1)S(1)}, bf16[96,1024]{1,0:T(8,128)(2,1)S(1)}, u32[]{:S(2)}, u32[]{:S(2)}) collective-permute-start(bf16[96,1024]{1,0:T(8,128)(2,1)S(1)} %get-tuple-element.131), channel_id=1, source_target_pairs={{0,8},{1,9},{2,10},{3,11},{4,12},{5,13},{6,14},{7,15},{8,0},{9,1},... | collective-permute-start | bytes 589832 | tf_op jit(solution)/shard_map/ppermute | solution.py:52
  148.1 8.5 %collective-permute-start.36 = (bf16[24,4096]{1,0:T(8,128)(2,1)S(1)}, bf16[24,4096]{1,0:T(8,128)(2,1)S(1)}, u32[]{:S(2)}, u32[]{:S(2)}) collective-permute-start(bf16[24,4096]{1,0:T(8,128)(2,1)S(1)} %get-tuple-element.124), channel_id=1, source_target_pairs={{0,0},{1,64},{2,2},{3,66},{4,4},{5,68},{6,6},{7,70},{8,8},{9,72},{... | collective-permute-start | bytes 589832 | tf_op jit(solution)/shard_map/ppermute | solution.py:52
  148.8 7.8 %collective-permute-start.37 = (bf16[24,4096]{1,0:T(8,128)(2,1)S(1)}, bf16[24,4096]{1,0:T(8,128)(2,1)S(1)}, u32[]{:S(2)}, u32[]{:S(2)}) collective-permute-start(bf16[24,4096]{1,0:T(8,128)(2,1)S(1)} %get-tuple-element.125), channel_id=1, source_target_pairs={{0,48},{1,112},{2,50},{3,114},{4,52},{5,116},{6,54},{7,118},{8,56}... | collective-permute-start | bytes 589832 | tf_op jit(solution)/shard_map/ppermute | solution.py:52
  151.1 7.2 %collective-permute-start.38 = (bf16[24,4096]{1,0:T(8,128)(2,1)S(1)}, bf16[24,4096]{1,0:T(8,128)(2,1)S(1)}, u32[]{:S(2)}, u32[]{:S(2)}) collective-permute-start(bf16[24,4096]{1,0:T(8,128)(2,1)S(1)} %get-tuple-element.126), channel_id=1, source_target_pairs={{0,32},{1,96},{2,34},{3,98},{4,36},{5,100},{6,38},{7,102},{8,40},{... | collective-permute-start | bytes 589832 | tf_op jit(solution)/shard_map/ppermute | solution.py:52
  155.1 10.9 %collective-permute-start.39 = (bf16[24,4096]{1,0:T(8,128)(2,1)S(1)}, bf16[24,4096]{1,0:T(8,128)(2,1)S(1)}, u32[]{:S(2)}, u32[]{:S(2)}) collective-permute-start(bf16[24,4096]{1,0:T(8,128)(2,1)S(1)} %get-tuple-element.127), channel_id=1, source_target_pairs={{0,16},{1,80},{2,18},{3,82},{4,20},{5,84},{6,22},{7,86},{8,24},{9,... | collective-permute-start | bytes 589832 | tf_op jit(solution)/shard_map/ppermute | solution.py:52
  167.5 2.0 %collective-permute-start.43 = (f32[32,4096]{1,0:T(8,128)S(1)}, f32[32,4096]{1,0:T(8,128)S(1)}, u32[]{:S(2)}, u32[]{:S(2)}) collective-permute-start(f32[32,4096]{1,0:T(8,128)S(1)} %get-tuple-element.138), channel_id=1, source_target_pairs={{0,1},{1,0},{2,3},{3,2},{4,5},{5,4},{6,7},{7,6},{8,9},{9,8},{10,11... | collective-permute-start | bytes 1572872 | tf_op jit(solution)/shard_map/ppermute | solution.py:52

commit v2 on v0

v2 whole, which is shorter than its diff:
```python
import functools

import jax
import jax.numpy as jnp
from jax import lax
from jax.experimental import pallas as pl
from jax.experimental.pallas import tpu as pltpu
from jax.sharding import PartitionSpec as P

beta_first = 0.9
beta_second = 0.95
learn_rate = 0.01
weight_decay = 0.1
adam_epsilon = 1e-08
bias_first = 1.0 - 0.9**50
bias_second = 1.0 - 0.95**50

F32 = jnp.float32
BF16 = jnp.bfloat16
VMEM = pl.BlockSpec(memory_space=pltpu.VMEM)
SMEM = pl.BlockSpec(memory_space=pltpu.SMEM)
ANY = pl.BlockSpec(memory_space=pl.ANY)
NT = (((1,), (1,)), ((), ()))

SHIFTS = (0, -1, 1, 2)
AXES = ("xl", "z", "y", "xh", "core")
SLOTS = 12


def adamw_update(master, grads, first, second):
    moment_one = beta_first * first + (1.0 - beta_first) * grads
    moment_two = beta_second * second + (1.0 - beta_second) * grads * grads
    scaled = moment_one * (1.0 / bias_first)
    scaled = scaled / (jnp.sqrt(moment_two * (1.0 / bias_second)) + adam_epsilon)
    return master - learn_rate * (scaled + weight_decay * master)


def params(mib=20):
    return pltpu.CompilerParams(vmem_limit_bytes=mib << 20)


def cost(flops, nbytes):
    return pl.CostEstimate(flops=int(flops), bytes_accessed=int(nbytes), transcendentals=0)


def move(array, target):
    pairs = []
    for i in range(128):
        xl, z, y, xh, core = i // 64, i // 16 % 4, i // 4 % 4, i // 2 % 2, i % 2
        a, b, c, d, f = target(xl, z, y, xh, core)
        pairs.append((i, ((a * 4 + b % 4) * 4 + c % 4) * 4 + d * 2 + f))
    return lax.ppermute(array, AXES, pairs)


def move_y(array, shift):
    return move(array, lambda xl, z, y, xh, core: (xl, z, y + shift, xh, core))


def move_xh(array):
    return move(array, lambda xl, z, y, xh, core: (xl, z, y, 1 - xh, core))


def move_core(array):
    return move(array, lambda xl, z, y, xh, core: (xl, z, y, xh, 1 - core))


def staged(arrays):
    return lax.optimization_barrier(arrays)


def after(arrays, others):
    return lax.optimization_barrier((arrays, others))[0]


def adam_kernel(count, parts, rows, blocks_ref, *refs):
    ins, rest = refs[:4], refs[4:]
    new_ref, pieces = rest[-(count + 5)], rest[-(count + 4) : -4]
    held_ref, made_ref, in_sem, out_sem = rest[-4:]
    steps = [(i, p, q) for i in range(count) for p in range(parts) for q in range(rows // 384)]

    def at(ref, step):
        i, part, q = steps[step]
        start = pl.multiple_of(blocks_ref[i] * rows + q * 384, 384)
        return ref.at[0, part, pl.ds(start, 384)]

    copies = [
        [
            pltpu.make_async_copy(at(ref, step), held_ref.at[step, j], in_sem.at[step, j])
            for j, ref in enumerate(ins)
        ]
        for step in range(len(steps))
    ]
    for step in copies:
        for copy in step:
            copy.start()
    outs = []
    for step, (i, part, q) in enumerate(steps):
        for copy in copies[step]:
            copy.wait()

        def some(r, carry, step=step, i=i, part=part, q=q):
            here = pl.ds(pl.multiple_of(r * 64, 64), 64)
            new = adamw_update(*(held_ref[step, j, here] for j in range(4)))
            made_ref[step, here] = new
            pieces[i][part, pl.ds(pl.multiple_of(q * 384 + r * 64, 64), 64)] = new.astype(BF16)
            return carry

        lax.fori_loop(0, 6, some, 0)
        out = pltpu.make_async_copy(made_ref.at[step], at(new_ref, step), out_sem.at[step])
        out.start()
        outs.append(out)
    for out in outs:
        out.wait()


def adam(blocks, arrays, target, rows):
    count, parts = blocks.shape[0], arrays[0].shape[1]
    steps = count * parts * (rows // 384)
    given = [] if target is None else [target]
    return pl.pallas_call(
        functools.partial(adam_kernel, count, parts, rows),
        in_specs=[SMEM] + [ANY] * (4 + len(given)),
        out_specs=[ANY] + [VMEM] * count,
        out_shape=[jax.ShapeDtypeStruct(arrays[0].shape, F32)]
        + [jax.ShapeDtypeStruct((parts, rows, 256), BF16)] * count,
        scratch_shapes=[
            pltpu.VMEM((steps, 4, 384, 256), F32),
            pltpu.VMEM((steps, 384, 256), F32),
            pltpu.SemaphoreType.DMA((steps, 4)),
            pltpu.SemaphoreType.DMA((steps,)),
        ],
        input_output_aliases={5: 0} if given else {},
        cost_estimate=cost(0, count * parts * rows * 256 * 22),
        compiler_params=params(56),
        name="adam",
    )(blocks, *arrays, *given)


def packed_row(row):
    expert = (row * 2731) >> 16
    rest = row - 24 * expert
    half = (rest >= SLOTS).astype(jnp.int32)
    return expert, half, rest - SLOTS * half


def iota(shape, axis):
    return lax.broadcasted_iota(jnp.int32, shape, axis)


def dispatch_kernel(ids_ref, tokens_ref, out_ref):
    expert = iota((128, 32), 0)
    named = jnp.where((ids_ref[0:1, :] == expert) | (ids_ref[1:2, :] == expert), 1.0, 0.0)
    before = jnp.where(iota((32, 32), 0) < iota((32, 32), 1), 1.0, 0.0).astype(BF16)
    place = jnp.dot(named.astype(BF16), before, preferred_element_type=F32)
    place = jnp.where(named > 0.0, place, 99.0).astype(BF16)
    owner, _, _ = packed_row(iota((192, 128), 0))
    at_expert = jnp.where(owner == iota((192, 128), 1), 1.0, 0.0).astype(BF16)
    found = jnp.dot(at_expert, place, preferred_element_type=F32)
    _, half, slot = packed_row(iota((192, 32), 0))
    hit = found == slot.astype(F32)
    low = jnp.where(hit & (half == 0), 1.0, 0.0).astype(BF16)
    high = jnp.where(hit & (half == 1), 1.0, 0.0).astype(BF16)
    packed = jnp.dot(low, tokens_ref[:, :2048], preferred_element_type=F32)
    packed += jnp.dot(high, tokens_ref[:, 2048:], preferred_element_type=F32)
    for e in range(8):
        out_ref[e] = packed[e * 24 : (e + 1) * 24].astype(BF16)


def dispatch(ids, tokens):
    return pl.pallas_call(
        dispatch_kernel,
        in_specs=[VMEM] * 2,
        out_specs=VMEM,
        out_shape=jax.ShapeDtypeStruct((8, 24, 2048), BF16),
        cost_estimate=cost(2 * 192 * 64 * 2048, 2 << 20),
        compiler_params=params(),
        name="dispatch",
    )(ids, tokens)


def unpack_kernel(where_ref, packed_ref, head_ref, tail_ref):
    packed = jnp.concatenate([packed_ref[e].astype(F32) for e in range(8)], axis=0).astype(BF16)
    expert, half, slot = packed_row(iota((96, 192), 1))
    mine = iota((96, 192), 0) == expert * SLOTS + slot
    for h in range(2):
        taking = jnp.where(mine & (half == h), 1.0, 0.0).astype(BF16)
        rows = jnp.dot(taking, packed, preferred_element_type=F32)
        head_ref[:, h * 2048 : (h + 1) * 2048] = rows[:48].astype(BF16)
        tail_ref[:, h * 2048 : (h + 1) * 2048] = rows[48:].astype(BF16)


def unpack(where, packed):
    return pl.pallas_call(
        unpack_kernel,
        in_specs=[SMEM, VMEM],
        out_specs=[VMEM] * 2,
        out_shape=[jax.ShapeDtypeStruct((48, 4096), BF16)] * 2,
        cost_estimate=cost(4 * 96 * 192 * 2048, 2 << 20),
        compiler_params=params(),
        name="unpack",
    )(where, packed)


def mix_kernel(ids_ref, weights_ref, out_ref):
    expert = iota((128, 32), 0)
    first, second = ids_ref[0:1, :] == expert, ids_ref[1:2, :] == expert
    named = jnp.where(first | second, 1.0, 0.0)
    before = jnp.where(iota((32, 32), 0) < iota((32, 32), 1), 1.0, 0.0).astype(BF16)
    place = jnp.dot(named.astype(BF16), before, preferred_element_type=F32)
    place = jnp.where(named > 0.0, place, 99.0).astype(BF16)
    left = jnp.where(first, weights_ref[0:1, :], 0.0) + jnp.where(second, weights_ref[1:2, :], 0.0)
    owner, _, _ = packed_row(iota((192, 128), 0))
    at_expert = jnp.where(owner == iota((192, 128), 1), 1.0, 0.0).astype(BF16)
    found = jnp.dot(at_expert, place, preferred_element_type=F32)
    _, half, slot = packed_row(iota((192, 32), 0))
    hit = found == slot.astype(F32)
    same = jnp.where(iota((32, 32), 0) == iota((32, 32), 1), 1.0, 0.0).astype(BF16)
    for n in range(3):
        piece = left.astype(BF16)
        left = left - piece.astype(F32)
        spread = jnp.dot(at_expert, piece, preferred_element_type=F32)
        for h in range(2):
            part = jnp.where(hit & (half == h), spread, 0.0).astype(BF16)
            turned = lax.dot_general(same, part, NT, preferred_element_type=F32)
            out_ref[n * 64 + h * 32 : n * 64 + h * 32 + 32, :] = turned.astype(BF16)


def mix(ids, weights):
    return pl.pallas_call(
        mix_kernel,
        in_specs=[VMEM] * 2,
        out_specs=VMEM,
        out_shape=jax.ShapeDtypeStruct((192, 192), BF16),
        cost_estimate=cost(0, 1 << 18),
        compiler_params=params(),
        name="mix",
    )(ids, weights)


def combine_kernel(mixing_ref, back_ref, out_ref):
    for block in range(4):
        back = jnp.concatenate([back_ref[e * 4 + block].astype(F32) for e in range(8)], axis=0)
        mixed = jnp.dot(mixing_ref[...], back.astype(BF16), preferred_element_type=F32)
        for h in range(2):
            part = mixed[h * 32 : h * 32 + 32] + mixed[h * 32 + 64 : h * 32 + 96]
            part += mixed[h * 32 + 128 : h * 32 + 160]
            start = block * 1024 + h * 512
            out_ref[:, start : start + 512] = part.astype(BF16)


def combine(mixing, back):
    return pl.pallas_call(
        combine_kernel,
        in_specs=[VMEM] * 2,
        out_specs=VMEM,
        out_shape=jax.ShapeDtypeStruct((32, 4096), BF16),
        cost_estimate=cost(2 * 192 * 192 * 2048, 2 << 20),
        compiler_params=params(),
        name="combine",
    )(mixing, back)


def wrap(y):
    y = jnp.where(y >= 4, y - 4, y)
    return jnp.where(y < 0, y + 4, y)


PIECES = (((0, 0), (-1, 0), (1, 0), (0, 1)), ((2, 0), (-1, 1), (1, 1)), ((2, 1),))


def piece_columns(where_ref, crossed):
    y, xh, core = where_ref[0], where_ref[1], where_ref[2]
    core = 1 - core if crossed else core
    for f, group in enumerate(PIECES):
        for i, (shift, other) in enumerate(group):
            block = wrap(y + shift) * 4 + (1 - xh if other else xh) * 2 + core
            yield f, i, pl.ds(pl.multiple_of(block * 256, 256), 256)


def half_product(where_ref, x_ref, groups, x_copies, crossed, xc_ref, w_ref, w_sem):
    places = list(piece_columns(where_ref, crossed))
    copies = [
        pltpu.make_async_copy(
            groups[f].at[pl.ds(2 * i, 2)], w_ref.at[:, :, pl.ds(n * 256, 256)], w_sem.at[n]
        )
        for n, (f, i, _) in enumerate(places)
    ]
    for copy in x_copies + copies:
        copy.start()
    for copy in x_copies:
        copy.wait()
    for n, (_, _, columns) in enumerate(places):
        xc_ref[:, n * 256 : n * 256 + 256] = x_ref[:, columns]
    for copy in copies:
        copy.wait()
    return [
        lax.dot_general(xc_ref[...], w_ref[g], NT, preferred_element_type=F32) for g in range(2)
    ]


def first_half_kernel(where_ref, *refs):
    rows, groups = refs[:8], refs[8:11]
    x_ref, acc_ref, xc_ref, w_ref, x_sem, w_sem = refs[11:]
    x_copies = [
        pltpu.make_async_copy(rows[i], x_ref.at[pl.ds(i * 48, 48)], x_sem.at[i]) for i in range(8)
    ]
    products = half_product(where_ref, x_ref, groups, x_copies, False, xc_ref, w_ref, w_sem)
    acc_ref[0], acc_ref[1] = products


def last_half_kernel(where_ref, x_ref, acc_ref, *refs):
    groups, (hidden_ref, xc_ref, w_ref, w_sem) = refs[:3], refs[3:]
    gate, up = half_product(where_ref, x_ref, groups, [], True, xc_ref, w_ref, w_sem)
    gate, up = acc_ref[0] + gate, acc_ref[1] + up
    hidden_ref[...] = (gate / (1.0 + jnp.exp(-gate)) * up).astype(BF16)


HALF_SCRATCH = [pltpu.VMEM((384, 2048), BF16), pltpu.VMEM((2, 384, 2048), BF16)]


def first_half(where, rows, groups):
    return pl.pallas_call(
        first_half_kernel,
        in_specs=[SMEM] + [ANY] * 11,
        out_specs=[VMEM] * 2,
        out_shape=[
            jax.ShapeDtypeStruct((384, 4096), BF16),
            jax.ShapeDtypeStruct((2, 384, 384), F32),
        ],
        scratch_shapes=HALF_SCRATCH
        + [pltpu.SemaphoreType.DMA((8,)), pltpu.SemaphoreType.DMA((8,))],
        cost_estimate=cost(2 * 384 * 768 * 2048, 8 << 20),
        compiler_params=params(36),
        name="first_half",
    )(where, *rows, *groups)


def last_half(where, x, acc, groups):
    return pl.pallas_call(
        last_half_kernel,
        in_specs=[SMEM, VMEM, VMEM] + [ANY] * 3,
        out_specs=VMEM,
        out_shape=jax.ShapeDtypeStruct((384, 384), BF16),
        scratch_shapes=HALF_SCRATCH + [pltpu.SemaphoreType.DMA((8,))],
        cost_estimate=cost(2 * 384 * 768 * 2048, 8 << 20),
        compiler_params=params(),
        name="last_half",
    )(where, x, acc, *groups)


def place_gate_up_kernel(where_ref, *refs):
    groups, out_ref, sem = (refs[:3], refs[3:6]), refs[6], refs[7]
    first = pl.multiple_of((where_ref[1] * 2 + where_ref[2]) * 96, 96)
    copies = []
    for side in range(2):
        for n, (f, i, columns) in enumerate(piece_columns(where_ref, side == 1)):
            copies.append(
                pltpu.make_async_copy(
                    groups[side][f].at[pl.ds(2 * i, 2), pl.ds(first, 96), :],
                    out_ref.at[0, :, :, columns],
                    sem.at[side, n],
                )
            )
    for copy in copies:
        copy.start()
    for copy in copies:
        copy.wait()


def place_gate_up(where, groups):
    return pl.pallas_call(
        place_gate_up_kernel,
        in_specs=[SMEM] + [ANY] * 6,
        out_specs=VMEM,
        out_shape=jax.ShapeDtypeStruct((1, 2, 96, 4096), BF16),
        scratch_shapes=[pltpu.SemaphoreType.DMA((2, 8))],
        cost_estimate=cost(0, 4 << 20),
        compiler_params=params(),
        name="place_gate_up",
    )(where, *groups)


def spread_kernel(where_ref, *refs):
    downs, d_ref, slices, d_sem, out_sem = refs[:4], refs[4], refs[5:9], refs[9], refs[10]
    y, xh, core = where_ref[0], where_ref[1], where_ref[2]
    copies = []
    for side in range(2):
        rest, first = downs[2 * side], downs[2 * side + 1]
        from_core = 1 - core if side else core
        same, other = (
            pl.ds(pl.multiple_of((from_xh * 2 + from_core) * 256, 256), 256)
            for from_xh in (xh, 1 - xh)
        )
        for source, rows, columns in (
            (rest.at[pl.ds(0, 1536)], pl.ds(0, 1536), same),
            (rest.at[pl.ds(1536, 768)], pl.ds(768, 768), other),
            (first.at[2], pl.ds(0, 384), other),
            (first.at[3], pl.ds(384, 384), other),
        ):
            n = len(copies)
            copies.append(pltpu.make_async_copy(source, d_ref.at[rows, columns], d_sem.at[n]))
    for copy in copies:
        copy.start()
    for copy in copies:
        copy.wait()
    sends = []
    for j, shift in enumerate(SHIFTS):
        first = pl.multiple_of((wrap(y + shift) * 4 + xh * 2 + core) * 96, 96)
        send = pltpu.make_async_copy(d_ref.at[pl.ds(first, 96)], slices[j], out_sem.at[j])
        send.start()
        sends.append(send)
    for send in sends:
        send.wait()


def spread_down(where, downs):
    return pl.pallas_call(
        spread_kernel,
        in_specs=[SMEM] + [ANY] * 4,
        out_specs=[VMEM] * 5,
        out_shape=[jax.ShapeDtypeStruct((1536, 1024), BF16)]
        + [jax.ShapeDtypeStruct((96, 1024), BF16)] * 4,
        scratch_shapes=[pltpu.SemaphoreType.DMA((8,)), pltpu.SemaphoreType.DMA((4,))],
        cost_estimate=cost(0, 8 << 20),
        compiler_params=params(),
        name="spread_down",
    )(where, *downs)


def second_kernel(where_ref, *refs):
    hidden, d_ref, sent_ref, h_ref, out_ref, h_sem, out_sem = refs[:5], *refs[5:]
    y = where_ref[0]
    h_copies = []
    for d, shift in enumerate(SHIFTS):
        columns = pl.ds(pl.multiple_of(wrap(y + shift) * 384, 128), 384)
        for g, origin in enumerate(SHIFTS):
            there = [(s - origin + shift) % 4 for s in SHIFTS].index(0)
            h_copies.append(
                pltpu.make_async_copy(
                    hidden[d + there // 2].at[pl.ds(there % 2 * 96, 96)]
                    if d == 3
                    else hidden[d].at[pl.ds(there * 96, 96)],
                    h_ref.at[pl.ds(g * 96, 96), columns],
                    h_sem.at[d * 4 + g],
                )
            )
    for copy in h_copies:
        copy.start()
    for copy in h_copies:
        copy.wait()
    halves = [
        jnp.dot(h_ref[...], d_ref[:, h * 512 : h * 512 + 512], preferred_element_type=F32)
        for h in range(2)
    ]
    halves = [half.astype(BF16) for half in halves]
    expert, half, slot = packed_row(iota((192, 96), 0))
    mine = iota((192, 96), 1) == expert * SLOTS + slot
    packing = [jnp.where(mine & (half == h), 1.0, 0.0).astype(BF16) for h in range(2)]
    for g, shift in enumerate(SHIFTS):
        rows = slice(g * 96, (g + 1) * 96)
        packed = jnp.dot(packing[0], halves[0][rows], preferred_element_type=F32)
        packed += jnp.dot(packing[1], halves[1][rows], preferred_element_type=F32)
        for e in range(8):
            out_ref[e * 4 + wrap(y + shift)] = packed[e * 24 : (e + 1) * 24].astype(BF16)
    send = pltpu.make_async_copy(out_ref, sent_ref, out_sem)
    send.start()
    send.wait()


def second_matmul(where, hidden, down):
    return pl.pallas_call(
        second_kernel,
        in_specs=[SMEM] + [ANY] * 5 + [VMEM],
        out_specs=ANY,
        out_shape=jax.ShapeDtypeStruct((32, 24, 512), BF16),
        scratch_shapes=[
            pltpu.VMEM((384, 1536), BF16),
            pltpu.VMEM((32, 24, 512), BF16),
            pltpu.SemaphoreType.DMA((16,)),
            pltpu.SemaphoreType.DMA,
        ],
        cost_estimate=cost(2 * 384 * 1536 * 1024, 6 << 20),
        compiler_params=params(),
        name="second_matmul",
    )(where, *hidden, down)


def place_kernel(where_ref, *refs):
    parts, out_ref, sem = refs[:4], refs[4], refs[5]
    copies = []
    for j, shift in enumerate(SHIFTS):
        columns = pl.ds(pl.multiple_of(wrap(where_ref[0] - shift) * 1024, 1024), 1024)
        copies.append(pltpu.make_async_copy(parts[j], out_ref.at[0, :, columns], sem.at[j]))
    for copy in copies:
        copy.start()
    for copy in copies:
        copy.wait()


def place_down(where, parts):
    return pl.pallas_call(
        place_kernel,
        in_specs=[SMEM] + [ANY] * 4,
        out_specs=ANY,
        out_shape=jax.ShapeDtypeStruct((1, 96, 4096), BF16),
        scratch_shapes=[pltpu.SemaphoreType.DMA((4,))],
        cost_estimate=cost(0, 2 << 20),
        compiler_params=params(),
        name="place_down",
    )(where, *parts)


def body(
    master_gate_up,
    grad_gate_up,
    first_gate_up,
    second_gate_up,
    master_down,
    grad_down,
    first_down,
    second_down,
    tokens,
    route_ids,
    route_weights,
):
    y, xh, core = lax.axis_index("y"), lax.axis_index("xh"), lax.axis_index("core")
    where = jnp.stack([y, xh, core]).astype(jnp.int32)

    dispatched = dispatch(route_ids.T, tokens)
    packed = lax.all_to_all(dispatched, ("xl", "z"), split_axis=0, concat_axis=0, tiled=True)

    gate_up = (master_gate_up, grad_gate_up, first_gate_up, second_gate_up)
    near = jnp.stack([(y + 1) % 4, (y + 3) % 4, y]).astype(jnp.int32)
    near = after(near, dispatched)
    partial, to_next, to_last, stays = adam(near, gate_up, None, 384)
    from_last, from_next, stays_across = move_y(to_next, 1), move_y(to_last, -1), move_xh(stays)
    far = ((y + 2) % 4).astype(jnp.int32)[None]
    new_master_gate_up, to_far = adam(far, gate_up, partial, 384)

    down_arrays = tuple(a[:, None] for a in (master_down, grad_down, first_down, second_down))
    whole = after(jnp.zeros((1,), jnp.int32), to_far)
    new_master_down, down = adam(whole, down_arrays, None, 1536)
    new_master_down, down = new_master_down[:, 0], down[0]

    from_last, from_next, stays_across, packed, to_far, down = staged(
        (from_last, from_next, stays_across, packed, to_far, down)
    )
    head, tail = unpack(where, packed)
    from_far, last_head, next_tail = move_y(to_far, 2), move_y(head, 1), move_y(tail, -1)
    last_across, next_across = move_xh(from_last), move_xh(from_next)
    first_four = jnp.concatenate([stays, from_last, from_next, stays_across], axis=0)
    from_far, last_head, next_tail, last_across, next_across, down, first_four, head, tail = staged(
        (from_far, last_head, next_tail, last_across, next_across, down, first_four, head, tail)
    )
    far_head, far_tail = move_y(last_head, 1), move_y(next_tail, -1)
    last_tail, next_head = move_y(tail, 1), move_y(head, -1)
    far_across = move_xh(
        jnp.concatenate([from_far, down[:768].reshape(2, 384, 256)], axis=0)
    )
    second_three = jnp.concatenate([from_far, last_across, next_across], axis=0)
    rows = [head, tail, last_head, last_tail, next_head, next_tail, far_head, far_tail]
    rows, groups, down = staged((rows, [first_four, second_three, far_across], down))
    crossed = [move_core(group) for group in groups]
    down_across = move_xh(down[768:])
    mixing = mix(after(route_ids.T, down), route_weights.T)
    hidden = last_half(where, *first_half(where, rows, groups), crossed)

    from_last, from_next = move_y(hidden, 1), move_y(hidden, -1)
    far_first, far_second = move_y(from_last[:192], 1), move_y(from_next[192:], -1)
    hiddens = [hidden, from_last, from_next, far_first, far_second]
    rest = jnp.concatenate(after([down, down_across], hidden), axis=0)
    rest_crossed = move_core(rest)
    downs = [rest, groups[2], rest_crossed, crossed[2]]
    downs, *slices = spread_down(where, downs)
    slices = [slices[0]] + [move_y(part, shift) for part, shift in zip(slices[1:], SHIFTS[1:])]
    rollout_down = place_down(where, slices)
    hiddens, rollout_down = staged((hiddens, rollout_down))
    result = second_matmul(where, hiddens, downs)
    back = lax.all_to_all(result, ("xl", "z", "y"), split_axis=0, concat_axis=0, tiled=True)
    rollout_gate_up = place_gate_up(where, groups + crossed)
    moe_out = combine(mixing, back)
    return (new_master_gate_up, new_master_down, rollout_gate_up, rollout_down, moe_out)


def solution(mesh):
    parts = jax.sharding.Mesh(mesh.devices.reshape(2, 4, 4, 2, 2), AXES)
    exp, ten = ("xl", "z"), ("y", "xh", "core")
    wide, tall, rows = P(exp, None, None, ten), P(exp, None, ten), P(AXES, None)
    return jax.shard_map(
        body,
        mesh=parts,
        in_specs=(wide,) * 4 + (tall,) * 4 + (rows,) * 3,
        out_specs=(wide, tall, P(exp, None, ten, None), P(exp, ten, None), rows),
        check_vma=False,
    )
```

time: 390 us -> 139 us (0.36)
  waiting for transfers between devices: 245 us -> 46.7 us
  Pallas kernels: 0 us -> 38 us
  matrix products: 31.4 us -> 0 us
  local copies, waits for them, and re-layouts: 34.6 us -> 8.09 us
  starting transfers between devices: 18.6 us -> 43.3 us
  other arithmetic: 23.6 us -> 1.04 us
  blocking collectives: 21.9 us -> 0 us
  between operations: 14.2 us -> 0.95 us
    reduce_scatter x1 -> x0, waiting for transfers between devices: 187 us -> none  [body(): lax.psum_scatter(jnp.dot(hidden, rollout_down[0], preferred_element_type=...]
    all_to_all x3 -> x2, waiting for transfers between devices: 49.4 us -> 6.31 us  [the longest x1 6.31 us: body(): lax.all_to_all(result, ('xl', 'z', 'y'), split_axis=0, concat_axis=0, til...]
    ppermute x0 -> x25, waiting for transfers between devices: none -> 40.4 us  [move(): return lax.ppermute(array, AXES, pairs)]
    pallas_call x0 -> x13, Pallas kernels: none -> 38 us  [the longest x3 16.1 us: adam(): pl.pallas_call(functools.partial(adam_kernel, count, parts, rows), in_spe...]
    dot_general x4 -> x0, matrix products: 31.4 us -> none  [the longest x1 20.5 us: body(): jnp.dot(hidden, rollout_down[0], preferred_element_type=jnp.float32)]
    ppermute x0 -> x25, starting transfers between devices: none -> 31.3 us  [move(): return lax.ppermute(array, AXES, pairs)]
    all_to_all x1 -> x0, blocking collectives: 21.9 us -> none  [body(): lax.all_to_all(dispatch, 'exp', split_axis=0, concat_axis=0, tiled=True)]
    reshape x6 -> x0, local copies, waits for them, and re-layouts: 12.6 us -> none  [the longest x1 8.75 us: body(): send_down = local_down.reshape(1, 1, hidden_units, local_width)]
  transfers between devices with their start and end apart: 5 -> 27, of which waited for: 4 -> 14; matrix products, arithmetic and copies ran while one was open for 12% -> 1% of each run, Pallas kernels for 0% -> 23%
where the time goes in v2:
time: 139 us; the launch traced here: 138 us
  waiting for transfers between devices  46.7 us (34%)
  starting transfers between devices  43.3 us (31%)
  Pallas kernels  38 us (27%)
  local copies, waits for them, and re-layouts  8.09 us (6%)
    ppermute x25, waiting for transfers between devices, move(): return lax.ppermute(array, AXES, pairs)  40.4 us
    ppermute x25, starting transfers between devices, move(): return lax.ppermute(array, AXES, pairs)  31.3 us
    pallas_call x3, Pallas kernels, adam(): pl.pallas_call(functools.partial(adam_kernel, count, parts, rows), in_spe...  16.1 us
    unnamed x33, local copies, waits for them, and re-layouts  7.98 us
    all_to_all x1, starting transfers between devices, body(): lax.all_to_all(dispatched, ('xl', 'z'), split_axis=0, concat_axis=0, tile...  6.32 us
    all_to_all x1, waiting for transfers between devices, body(): lax.all_to_all(result, ('xl', 'z', 'y'), split_axis=0, concat_axis=0, til...  6.31 us
    all_to_all x1, starting transfers between devices, body(): lax.all_to_all(result, ('xl', 'z', 'y'), split_axis=0, concat_axis=0, til...  5.65 us
    pallas_call x1, Pallas kernels, first_half(): pl.pallas_call(first_half_kernel, in_specs=[SMEM] + [ANY] * 11, out_specs...  4.67 us
  transfers between devices with their start and end apart: 27, of which 14 were waited for; matrix products, arithmetic and copies ran while one was open for 1% of the time, Pallas kernels for 23%

profile of v2, /device:TPU:0, one launch (start us, length us, event | category | flops | bytes accessed | tf_op | source)
XLA Modules:
  0.0 138.0 jit_solution(2270174998337255416)
XLA Ops:
  0.6 0.9 copy-done.9
  2.3 1.7 %dispatch.1 = bf16[8,24,2048]{2,1,0:T(8,128)(2,1)} custom-call(s32[2,32]{1,0:T(2,128)S(1)} %bitcast.15, bf16[32,4096]{1,0:T(8,128)(2,1)S(1)} %copy-done.9), custom_call_target="tpu_custom_call" | custom-call | flops 50331648 | bytes 2097152 | tf_op jit(solution)/shard_map/dispatch/pallas_call | solution.py:170
  3.9 6.3 %all-to-all-start = ((bf16[8,24,2048]{2,1,0:T(8,128)(2,1)}), bf16[8,24,2048]{2,1,0:T(8,128)(2,1)S(1)}, u32[]{:S(2)}, u32[]{:S(2)}) async-start(bf16[8,24,2048]{2,1,0:T(8,128)(2,1)} %dispatch.1), calls=%async_computation | async-start | bytes 1572864 | tf_op jit(solution)/shard_map/all_to_all | solution.py:530
  10.9 7.2 %adam.3 = (f32[1,2,1536,256]{3,2,1,0:T(8,128)}, bf16[2,384,256]{2,1,0:T(8,128)(2,1)}, bf16[2,384,256]{2,1,0:T(8,128)(2,1)}, bf16[2,384,256]{2,1,0:T(8,128)(2,1)}) custom-call(s32[3]{0:T(128)} %get-tuple-element.60.blocks_ref, f32[1,2,1536,256]{3,2,1,0:T(8,128)} %refs_0_.3, f32[1,2,1536,256]{3,2,1,0:T(8,128)} %refs_1_.3, f32[1,2,1536,256]{3,2,1,0:T(8,128)} %refs_2_.3, ...), custom_call_target="tpu_custom_call" | custom-call | bytes 12976128 | tf_op jit(solution)/shard_map/adam/pallas_call | solution.py:120
  18.1 1.6 %collective-permute-start = (bf16[2,384,256]{2,1,0:T(8,128)(2,1)}, bf16[2,384,256]{2,1,0:T(8,128)(2,1)S(1)}, u32[]{:S(2)}, u32[]{:S(2)}) collective-permute-start(bf16[2,384,256]{2,1,0:T(8,128)(2,1)} %get-tuple-element.66), channel_id=1, source_target_pairs={{0,4},{1,5},{2,6},{3,7},{4,8},{5,9},{6,10},{7,11},{8,12},{9,13},{1... | collective-permute-start | bytes 1179656 | tf_op jit(solution)/shard_map/ppermute | solution.py:52
  19.7 1.7 %collective-permute-start.1 = (bf16[2,384,256]{2,1,0:T(8,128)(2,1)}, bf16[2,384,256]{2,1,0:T(8,128)(2,1)S(1)}, u32[]{:S(2)}, u32[]{:S(2)}) collective-permute-start(bf16[2,384,256]{2,1,0:T(8,128)(2,1)} %get-tuple-element.67), channel_id=1, source_target_pairs={{0,12},{1,13},{2,14},{3,15},{4,0},{5,1},{6,2},{7,3},{8,4},{9,5},{1... | collective-permute-start | bytes 1179656 | tf_op jit(solution)/shard_map/ppermute | solution.py:52
  21.4 2.7 %collective-permute-start.2 = (bf16[2,384,256]{2,1,0:T(8,128)(2,1)}, bf16[2,384,256]{2,1,0:T(8,128)(2,1)S(1)}, u32[]{:S(2)}, u32[]{:S(2)}) collective-permute-start(bf16[2,384,256]{2,1,0:T(8,128)(2,1)} %get-tuple-element.68), channel_id=1, source_target_pairs={{0,2},{1,3},{2,0},{3,1},{4,6},{5,7},{6,4},{7,5},{8,10},{9,11},{10,... | collective-permute-start | bytes 1179656 | tf_op jit(solution)/shard_map/ppermute | solution.py:52
  24.1 3.8 %adam.4 = (f32[1,2,1536,256]{3,2,1,0:T(8,128)}, bf16[2,384,256]{2,1,0:T(8,128)(2,1)}) custom-call(s32[1]{0:T(128)} %bitcast.blocks_ref, f32[1,2,1536,256]{3,2,1,0:T(8,128)} %refs_0_.3, f32[1,2,1536,256]{3,2,1,0:T(8,128)} %refs_1_.3, f32[1,2,1536,256]{3,2,1,0:T(8,128)} %refs_2_.3, f32[1,2,1536,256]{3,2,1,0:T(8,128)} %refs_3_.3, ...), custom_call_target="tpu_custom_call", output_to_operand_aliasing={{0}: (5, {})} | custom-call | bytes 4325376 | tf_op jit(solution)/shard_map/adam/pallas_call | solution.py:120
  28.0 5.2 %adam.5 = (f32[1,1,1536,256]{3,2,1,0:T(8,128)}, bf16[1,1536,256]{2,1,0:T(8,128)(2,1)}) custom-call(s32[1]{0:T(128)} %constant.37.clone.1.blocks_ref, f32[1,1,1536,256]{3,2,1,0:T(8,128)} %bitcast.22, f32[1,1,1536,256]{3,2,1,0:T(8,128)} %bitcast.23, f32[1,1,1536,256]{3,2,1,0:T(8,128)} %bitcast.24, f32[1,1,1536,256]{3,2,1,0:T(8,128)} %bitcast.25), custom_call_target="tpu_custom_call" | custom-call | bytes 8650752 | tf_op jit(solution)/shard_map/adam/pallas_call | solution.py:120
  33.3 2.0 %collective-permute-start.3 = (bf16[2,384,256]{2,1,0:T(8,128)(2,1)S(1)}, bf16[2,384,256]{2,1,0:T(8,128)(2,1)S(1)}, u32[]{:S(2)}, u32[]{:S(2)}) collective-permute-start(bf16[2,384,256]{2,1,0:T(8,128)(2,1)S(1)} %copy-done.15), channel_id=1, source_target_pairs={{0,8},{1,9},{2,10},{3,11},{4,12},{5,13},{6,14},{7,15},{8,0},{9,1},... | collective-permute-start | bytes 1179656 | tf_op jit(solution)/shard_map/ppermute | solution.py:52
  35.3 2.6 %collective-permute-start.6 = (bf16[2,384,256]{2,1,0:T(8,128)(2,1)S(1)}, bf16[2,384,256]{2,1,0:T(8,128)(2,1)S(1)}, u32[]{:S(2)}, u32[]{:S(2)}) collective-permute-start(bf16[2,384,256]{2,1,0:T(8,128)(2,1)S(1)} %collective-permute-done), channel_id=1, source_target_pairs={{0,2},{1,3},{2,0},{3,1},{4,6},{5,7},{6,4},{7,5},{8,10},{9,11},{10,... | collective-permute-start | bytes 1179656 | tf_op jit(solution)/shard_map/ppermute | solution.py:52
  37.8 0.9 collective-permute-start.7
  38.8 0.9 unpack.1
  40.5 2.6 %collective-permute-start.5 = (bf16[48,4096]{1,0:T(8,128)(2,1)S(1)}, bf16[48,4096]{1,0:T(8,128)(2,1)S(1)}, u32[]{:S(2)}, u32[]{:S(2)}) collective-permute-start(bf16[48,4096]{1,0:T(8,128)(2,1)S(1)} %get-tuple-element.91.refs_1_), channel_id=1, source_target_pairs={{0,12},{1,13},{2,14},{3,15},{4,0},{5,1},{6,2},{7,3},{8,4},{9,5},{1... | collective-permute-start | bytes 1179656 | tf_op jit(solution)/shard_map/ppermute | solution.py:52
  43.2 3.6 %collective-permute-done.3 = bf16[2,384,256]{2,1,0:T(8,128)(2,1)S(1)} collective-permute-done((bf16[2,384,256]{2,1,0:T(8,128)(2,1)S(1)}, bf16[2,384,256]{2,1,0:T(8,128)(2,1)S(1)}, u32[]{:S(2)}, u32[]{:S(2)}) %collective-permute-start.3) | collective-permute-done | bytes 393248 | tf_op jit(solution)/shard_map/ppermute | solution.py:52
  46.8 2.0 %collective-permute-done.6 = bf16[2,384,256]{2,1,0:T(8,128)(2,1)S(1)} collective-permute-done((bf16[2,384,256]{2,1,0:T(8,128)(2,1)S(1)}, bf16[2,384,256]{2,1,0:T(8,128)(2,1)S(1)}, u32[]{:S(2)}, u32[]{:S(2)}) %collective-permute-start.6) | collective-permute-done | bytes 393248 | tf_op jit(solution)/shard_map/ppermute | solution.py:52
  48.8 5.8 %collective-permute-done.7 = bf16[2,384,256]{2,1,0:T(8,128)(2,1)S(1)} collective-permute-done((bf16[2,384,256]{2,1,0:T(8,128)(2,1)S(1)}, bf16[2,384,256]{2,1,0:T(8,128)(2,1)S(1)}, u32[]{:S(2)}, u32[]{:S(2)}) %collective-permute-start.7) | collective-permute-done | bytes 393248 | tf_op jit(solution)/shard_map/ppermute | solution.py:52
  54.8 2.0 %collective-permute-start.12 = (bf16[4,384,256]{2,1,0:T(8,128)(2,1)S(1)}, bf16[4,384,256]{2,1,0:T(8,128)(2,1)S(1)}, u32[]{:S(2)}, u32[]{:S(2)}) collective-permute-start(bf16[4,384,256]{2,1,0:T(8,128)(2,1)S(1)} %pad_maximum_fusion.2), channel_id=1, source_target_pairs={{0,2},{1,3},{2,0},{3,1},{4,6},{5,7},{6,4},{7,5},{8,10},{9,11},{10,... | collective-permute-start | bytes 2359304 | tf_op jit(solution)/shard_map/ppermute | solution.py:52
  56.8 1.1 collective-permute-start.9
  57.8 1.0 collective-permute-start.8
  59.5 2.6 %collective-permute-start.11 = (bf16[48,4096]{1,0:T(8,128)(2,1)S(1)}, bf16[48,4096]{1,0:T(8,128)(2,1)S(1)}, u32[]{:S(2)}, u32[]{:S(2)}) collective-permute-start(bf16[48,4096]{1,0:T(8,128)(2,1)S(1)} %collective-permute-done.5.refs_5_), channel_id=1, source_target_pairs={{0,12},{1,13},{2,14},{3,15},{4,0},{5,1},{6,2},{7,3},{8,4},{9,5},{1... | collective-permute-start | bytes 1179656 | tf_op jit(solution)/shard_map/ppermute | solution.py:52
  62.2 6.6 %collective-permute-done.9.refs_4_ = bf16[48,4096]{1,0:T(8,128)(2,1)S(1)} collective-permute-done((bf16[48,4096]{1,0:T(8,128)(2,1)S(1)}, bf16[48,4096]{1,0:T(8,128)(2,1)S(1)}, u32[]{:S(2)}, u32[]{:S(2)}) %collective-permute-start.9) | collective-permute-done | bytes 393248 | tf_op jit(solution)/shard_map/ppermute | solution.py:52
  68.7 2.4 %collective-permute-done.8.refs_3_ = bf16[48,4096]{1,0:T(8,128)(2,1)S(1)} collective-permute-done((bf16[48,4096]{1,0:T(8,128)(2,1)S(1)}, bf16[48,4096]{1,0:T(8,128)(2,1)S(1)}, u32[]{:S(2)}, u32[]{:S(2)}) %collective-permute-start.8) | collective-permute-done | bytes 393248 | tf_op jit(solution)/shard_map/ppermute | solution.py:52
  71.1 4.4 %collective-permute-done.10.refs_6_ = bf16[48,4096]{1,0:T(8,128)(2,1)S(1)} collective-permute-done((bf16[48,4096]{1,0:T(8,128)(2,1)S(1)}, bf16[48,4096]{1,0:T(8,128)(2,1)S(1)}, u32[]{:S(2)}, u32[]{:S(2)}) %collective-permute-start.10) | collective-permute-done | bytes 393248 | tf_op jit(solution)/shard_map/ppermute | solution.py:52
  76.3 1.8 %collective-permute-start.20 = (bf16[768,256]{1,0:T(8,128)(2,1)S(1)}, bf16[768,256]{1,0:T(8,128)(2,1)S(1)}, u32[]{:S(2)}, u32[]{:S(2)}) collective-permute-start(bf16[768,256]{1,0:T(8,128)(2,1)S(1)} %slice.15), channel_id=1, source_target_pairs={{0,2},{1,3},{2,0},{3,1},{4,6},{5,7},{6,4},{7,5},{8,10},{9,11},{10,... | collective-permute-start | bytes 1179656 | tf_op jit(solution)/shard_map/ppermute | solution.py:52
  78.1 4.7 %first_half.1 = (bf16[384,4096]{1,0:T(8,128)(2,1)S(1)}, f32[2,384,384]{2,1,0:T(8,128)S(1)}) custom-call(s32[3]{0:T(128)S(1)} %get-tuple-element.116.where_ref, bf16[48,4096]{1,0:T(8,128)(2,1)S(1)} %get-tuple-element.90.refs_0_, bf16[48,4096]{1,0:T(8,128)(2,1)S(1)} %get-tuple-element.91.refs_1_, bf16[48,4096]{1,0:T(8,128)(2,1)S(1)} %collective-permute-done.4.refs_2_, ...), custom_call_target="tpu_custom_call" | custom-call | flops 1207959552 | bytes 8388608 | tf_op jit(solution)/shard_map/first_half/pallas_call | solution.py:322
  82.8 3.1 %last_half.1.refs_0_ = bf16[384,384]{1,0:T(8,128)(2,1)S(1)} custom-call(s32[3]{0:T(128)S(1)} %get-tuple-element.116.where_ref, bf16[384,4096]{1,0:T(8,128)(2,1)S(1)} %get-tuple-element.98.x_ref, f32[2,384,384]{2,1,0:T(8,128)S(1)} %get-tuple-element.99.acc_ref, bf16[8,384,256]{2,1,0:T(8,128)(2,1)S(1)} %collective-permute-done.13.refs_3_.refs_0_, ...), custom_call_target="tpu_custom_call" | custom-call | flops 1207959552 | bytes 8388608 | tf_op jit(solution)/shard_map/last_half/pallas_call | solution.py:339
  86.0 3.5 %collective-permute-done.20 = bf16[768,256]{1,0:T(8,128)(2,1)S(1)} collective-permute-done((bf16[768,256]{1,0:T(8,128)(2,1)S(1)}, bf16[768,256]{1,0:T(8,128)(2,1)S(1)}, u32[]{:S(2)}, u32[]{:S(2)}) %collective-permute-start.20) | collective-permute-done | bytes 393248 | tf_op jit(solution)/shard_map/ppermute | solution.py:52
  89.9 1.8 %collective-permute-start.16 = (bf16[384,384]{1,0:T(8,128)(2,1)S(1)}, bf16[384,384]{1,0:T(8,128)(2,1)S(1)}, u32[]{:S(2)}, u32[]{:S(2)}) collective-permute-start(bf16[384,384]{1,0:T(8,128)(2,1)S(1)} %last_half.1.refs_0_), channel_id=1, source_target_pairs={{0,4},{1,5},{2,6},{3,7},{4,8},{5,9},{6,10},{7,11},{8,12},{9,13},{1... | collective-permute-start | bytes 884744 | tf_op jit(solution)/shard_map/ppermute | solution.py:52
  92.5 2.2 %spread_down.1 = (bf16[1536,1024]{1,0:T(8,128)(2,1)S(1)}, bf16[96,1024]{1,0:T(8,128)(2,1)S(1)}, bf16[96,1024]{1,0:T(8,128)(2,1)S(1)}, bf16[96,1024]{1,0:T(8,128)(2,1)S(1)}, bf16[96,1024]{1,0:T(8,128)(2,1)S(1)}) custom-call(s32[3]{0:T(128)S(1)} %get-tuple-element.116.where_ref, bf16[2304,256]{1,0:T(8,128)(2,1)S(1)} %constant_dynamic-update-slice_fusion.refs_0_, ...), custom_call_target="tpu_custom_call" | custom-call | bytes 8388608 | tf_op jit(solution)/shard_map/spread_down/pallas_call | solution.py:417
  95.4 1.4 collective-permute-start.23
  96.9 2.6 %collective-permute-done.17.refs_2_ = bf16[384,384]{1,0:T(8,128)(2,1)S(1)} collective-permute-done((bf16[384,384]{1,0:T(8,128)(2,1)S(1)}, bf16[384,384]{1,0:T(8,128)(2,1)S(1)}, u32[]{:S(2)}, u32[]{:S(2)}) %collective-permute-start.17) | collective-permute-done | bytes 294944 | tf_op jit(solution)/shard_map/ppermute | solution.py:52
  99.6 1.5 %collective-permute-start.19 = (bf16[192,384]{1,0:T(8,128)(2,1)S(1)}, bf16[192,384]{1,0:T(8,128)(2,1)S(1)}, u32[]{:S(2)}, u32[]{:S(2)}) collective-permute-start(bf16[192,384]{1,0:T(8,128)(2,1)S(1)} %slice.17), channel_id=1, source_target_pairs={{0,12},{1,13},{2,14},{3,15},{4,0},{5,1},{6,2},{7,3},{8,4},{9,5},{1... | collective-permute-start | bytes 442376 | tf_op jit(solution)/shard_map/ppermute | solution.py:52
  101.8 2.0 %collective-permute-done.22.refs_1_ = bf16[96,1024]{1,0:T(8,128)(2,1)S(1)} collective-permute-done((bf16[96,1024]{1,0:T(8,128)(2,1)S(1)}, bf16[96,1024]{1,0:T(8,128)(2,1)S(1)}, u32[]{:S(2)}, u32[]{:S(2)}) %collective-permute-start.22) | collective-permute-done | bytes 196640 | tf_op jit(solution)/shard_map/ppermute | solution.py:52
  103.8 5.6 %collective-permute-done.23.refs_2_ = bf16[96,1024]{1,0:T(8,128)(2,1)S(1)} collective-permute-done((bf16[96,1024]{1,0:T(8,128)(2,1)S(1)}, bf16[96,1024]{1,0:T(8,128)(2,1)S(1)}, u32[]{:S(2)}, u32[]{:S(2)}) %collective-permute-start.23) | collective-permute-done | bytes 196640 | tf_op jit(solution)/shard_map/ppermute | solution.py:52
  109.4 1.5 %place_down.1 = bf16[1,96,4096]{2,1,0:T(8,128)(2,1)} custom-call(s32[3]{0:T(128)S(1)} %get-tuple-element.116.where_ref, bf16[96,1024]{1,0:T(8,128)(2,1)S(1)} %get-tuple-element.103.refs_0_, bf16[96,1024]{1,0:T(8,128)(2,1)S(1)} %collective-permute-done.22.refs_1_, bf16[96,1024]{1,0:T(8,128)(2,1)S(1)} %collective-permute-done.23.refs_2_, ...), custom_call_target="tpu_custom_call" | custom-call | bytes 2097152 | tf_op jit(solution)/shard_map/place_down/pallas_call | solution.py:501
  110.9 1.0 collective-permute-done.18.refs_3_
  111.9 2.8 %second_matmul.1 = bf16[32,24,512]{2,1,0:T(8,128)(2,1)S(1)} custom-call(s32[3]{0:T(128)S(1)} %get-tuple-element.116.where_ref, bf16[384,384]{1,0:T(8,128)(2,1)S(1)} %last_half.1.refs_0_, bf16[384,384]{1,0:T(8,128)(2,1)S(1)} %collective-permute-done.16.refs_1_, bf16[384,384]{1,0:T(8,128)(2,1)S(1)} %collective-permute-done.17.refs_2_, ...), custom_call_target="tpu_custom_call" | custom-call | flops 1207959552 | bytes 6291456 | tf_op jit(solution)/shard_map/second_matmul/pallas_call | solution.py:471
  114.7 0.9 copy-done.6
  115.6 5.7 %all-to-all-start.1 = ((bf16[32,24,512]{2,1,0:T(8,128)(2,1)}), bf16[32,24,512]{2,1,0:T(8,128)(2,1)}, u32[]{:S(2)}, u32[]{:S(2)}) async-start(bf16[32,24,512]{2,1,0:T(8,128)(2,1)} %copy-done.6), calls=%async_computation.1 | async-start | bytes 1572864 | tf_op jit(solution)/shard_map/all_to_all | solution.py:579
  121.3 0.8 mix.1.mixing_ref
  122.7 1.1 copy-done.1
  123.9 1.4 %copy-done.3 = bf16[8,384,256]{2,1,0:T(8,128)(2,1)S(1)} copy-done((bf16[8,384,256]{2,1,0:T(8,128)(2,1)S(1)}, bf16[8,384,256]{2,1,0:T(8,128)(2,1)}, u32[]{:S(2)}) %copy-start.3) | copy-done | bytes 1572888
  125.3 1.3 copy-done.5
  126.6 2.1 %place_gate_up.1 = bf16[1,2,96,4096]{3,2,1,0:T(8,128)(2,1)} custom-call(s32[3]{0:T(128)S(1)} %get-tuple-element.116.where_ref, bf16[8,384,256]{2,1,0:T(8,128)(2,1)S(1)} %pad_maximum_fusion.refs_0_.refs_8_, bf16[6,384,256]{2,1,0:T(8,128)(2,1)S(1)} %pad_maximum_fusion.1.refs_1_.refs_9_, bf16[4,384,256]{2,1,0:T(8,128)(2,1)S(1)} %copy-done.1, ...), custom_call_target="tpu_custom_call" | custom-call | bytes 4194304 | tf_op jit(solution)/shard_map/place_gate_up/pallas_call | solution.py:371
  128.7 6.3 %all-to-all-done.1.back_ref = bf16[32,24,512]{2,1,0:T(8,128)(2,1)} async-done(((bf16[32,24,512]{2,1,0:T(8,128)(2,1)}), bf16[32,24,512]{2,1,0:T(8,128)(2,1)}, u32[]{:S(2)}, u32[]{:S(2)}) %all-to-all-start.1) | async-done | bytes 786464 | tf_op jit(solution)/shard_map/all_to_all | solution.py:579
  135.0 0.9 copy-done.8
  135.9 2.2 %combine.1 = bf16[32,4096]{1,0:T(8,128)(2,1)} custom-call(bf16[192,192]{1,0:T(8,128)(2,1)S(1)} %copy-done.8, bf16[32,24,512]{2,1,0:T(8,128)(2,1)} %all-to-all-done.1.back_ref), custom_call_target="tpu_custom_call" | custom-call | flops 150994944 | bytes 2097152 | tf_op jit(solution)/shard_map/combine/pallas_call | solution.py:252
  (61 shorter events, 7.6 us)
Async XLA Ops:
  0.6 1.0 copy-start.9
  1.6 0.7 copy-start.10
  3.9 29.3 %all-to-all-start = ((bf16[8,24,2048]{2,1,0:T(8,128)(2,1)}), bf16[8,24,2048]{2,1,0:T(8,128)(2,1)S(1)}, u32[]{:S(2)}, u32[]{:S(2)}) async-start(bf16[8,24,2048]{2,1,0:T(8,128)(2,1)} %dispatch.1), calls=%async_computation | async-start | bytes 1572864 | tf_op jit(solution)/shard_map/all_to_all | solution.py:530
  18.1 15.0 %collective-permute-start = (bf16[2,384,256]{2,1,0:T(8,128)(2,1)}, bf16[2,384,256]{2,1,0:T(8,128)(2,1)S(1)}, u32[]{:S(2)}, u32[]{:S(2)}) collective-permute-start(bf16[2,384,256]{2,1,0:T(8,128)(2,1)} %get-tuple-element.66), channel_id=1, source_target_pairs={{0,4},{1,5},{2,6},{3,7},{4,8},{5,9},{6,10},{7,11},{8,12},{9,13},{1... | collective-permute-start | bytes 1179656 | tf_op jit(solution)/shard_map/ppermute | solution.py:52
  19.7 13.4 %collective-permute-start.1 = (bf16[2,384,256]{2,1,0:T(8,128)(2,1)}, bf16[2,384,256]{2,1,0:T(8,128)(2,1)S(1)}, u32[]{:S(2)}, u32[]{:S(2)}) collective-permute-start(bf16[2,384,256]{2,1,0:T(8,128)(2,1)} %get-tuple-element.67), channel_id=1, source_target_pairs={{0,12},{1,13},{2,14},{3,15},{4,0},{5,1},{6,2},{7,3},{8,4},{9,5},{1... | collective-permute-start | bytes 1179656 | tf_op jit(solution)/shard_map/ppermute | solution.py:52
  21.4 11.9 %collective-permute-start.2 = (bf16[2,384,256]{2,1,0:T(8,128)(2,1)}, bf16[2,384,256]{2,1,0:T(8,128)(2,1)S(1)}, u32[]{:S(2)}, u32[]{:S(2)}) collective-permute-start(bf16[2,384,256]{2,1,0:T(8,128)(2,1)} %get-tuple-element.68), channel_id=1, source_target_pairs={{0,2},{1,3},{2,0},{3,1},{4,6},{5,7},{6,4},{7,5},{8,10},{9,11},{10,... | collective-permute-start | bytes 1179656 | tf_op jit(solution)/shard_map/ppermute | solution.py:52
  28.0 5.3 %copy-start.15 = (bf16[2,384,256]{2,1,0:T(8,128)(2,1)S(1)}, bf16[2,384,256]{2,1,0:T(8,128)(2,1)}, u32[]{:S(2)}) copy-start(bf16[2,384,256]{2,1,0:T(8,128)(2,1)} %get-tuple-element.70) | copy-start | bytes 1179652
  28.0 15.1 %copy-start.14 = (bf16[2,384,256]{2,1,0:T(8,128)(2,1)S(1)}, bf16[2,384,256]{2,1,0:T(8,128)(2,1)}, u32[]{:S(2)}) copy-start(bf16[2,384,256]{2,1,0:T(8,128)(2,1)} %get-tuple-element.68) | copy-start | bytes 1179652
  33.3 13.6 %collective-permute-start.3 = (bf16[2,384,256]{2,1,0:T(8,128)(2,1)S(1)}, bf16[2,384,256]{2,1,0:T(8,128)(2,1)S(1)}, u32[]{:S(2)}, u32[]{:S(2)}) collective-permute-start(bf16[2,384,256]{2,1,0:T(8,128)(2,1)S(1)} %copy-done.15), channel_id=1, source_target_pairs={{0,8},{1,9},{2,10},{3,11},{4,12},{5,13},{6,14},{7,15},{8,0},{9,1},... | collective-permute-start | bytes 1179656 | tf_op jit(solution)/shard_map/ppermute | solution.py:52
  35.3 13.6 %collective-permute-start.6 = (bf16[2,384,256]{2,1,0:T(8,128)(2,1)S(1)}, bf16[2,384,256]{2,1,0:T(8,128)(2,1)S(1)}, u32[]{:S(2)}, u32[]{:S(2)}) collective-permute-start(bf16[2,384,256]{2,1,0:T(8,128)(2,1)S(1)} %collective-permute-done), channel_id=1, source_target_pairs={{0,2},{1,3},{2,0},{3,1},{4,6},{5,7},{6,4},{7,5},{8,10},{9,11},{10,... | collective-permute-start | bytes 1179656 | tf_op jit(solution)/shard_map/ppermute | solution.py:52
  37.8 16.8 %collective-permute-start.7 = (bf16[2,384,256]{2,1,0:T(8,128)(2,1)S(1)}, bf16[2,384,256]{2,1,0:T(8,128)(2,1)S(1)}, u32[]{:S(2)}, u32[]{:S(2)}) collective-permute-start(bf16[2,384,256]{2,1,0:T(8,128)(2,1)S(1)} %collective-permute-done.1), channel_id=1, source_target_pairs={{0,2},{1,3},{2,0},{3,1},{4,6},{5,7},{6,4},{7,5},{8,10},{9,11},{10,... | collective-permute-start | bytes 1179656 | tf_op jit(solution)/shard_map/ppermute | solution.py:52
  39.7 14.9 %collective-permute-start.4 = (bf16[48,4096]{1,0:T(8,128)(2,1)S(1)}, bf16[48,4096]{1,0:T(8,128)(2,1)S(1)}, u32[]{:S(2)}, u32[]{:S(2)}) collective-permute-start(bf16[48,4096]{1,0:T(8,128)(2,1)S(1)} %get-tuple-element.90.refs_0_), channel_id=1, source_target_pairs={{0,4},{1,5},{2,6},{3,7},{4,8},{5,9},{6,10},{7,11},{8,12},{9,13},{1... | collective-permute-start | bytes 1179656 | tf_op jit(solution)/shard_map/ppermute | solution.py:52
  40.4 14.2 %copy-start.13 = (bf16[1,1536,256]{2,1,0:T(8,128)(2,1)S(1)}, bf16[1,1536,256]{2,1,0:T(8,128)(2,1)}, u32[]{:S(2)}) copy-start(bf16[1,1536,256]{2,1,0:T(8,128)(2,1)} %get-tuple-element.69) | copy-start | bytes 2359300
  40.5 14.2 %collective-permute-start.5 = (bf16[48,4096]{1,0:T(8,128)(2,1)S(1)}, bf16[48,4096]{1,0:T(8,128)(2,1)S(1)}, u32[]{:S(2)}, u32[]{:S(2)}) collective-permute-start(bf16[48,4096]{1,0:T(8,128)(2,1)S(1)} %get-tuple-element.91.refs_1_), channel_id=1, source_target_pairs={{0,12},{1,13},{2,14},{3,15},{4,0},{5,1},{6,2},{7,3},{8,4},{9,5},{1... | collective-permute-start | bytes 1179656 | tf_op jit(solution)/shard_map/ppermute | solution.py:52
  54.8 20.8 %collective-permute-start.12 = (bf16[4,384,256]{2,1,0:T(8,128)(2,1)S(1)}, bf16[4,384,256]{2,1,0:T(8,128)(2,1)S(1)}, u32[]{:S(2)}, u32[]{:S(2)}) collective-permute-start(bf16[4,384,256]{2,1,0:T(8,128)(2,1)S(1)} %pad_maximum_fusion.2), channel_id=1, source_target_pairs={{0,2},{1,3},{2,0},{3,1},{4,6},{5,7},{6,4},{7,5},{8,10},{9,11},{10,... | collective-permute-start | bytes 2359304 | tf_op jit(solution)/shard_map/ppermute | solution.py:52
  56.8 12.0 %collective-permute-start.9 = (bf16[48,4096]{1,0:T(8,128)(2,1)S(1)}, bf16[48,4096]{1,0:T(8,128)(2,1)S(1)}, u32[]{:S(2)}, u32[]{:S(2)}) collective-permute-start(bf16[48,4096]{1,0:T(8,128)(2,1)S(1)} %get-tuple-element.90.refs_0_), channel_id=1, source_target_pairs={{0,12},{1,13},{2,14},{3,15},{4,0},{5,1},{6,2},{7,3},{8,4},{9,5},{1... | collective-permute-start | bytes 1179656 | tf_op jit(solution)/shard_map/ppermute | solution.py:52
  57.8 13.3 %collective-permute-start.8 = (bf16[48,4096]{1,0:T(8,128)(2,1)S(1)}, bf16[48,4096]{1,0:T(8,128)(2,1)S(1)}, u32[]{:S(2)}, u32[]{:S(2)}) collective-permute-start(bf16[48,4096]{1,0:T(8,128)(2,1)S(1)} %get-tuple-element.91.refs_1_), channel_id=1, source_target_pairs={{0,4},{1,5},{2,6},{3,7},{4,8},{5,9},{6,10},{7,11},{8,12},{9,13},{1... | collective-permute-start | bytes 1179656 | tf_op jit(solution)/shard_map/ppermute | solution.py:52
  58.8 16.7 %collective-permute-start.10 = (bf16[48,4096]{1,0:T(8,128)(2,1)S(1)}, bf16[48,4096]{1,0:T(8,128)(2,1)S(1)}, u32[]{:S(2)}, u32[]{:S(2)}) collective-permute-start(bf16[48,4096]{1,0:T(8,128)(2,1)S(1)} %collective-permute-done.4.refs_2_), channel_id=1, source_target_pairs={{0,4},{1,5},{2,6},{3,7},{4,8},{5,9},{6,10},{7,11},{8,12},{9,13},{1... | collective-permute-start | bytes 1179656 | tf_op jit(solution)/shard_map/ppermute | solution.py:52
  59.5 16.0 %collective-permute-start.11 = (bf16[48,4096]{1,0:T(8,128)(2,1)S(1)}, bf16[48,4096]{1,0:T(8,128)(2,1)S(1)}, u32[]{:S(2)}, u32[]{:S(2)}) collective-permute-start(bf16[48,4096]{1,0:T(8,128)(2,1)S(1)} %collective-permute-done.5.refs_5_), channel_id=1, source_target_pairs={{0,12},{1,13},{2,14},{3,15},{4,0},{5,1},{6,2},{7,3},{8,4},{9,5},{1... | collective-permute-start | bytes 1179656 | tf_op jit(solution)/shard_map/ppermute | solution.py:52
  75.5 17.0 %copy-start = (bf16[4,384,256]{2,1,0:T(8,128)(2,1)}, bf16[4,384,256]{2,1,0:T(8,128)(2,1)S(1)}, u32[]{:S(2)}) copy-start(bf16[4,384,256]{2,1,0:T(8,128)(2,1)S(1)} %collective-permute-done.12.refs_2_.refs_10_.refs_1_) | copy-start | bytes 2359300
  75.5 7.3 %collective-permute-start.13 = (bf16[8,384,256]{2,1,0:T(8,128)(2,1)S(1)}, bf16[8,384,256]{2,1,0:T(8,128)(2,1)S(1)}, u32[]{:S(2)}, u32[]{:S(2)}) collective-permute-start(bf16[8,384,256]{2,1,0:T(8,128)(2,1)S(1)} %pad_maximum_fusion.refs_0_.refs_8_), channel_id=1, source_target_pairs={{0,1},{1,0},{2,3},{3,2},{4,5},{5,4},{6,7},{7,6},{8,9},{9,8},{10,11... | collective-permute-start | bytes 4718600 | tf_op jit(solution)/shard_map/ppermute | solution.py:52
  75.6 7.2 %collective-permute-start.14 = (bf16[6,384,256]{2,1,0:T(8,128)(2,1)S(1)}, bf16[6,384,256]{2,1,0:T(8,128)(2,1)S(1)}, u32[]{:S(2)}, u32[]{:S(2)}) collective-permute-start(bf16[6,384,256]{2,1,0:T(8,128)(2,1)S(1)} %pad_maximum_fusion.1.refs_1_.refs_9_), channel_id=1, source_target_pairs={{0,1},{1,0},{2,3},{3,2},{4,5},{5,4},{6,7},{7,6},{8,9},{9,8},{10,11... | collective-permute-start | bytes 3538952 | tf_op jit(solution)/shard_map/ppermute | solution.py:52
  76.1 6.6 %collective-permute-start.15 = (bf16[4,384,256]{2,1,0:T(8,128)(2,1)S(1)}, bf16[4,384,256]{2,1,0:T(8,128)(2,1)S(1)}, u32[]{:S(2)}, u32[]{:S(2)}) collective-permute-start(bf16[4,384,256]{2,1,0:T(8,128)(2,1)S(1)} %collective-permute-done.12.refs_2_.refs_10_.refs_1_), channel_id=1, source_target_pairs={{0,1},{1,0},{2,3},{3,2},{4,5},{5,4},{6,7},{7,6},{8,9},{9,8},{10,11... | collective-permute-start | bytes 2359304 | tf_op jit(solution)/shard_map/ppermute | solution.py:52
  76.3 13.2 %collective-permute-start.20 = (bf16[768,256]{1,0:T(8,128)(2,1)S(1)}, bf16[768,256]{1,0:T(8,128)(2,1)S(1)}, u32[]{:S(2)}, u32[]{:S(2)}) collective-permute-start(bf16[768,256]{1,0:T(8,128)(2,1)S(1)} %slice.15), channel_id=1, source_target_pairs={{0,2},{1,3},{2,0},{3,1},{4,6},{5,7},{6,4},{7,5},{8,10},{9,11},{10,... | collective-permute-start | bytes 1179656 | tf_op jit(solution)/shard_map/ppermute | solution.py:52
  82.8 3.2 %copy-start.4 = (bf16[6,384,256]{2,1,0:T(8,128)(2,1)}, bf16[6,384,256]{2,1,0:T(8,128)(2,1)S(1)}, u32[]{:S(2)}) copy-start(bf16[6,384,256]{2,1,0:T(8,128)(2,1)S(1)} %collective-permute-done.14.refs_4_.refs_1_) | copy-start | bytes 3538948
  82.8 3.2 %copy-start.2 = (bf16[8,384,256]{2,1,0:T(8,128)(2,1)}, bf16[8,384,256]{2,1,0:T(8,128)(2,1)S(1)}, u32[]{:S(2)}) copy-start(bf16[8,384,256]{2,1,0:T(8,128)(2,1)S(1)} %collective-permute-done.13.refs_3_.refs_0_) | copy-start | bytes 4718596
  89.6 2.9 %collective-permute-start.21 = (bf16[2304,256]{1,0:T(8,128)(2,1)S(1)}, bf16[2304,256]{1,0:T(8,128)(2,1)S(1)}, u32[]{:S(2)}, u32[]{:S(2)}) collective-permute-start(bf16[2304,256]{1,0:T(8,128)(2,1)S(1)} %constant_dynamic-update-slice_fusion.refs_0_), channel_id=1, source_target_pairs={{0,1},{1,0},{2,3},{3,2},{4,5},{5,4},{6,7},{7,6},{8,9},{9,8},{10,11... | collective-permute-start | bytes 3538952 | tf_op jit(solution)/shard_map/ppermute | solution.py:52
  89.7 9.9 %collective-permute-start.17 = (bf16[384,384]{1,0:T(8,128)(2,1)S(1)}, bf16[384,384]{1,0:T(8,128)(2,1)S(1)}, u32[]{:S(2)}, u32[]{:S(2)}) collective-permute-start(bf16[384,384]{1,0:T(8,128)(2,1)S(1)} %last_half.1.refs_0_), channel_id=1, source_target_pairs={{0,12},{1,13},{2,14},{3,15},{4,0},{5,1},{6,2},{7,3},{8,4},{9,5},{1... | collective-permute-start | bytes 884744 | tf_op jit(solution)/shard_map/ppermute | solution.py:52
  89.9 11.1 %collective-permute-start.16 = (bf16[384,384]{1,0:T(8,128)(2,1)S(1)}, bf16[384,384]{1,0:T(8,128)(2,1)S(1)}, u32[]{:S(2)}, u32[]{:S(2)}) collective-permute-start(bf16[384,384]{1,0:T(8,128)(2,1)S(1)} %last_half.1.refs_0_), channel_id=1, source_target_pairs={{0,4},{1,5},{2,6},{3,7},{4,8},{5,9},{6,10},{7,11},{8,12},{9,13},{1... | collective-permute-start | bytes 884744 | tf_op jit(solution)/shard_map/ppermute | solution.py:52
  94.7 9.1 %collective-permute-start.22 = (bf16[96,1024]{1,0:T(8,128)(2,1)S(1)}, bf16[96,1024]{1,0:T(8,128)(2,1)S(1)}, u32[]{:S(2)}, u32[]{:S(2)}) collective-permute-start(bf16[96,1024]{1,0:T(8,128)(2,1)S(1)} %get-tuple-element.104), channel_id=1, source_target_pairs={{0,12},{1,13},{2,14},{3,15},{4,0},{5,1},{6,2},{7,3},{8,4},{9,5},{1... | collective-permute-start | bytes 589832 | tf_op jit(solution)/shard_map/ppermute | solution.py:52
  95.4 14.0 %collective-permute-start.23 = (bf16[96,1024]{1,0:T(8,128)(2,1)S(1)}, bf16[96,1024]{1,0:T(8,128)(2,1)S(1)}, u32[]{:S(2)}, u32[]{:S(2)}) collective-permute-start(bf16[96,1024]{1,0:T(8,128)(2,1)S(1)} %get-tuple-element.105), channel_id=1, source_target_pairs={{0,4},{1,5},{2,6},{3,7},{4,8},{5,9},{6,10},{7,11},{8,12},{9,13},{1... | collective-permute-start | bytes 589832 | tf_op jit(solution)/shard_map/ppermute | solution.py:52
  96.8 12.7 %collective-permute-start.24 = (bf16[96,1024]{1,0:T(8,128)(2,1)S(1)}, bf16[96,1024]{1,0:T(8,128)(2,1)S(1)}, u32[]{:S(2)}, u32[]{:S(2)}) collective-permute-start(bf16[96,1024]{1,0:T(8,128)(2,1)S(1)} %get-tuple-element.106), channel_id=1, source_target_pairs={{0,8},{1,9},{2,10},{3,11},{4,12},{5,13},{6,14},{7,15},{8,0},{9,1},... | collective-permute-start | bytes 589832 | tf_op jit(solution)/shard_map/ppermute | solution.py:52
  99.6 11.3 %collective-permute-start.19 = (bf16[192,384]{1,0:T(8,128)(2,1)S(1)}, bf16[192,384]{1,0:T(8,128)(2,1)S(1)}, u32[]{:S(2)}, u32[]{:S(2)}) collective-permute-start(bf16[192,384]{1,0:T(8,128)(2,1)S(1)} %slice.17), channel_id=1, source_target_pairs={{0,12},{1,13},{2,14},{3,15},{4,0},{5,1},{6,2},{7,3},{8,4},{9,5},{1... | collective-permute-start | bytes 442376 | tf_op jit(solution)/shard_map/ppermute | solution.py:52
  101.0 10.8 %collective-permute-start.18 = (bf16[192,384]{1,0:T(8,128)(2,1)S(1)}, bf16[192,384]{1,0:T(8,128)(2,1)S(1)}, u32[]{:S(2)}, u32[]{:S(2)}) collective-permute-start(bf16[192,384]{1,0:T(8,128)(2,1)S(1)} %slice.16), channel_id=1, source_target_pairs={{0,4},{1,5},{2,6},{3,7},{4,8},{5,9},{6,10},{7,11},{8,12},{9,13},{1... | collective-permute-start | bytes 442376 | tf_op jit(solution)/shard_map/ppermute | solution.py:52
  114.7 0.9 copy-start.6
  115.6 5.7 %copy-start.11 = (s32[32,2]{0,1:T(2,128)S(1)}, s32[32,2]{0,1:T(2,128)}, u32[]{:S(2)}) copy-start(s32[32,2]{0,1:T(2,128)} %param.20) | copy-start | bytes 772
  115.6 5.7 %copy-start.12 = (f32[32,2]{0,1:T(2,128)S(1)}, f32[32,2]{0,1:T(2,128)}, u32[]{:S(2)}) copy-start(f32[32,2]{0,1:T(2,128)} %param.21) | copy-start | bytes 772
  115.6 19.4 %all-to-all-start.1 = ((bf16[32,24,512]{2,1,0:T(8,128)(2,1)}), bf16[32,24,512]{2,1,0:T(8,128)(2,1)}, u32[]{:S(2)}, u32[]{:S(2)}) async-start(bf16[32,24,512]{2,1,0:T(8,128)(2,1)} %copy-done.6), calls=%async_computation.1 | async-start | bytes 1572864 | tf_op jit(solution)/shard_map/all_to_all | solution.py:579
  122.1 0.7 copy-start.7
  122.7 1.1 copy-start.1
  123.9 1.4 %copy-start.3 = (bf16[8,384,256]{2,1,0:T(8,128)(2,1)S(1)}, bf16[8,384,256]{2,1,0:T(8,128)(2,1)}, u32[]{:S(2)}) copy-start(bf16[8,384,256]{2,1,0:T(8,128)(2,1)} %copy-done.2) | copy-start | bytes 4718596
  125.3 1.3 copy-start.5
  135.0 0.9 copy-start.8

commit v3 on v2

--- a/solution.py
+++ b/solution.py
@@ -147,7 +147,7 @@
     return lax.broadcasted_iota(jnp.int32, shape, axis)
 
 
-def dispatch_kernel(ids_ref, tokens_ref, out_ref):
+def dispatch_kernel(where_ref, near_ref, ids_ref, tokens_ref, out_ref):
     expert = iota((128, 32), 0)
     named = jnp.where((ids_ref[0:1, :] == expert) | (ids_ref[1:2, :] == expert), 1.0, 0.0)
     before = jnp.where(iota((32, 32), 0) < iota((32, 32), 1), 1.0, 0.0).astype(BF16)
@@ -166,16 +166,16 @@
         out_ref[e] = packed[e * 24 : (e + 1) * 24].astype(BF16)
 
 
-def dispatch(ids, tokens):
+def dispatch(where, near, ids, tokens):
     return pl.pallas_call(
         dispatch_kernel,
-        in_specs=[VMEM] * 2,
+        in_specs=[SMEM] * 2 + [VMEM] * 2,
         out_specs=VMEM,
         out_shape=jax.ShapeDtypeStruct((8, 24, 2048), BF16),
         cost_estimate=cost(2 * 192 * 64 * 2048, 2 << 20),
         compiler_params=params(),
         name="dispatch",
-    )(ids, tokens)
+    )(where, near, ids, tokens)
 
 
 def unpack_kernel(where_ref, packed_ref, head_ref, tail_ref):
@@ -505,7 +505,7 @@
         out_shape=jax.ShapeDtypeStruct((1, 96, 4096), BF16),
         scratch_shapes=[pltpu.SemaphoreType.DMA((4,))],
         cost_estimate=cost(0, 2 << 20),
-        compiler_params=params(),
+        compiler_params=params(56),
         name="place_down",
     )(where, *parts)
 
@@ -526,11 +526,11 @@
     y, xh, core = lax.axis_index("y"), lax.axis_index("xh"), lax.axis_index("core")
     where = jnp.stack([y, xh, core]).astype(jnp.int32)
 
-    dispatched = dispatch(route_ids.T, tokens)
+    near = jnp.stack([(y + 1) % 4, (y + 3) % 4, y]).astype(jnp.int32)
+    dispatched = dispatch(where, near, route_ids.T, tokens)
     packed = lax.all_to_all(dispatched, ("xl", "z"), split_axis=0, concat_axis=0, tiled=True)
 
     gate_up = (master_gate_up, grad_gate_up, first_gate_up, second_gate_up)
-    near = jnp.stack([(y + 1) % 4, (y + 3) % 4, y]).astype(jnp.int32)
     near = after(near, dispatched)
     partial, to_next, to_last, stays = adam(near, gate_up, None, 384)
     from_last, from_next, stays_across = move_y(to_next, 1), move_y(to_last, -1), move_xh(stays)
@@ -573,10 +573,10 @@
     downs = [rest, groups[2], rest_crossed, crossed[2]]
     downs, *slices = spread_down(where, downs)
     slices = [slices[0]] + [move_y(part, shift) for part, shift in zip(slices[1:], SHIFTS[1:])]
-    rollout_down = place_down(where, slices)
-    hiddens, rollout_down = staged((hiddens, rollout_down))
+    hiddens, slices = staged((hiddens, slices))
     result = second_matmul(where, hiddens, downs)
     back = lax.all_to_all(result, ("xl", "z", "y"), split_axis=0, concat_axis=0, tiled=True)
+    rollout_down = place_down(where, after(slices, result))
     rollout_gate_up = place_gate_up(where, groups + crossed)
     moe_out = combine(mixing, back)
     return (new_master_gate_up, new_master_down, rollout_gate_up, rollout_down, moe_out)

time: 139 us -> 158 us (1.14)
  Pallas kernels: 38 us -> 62.9 us
  waiting for transfers between devices: 46.7 us -> 41.9 us
    pallas_call x1, Pallas kernels: 1.45 us -> 25.8 us  [place_down(): pl.pallas_call(place_kernel, in_specs=[SMEM] + [ANY] * 4, out_specs=ANY,...]
    all_to_all x1, waiting for transfers between devices: 6.31 us -> 0.01 us  [body(): lax.all_to_all(result, ('xl', 'z', 'y'), split_axis=0, concat_axis=0, til...]
    unnamed x33 -> x45, local copies, waits for them, and re-layouts: 7.98 us -> 7.85 us
  transfers between devices with their start and end apart: 27 -> 27, of which waited for: 14 -> 12; matrix products, arithmetic and copies ran while one was open for 1% -> 0% of each run, Pallas kernels for 23% -> 35%
where the time goes in v3:
time: 158 us; the launch traced here: 157 us
  Pallas kernels  62.9 us (40%)
  starting transfers between devices  42.9 us (27%)
  waiting for transfers between devices  41.9 us (27%)
  local copies, waits for them, and re-layouts  7.96 us (5%)
    ppermute x25, waiting for transfers between devices, move(): return lax.ppermute(array, AXES, pairs)  41.9 us
    ppermute x25, starting transfers between devices, move(): return lax.ppermute(array, AXES, pairs)  31.2 us
    pallas_call x1, Pallas kernels, place_down(): pl.pallas_call(place_kernel, in_specs=[SMEM] + [ANY] * 4, out_specs=ANY,...  25.8 us
    pallas_call x3, Pallas kernels, adam(): pl.pallas_call(functools.partial(adam_kernel, count, parts, rows), in_spe...  16.1 us
    unnamed x45, local copies, waits for them, and re-layouts  7.85 us
    all_to_all x1, starting transfers between devices, body(): lax.all_to_all(dispatched, ('xl', 'z'), split_axis=0, concat_axis=0, tile...  6.32 us
    all_to_all x1, starting transfers between devices, body(): lax.all_to_all(result, ('xl', 'z', 'y'), split_axis=0, concat_axis=0, til...  5.33 us
    pallas_call x1, Pallas kernels, first_half(): pl.pallas_call(first_half_kernel, in_specs=[SMEM] + [ANY] * 11, out_specs...  4.67 us
  transfers between devices with their start and end apart: 27, of which 12 were waited for; matrix products, arithmetic and copies ran while one was open for 0% of the time, Pallas kernels for 35%

profile of v3, /device:TPU:0, one launch (start us, length us, event | category | flops | bytes accessed | tf_op | source)
XLA Modules:
  0.0 157.2 jit_solution(5046003972746482446)
XLA Ops:
  0.7 0.9 copy-done.9
  2.4 2.2 %dispatch.1 = bf16[8,24,2048]{2,1,0:T(8,128)(2,1)} custom-call(s32[3]{0:T(128)S(1)} %get-tuple-element.130.where_ref, s32[3]{0:T(128)S(1)} %get-tuple-element.67.near_ref.blocks_ref, s32[2,32]{1,0:T(2,128)S(1)} %bitcast.15, bf16[32,4096]{1,0:T(8,128)(2,1)S(1)} %copy-done.9), custom_call_target="tpu_custom_call" | custom-call | flops 50331648 | bytes 2097152 | tf_op jit(solution)/shard_map/dispatch/pallas_call | solution.py:170
  4.6 6.3 %all-to-all-start = ((bf16[8,24,2048]{2,1,0:T(8,128)(2,1)}), bf16[8,24,2048]{2,1,0:T(8,128)(2,1)S(1)}, u32[]{:S(2)}, u32[]{:S(2)}) async-start(bf16[8,24,2048]{2,1,0:T(8,128)(2,1)} %dispatch.1), calls=%async_computation | async-start | bytes 1572864 | tf_op jit(solution)/shard_map/all_to_all | solution.py:531
  10.9 7.2 %adam.3 = (f32[1,2,1536,256]{3,2,1,0:T(8,128)}, bf16[2,384,256]{2,1,0:T(8,128)(2,1)}, bf16[2,384,256]{2,1,0:T(8,128)(2,1)}, bf16[2,384,256]{2,1,0:T(8,128)(2,1)}) custom-call(s32[3]{0:T(128)} %copy-done.12, f32[1,2,1536,256]{3,2,1,0:T(8,128)} %refs_0_.3, f32[1,2,1536,256]{3,2,1,0:T(8,128)} %refs_1_.3, f32[1,2,1536,256]{3,2,1,0:T(8,128)} %refs_2_.3, ...), custom_call_target="tpu_custom_call" | custom-call | bytes 12976128 | tf_op jit(solution)/shard_map/adam/pallas_call | solution.py:120
  18.1 1.6 %collective-permute-start = (bf16[2,384,256]{2,1,0:T(8,128)(2,1)}, bf16[2,384,256]{2,1,0:T(8,128)(2,1)S(1)}, u32[]{:S(2)}, u32[]{:S(2)}) collective-permute-start(bf16[2,384,256]{2,1,0:T(8,128)(2,1)} %get-tuple-element.73), channel_id=1, source_target_pairs={{0,4},{1,5},{2,6},{3,7},{4,8},{5,9},{6,10},{7,11},{8,12},{9,13},{1... | collective-permute-start | bytes 1179656 | tf_op jit(solution)/shard_map/ppermute | solution.py:52
  19.8 1.7 %collective-permute-start.1 = (bf16[2,384,256]{2,1,0:T(8,128)(2,1)}, bf16[2,384,256]{2,1,0:T(8,128)(2,1)S(1)}, u32[]{:S(2)}, u32[]{:S(2)}) collective-permute-start(bf16[2,384,256]{2,1,0:T(8,128)(2,1)} %get-tuple-element.74), channel_id=1, source_target_pairs={{0,12},{1,13},{2,14},{3,15},{4,0},{5,1},{6,2},{7,3},{8,4},{9,5},{1... | collective-permute-start | bytes 1179656 | tf_op jit(solution)/shard_map/ppermute | solution.py:52
  21.4 2.7 %collective-permute-start.2 = (bf16[2,384,256]{2,1,0:T(8,128)(2,1)}, bf16[2,384,256]{2,1,0:T(8,128)(2,1)S(1)}, u32[]{:S(2)}, u32[]{:S(2)}) collective-permute-start(bf16[2,384,256]{2,1,0:T(8,128)(2,1)} %get-tuple-element.75), channel_id=1, source_target_pairs={{0,2},{1,3},{2,0},{3,1},{4,6},{5,7},{6,4},{7,5},{8,10},{9,11},{10,... | collective-permute-start | bytes 1179656 | tf_op jit(solution)/shard_map/ppermute | solution.py:52
  24.2 3.8 %adam.4 = (f32[1,2,1536,256]{3,2,1,0:T(8,128)}, bf16[2,384,256]{2,1,0:T(8,128)(2,1)}) custom-call(s32[1]{0:T(128)} %bitcast.blocks_ref, f32[1,2,1536,256]{3,2,1,0:T(8,128)} %refs_0_.3, f32[1,2,1536,256]{3,2,1,0:T(8,128)} %refs_1_.3, f32[1,2,1536,256]{3,2,1,0:T(8,128)} %refs_2_.3, f32[1,2,1536,256]{3,2,1,0:T(8,128)} %refs_3_.3, ...), custom_call_target="tpu_custom_call", output_to_operand_aliasing={{0}: (5, {})} | custom-call | bytes 4325376 | tf_op jit(solution)/shard_map/adam/pallas_call | solution.py:120
  28.0 5.2 %adam.5 = (f32[1,1,1536,256]{3,2,1,0:T(8,128)}, bf16[1,1536,256]{2,1,0:T(8,128)(2,1)}) custom-call(s32[1]{0:T(128)} %constant.38.clone.1.blocks_ref, f32[1,1,1536,256]{3,2,1,0:T(8,128)} %bitcast.22, f32[1,1,1536,256]{3,2,1,0:T(8,128)} %bitcast.23, f32[1,1,1536,256]{3,2,1,0:T(8,128)} %bitcast.24, f32[1,1,1536,256]{3,2,1,0:T(8,128)} %bitcast.25), custom_call_target="tpu_custom_call" | custom-call | bytes 8650752 | tf_op jit(solution)/shard_map/adam/pallas_call | solution.py:120
  33.3 1.9 %collective-permute-start.3 = (bf16[2,384,256]{2,1,0:T(8,128)(2,1)S(1)}, bf16[2,384,256]{2,1,0:T(8,128)(2,1)S(1)}, u32[]{:S(2)}, u32[]{:S(2)}) collective-permute-start(bf16[2,384,256]{2,1,0:T(8,128)(2,1)S(1)} %copy-done.21), channel_id=1, source_target_pairs={{0,8},{1,9},{2,10},{3,11},{4,12},{5,13},{6,14},{7,15},{8,0},{9,1},... | collective-permute-start | bytes 1179656 | tf_op jit(solution)/shard_map/ppermute | solution.py:52
  35.3 2.6 %collective-permute-start.6 = (bf16[2,384,256]{2,1,0:T(8,128)(2,1)S(1)}, bf16[2,384,256]{2,1,0:T(8,128)(2,1)S(1)}, u32[]{:S(2)}, u32[]{:S(2)}) collective-permute-start(bf16[2,384,256]{2,1,0:T(8,128)(2,1)S(1)} %collective-permute-done), channel_id=1, source_target_pairs={{0,2},{1,3},{2,0},{3,1},{4,6},{5,7},{6,4},{7,5},{8,10},{9,11},{10,... | collective-permute-start | bytes 1179656 | tf_op jit(solution)/shard_map/ppermute | solution.py:52
  37.9 0.9 collective-permute-start.7
  38.8 0.9 unpack.1
  39.7 0.7 collective-permute-start.4
  40.5 2.6 %collective-permute-start.5 = (bf16[48,4096]{1,0:T(8,128)(2,1)S(1)}, bf16[48,4096]{1,0:T(8,128)(2,1)S(1)}, u32[]{:S(2)}, u32[]{:S(2)}) collective-permute-start(bf16[48,4096]{1,0:T(8,128)(2,1)S(1)} %get-tuple-element.98.refs_1_), channel_id=1, source_target_pairs={{0,12},{1,13},{2,14},{3,15},{4,0},{5,1},{6,2},{7,3},{8,4},{9,5},{1... | collective-permute-start | bytes 1179656 | tf_op jit(solution)/shard_map/ppermute | solution.py:52
  43.2 3.7 %collective-permute-done.3 = bf16[2,384,256]{2,1,0:T(8,128)(2,1)S(1)} collective-permute-done((bf16[2,384,256]{2,1,0:T(8,128)(2,1)S(1)}, bf16[2,384,256]{2,1,0:T(8,128)(2,1)S(1)}, u32[]{:S(2)}, u32[]{:S(2)}) %collective-permute-start.3) | collective-permute-done | bytes 393248 | tf_op jit(solution)/shard_map/ppermute | solution.py:52
  46.9 1.9 %collective-permute-done.6 = bf16[2,384,256]{2,1,0:T(8,128)(2,1)S(1)} collective-permute-done((bf16[2,384,256]{2,1,0:T(8,128)(2,1)S(1)}, bf16[2,384,256]{2,1,0:T(8,128)(2,1)S(1)}, u32[]{:S(2)}, u32[]{:S(2)}) %collective-permute-start.6) | collective-permute-done | bytes 393248 | tf_op jit(solution)/shard_map/ppermute | solution.py:52
  48.8 5.8 %collective-permute-done.7 = bf16[2,384,256]{2,1,0:T(8,128)(2,1)S(1)} collective-permute-done((bf16[2,384,256]{2,1,0:T(8,128)(2,1)S(1)}, bf16[2,384,256]{2,1,0:T(8,128)(2,1)S(1)}, u32[]{:S(2)}, u32[]{:S(2)}) %collective-permute-start.7) | collective-permute-done | bytes 393248 | tf_op jit(solution)/shard_map/ppermute | solution.py:52
  54.8 2.1 %collective-permute-start.12 = (bf16[4,384,256]{2,1,0:T(8,128)(2,1)S(1)}, bf16[4,384,256]{2,1,0:T(8,128)(2,1)S(1)}, u32[]{:S(2)}, u32[]{:S(2)}) collective-permute-start(bf16[4,384,256]{2,1,0:T(8,128)(2,1)S(1)} %pad_maximum_fusion.2), channel_id=1, source_target_pairs={{0,2},{1,3},{2,0},{3,1},{4,6},{5,7},{6,4},{7,5},{8,10},{9,11},{10,... | collective-permute-start | bytes 2359304 | tf_op jit(solution)/shard_map/ppermute | solution.py:52
  56.8 1.1 collective-permute-start.9
  57.9 1.0 collective-permute-start.8
  59.6 2.6 %collective-permute-start.11 = (bf16[48,4096]{1,0:T(8,128)(2,1)S(1)}, bf16[48,4096]{1,0:T(8,128)(2,1)S(1)}, u32[]{:S(2)}, u32[]{:S(2)}) collective-permute-start(bf16[48,4096]{1,0:T(8,128)(2,1)S(1)} %collective-permute-done.5.refs_5_), channel_id=1, source_target_pairs={{0,12},{1,13},{2,14},{3,15},{4,0},{5,1},{6,2},{7,3},{8,4},{9,5},{1... | collective-permute-start | bytes 1179656 | tf_op jit(solution)/shard_map/ppermute | solution.py:52
  62.2 6.6 %collective-permute-done.9.refs_4_ = bf16[48,4096]{1,0:T(8,128)(2,1)S(1)} collective-permute-done((bf16[48,4096]{1,0:T(8,128)(2,1)S(1)}, bf16[48,4096]{1,0:T(8,128)(2,1)S(1)}, u32[]{:S(2)}, u32[]{:S(2)}) %collective-permute-start.9) | collective-permute-done | bytes 393248 | tf_op jit(solution)/shard_map/ppermute | solution.py:52
  68.8 2.4 %collective-permute-done.8.refs_3_ = bf16[48,4096]{1,0:T(8,128)(2,1)S(1)} collective-permute-done((bf16[48,4096]{1,0:T(8,128)(2,1)S(1)}, bf16[48,4096]{1,0:T(8,128)(2,1)S(1)}, u32[]{:S(2)}, u32[]{:S(2)}) %collective-permute-start.8) | collective-permute-done | bytes 393248 | tf_op jit(solution)/shard_map/ppermute | solution.py:52
  71.2 4.4 %collective-permute-done.10.refs_6_ = bf16[48,4096]{1,0:T(8,128)(2,1)S(1)} collective-permute-done((bf16[48,4096]{1,0:T(8,128)(2,1)S(1)}, bf16[48,4096]{1,0:T(8,128)(2,1)S(1)}, u32[]{:S(2)}, u32[]{:S(2)}) %collective-permute-start.10) | collective-permute-done | bytes 393248 | tf_op jit(solution)/shard_map/ppermute | solution.py:52
  76.3 1.8 %collective-permute-start.20 = (bf16[768,256]{1,0:T(8,128)(2,1)S(1)}, bf16[768,256]{1,0:T(8,128)(2,1)S(1)}, u32[]{:S(2)}, u32[]{:S(2)}) collective-permute-start(bf16[768,256]{1,0:T(8,128)(2,1)S(1)} %slice.15), channel_id=1, source_target_pairs={{0,2},{1,3},{2,0},{3,1},{4,6},{5,7},{6,4},{7,5},{8,10},{9,11},{10,... | collective-permute-start | bytes 1179656 | tf_op jit(solution)/shard_map/ppermute | solution.py:52
  78.1 4.7 %first_half.1 = (bf16[384,4096]{1,0:T(8,128)(2,1)S(1)}, f32[2,384,384]{2,1,0:T(8,128)S(1)}) custom-call(s32[3]{0:T(128)S(1)} %get-tuple-element.130.where_ref, bf16[48,4096]{1,0:T(8,128)(2,1)S(1)} %get-tuple-element.97.refs_0_, bf16[48,4096]{1,0:T(8,128)(2,1)S(1)} %get-tuple-element.98.refs_1_, bf16[48,4096]{1,0:T(8,128)(2,1)S(1)} %collective-permute-done.4.refs_2_, ...), custom_call_target="tpu_custom_call" | custom-call | flops 1207959552 | bytes 8388608 | tf_op jit(solution)/shard_map/first_half/pallas_call | solution.py:322
  82.9 3.1 %last_half.1.refs_0_ = bf16[384,384]{1,0:T(8,128)(2,1)S(1)} custom-call(s32[3]{0:T(128)S(1)} %get-tuple-element.130.where_ref, bf16[384,4096]{1,0:T(8,128)(2,1)S(1)} %get-tuple-element.105.x_ref, f32[2,384,384]{2,1,0:T(8,128)S(1)} %get-tuple-element.106.acc_ref, bf16[8,384,256]{2,1,0:T(8,128)(2,1)S(1)} %collective-permute-done.13.refs_3_.refs_0_, ...), custom_call_target="tpu_custom_call" | custom-call | flops 1207959552 | bytes 8388608 | tf_op jit(solution)/shard_map/last_half/pallas_call | solution.py:339
  86.0 3.5 %collective-permute-done.20 = bf16[768,256]{1,0:T(8,128)(2,1)S(1)} collective-permute-done((bf16[768,256]{1,0:T(8,128)(2,1)S(1)}, bf16[768,256]{1,0:T(8,128)(2,1)S(1)}, u32[]{:S(2)}, u32[]{:S(2)}) %collective-permute-start.20) | collective-permute-done | bytes 393248 | tf_op jit(solution)/shard_map/ppermute | solution.py:52
  90.0 1.8 %collective-permute-start.16 = (bf16[384,384]{1,0:T(8,128)(2,1)S(1)}, bf16[384,384]{1,0:T(8,128)(2,1)S(1)}, u32[]{:S(2)}, u32[]{:S(2)}) collective-permute-start(bf16[384,384]{1,0:T(8,128)(2,1)S(1)} %last_half.1.refs_0_), channel_id=1, source_target_pairs={{0,4},{1,5},{2,6},{3,7},{4,8},{5,9},{6,10},{7,11},{8,12},{9,13},{1... | collective-permute-start | bytes 884744 | tf_op jit(solution)/shard_map/ppermute | solution.py:52
  91.8 0.7 collective-permute-done.21.refs_2_
  92.6 2.2 %spread_down.1 = (bf16[1536,1024]{1,0:T(8,128)(2,1)S(1)}, bf16[96,1024]{1,0:T(8,128)(2,1)S(1)}, bf16[96,1024]{1,0:T(8,128)(2,1)S(1)}, bf16[96,1024]{1,0:T(8,128)(2,1)S(1)}, bf16[96,1024]{1,0:T(8,128)(2,1)S(1)}) custom-call(s32[3]{0:T(128)S(1)} %get-tuple-element.130.where_ref, bf16[2304,256]{1,0:T(8,128)(2,1)S(1)} %constant_dynamic-update-slice_fusion.refs_0_, ...), custom_call_target="tpu_custom_call" | custom-call | bytes 8388608 | tf_op jit(solution)/shard_map/spread_down/pallas_call | solution.py:417
  94.7 0.7 collective-permute-start.22
  95.5 1.4 collective-permute-start.23
  97.0 2.6 %collective-permute-done.17.refs_2_ = bf16[384,384]{1,0:T(8,128)(2,1)S(1)} collective-permute-done((bf16[384,384]{1,0:T(8,128)(2,1)S(1)}, bf16[384,384]{1,0:T(8,128)(2,1)S(1)}, u32[]{:S(2)}, u32[]{:S(2)}) %collective-permute-start.17) | collective-permute-done | bytes 294944 | tf_op jit(solution)/shard_map/ppermute | solution.py:52
  99.6 1.5 collective-permute-start.19
  101.8 9.0 %collective-permute-done.19.refs_4_ = bf16[192,384]{1,0:T(8,128)(2,1)S(1)} collective-permute-done((bf16[192,384]{1,0:T(8,128)(2,1)S(1)}, bf16[192,384]{1,0:T(8,128)(2,1)S(1)}, u32[]{:S(2)}, u32[]{:S(2)}) %collective-permute-start.19) | collective-permute-done | bytes 147488 | tf_op jit(solution)/shard_map/ppermute | solution.py:52
  110.8 1.2 collective-permute-done.18.refs_3_
  112.8 2.8 %second_matmul.1 = bf16[32,24,512]{2,1,0:T(8,128)(2,1)S(1)} custom-call(s32[3]{0:T(128)S(1)} %get-tuple-element.130.where_ref, bf16[384,384]{1,0:T(8,128)(2,1)S(1)} %last_half.1.refs_0_, bf16[384,384]{1,0:T(8,128)(2,1)S(1)} %collective-permute-done.16.refs_1_, bf16[384,384]{1,0:T(8,128)(2,1)S(1)} %collective-permute-done.17.refs_2_, ...), custom_call_target="tpu_custom_call" | custom-call | flops 1207959552 | bytes 6291456 | tf_op jit(solution)/shard_map/second_matmul/pallas_call | solution.py:471
  115.6 0.9 copy-done.6
  116.4 5.3 %all-to-all-start.1 = ((bf16[32,24,512]{2,1,0:T(8,128)(2,1)}), bf16[32,24,512]{2,1,0:T(8,128)(2,1)}, u32[]{:S(2)}, u32[]{:S(2)}) async-start(bf16[32,24,512]{2,1,0:T(8,128)(2,1)} %copy-done.6), calls=%async_computation.1 | async-start | bytes 1572864 | tf_op jit(solution)/shard_map/all_to_all | solution.py:578
  121.8 0.8 mix.1.mixing_ref
  123.3 1.1 copy-done.1
  124.4 1.4 copy-done.3
  125.8 1.3 copy-done.5
  127.1 2.1 %place_gate_up.1 = bf16[1,2,96,4096]{3,2,1,0:T(8,128)(2,1)} custom-call(s32[3]{0:T(128)S(1)} %get-tuple-element.130.where_ref, bf16[8,384,256]{2,1,0:T(8,128)(2,1)S(1)} %pad_maximum_fusion.refs_0_.refs_8_, bf16[6,384,256]{2,1,0:T(8,128)(2,1)S(1)} %pad_maximum_fusion.1.refs_1_.refs_9_, bf16[4,384,256]{2,1,0:T(8,128)(2,1)S(1)} %copy-done.1, ...), custom_call_target="tpu_custom_call" | custom-call | bytes 4194304 | tf_op jit(solution)/shard_map/place_gate_up/pallas_call | solution.py:371
  129.2 25.8 %place_down.1 = bf16[1,96,4096]{2,1,0:T(8,128)(2,1)} custom-call(s32[3]{0:T(128)} %copy-done.11, bf16[96,1024]{1,0:T(8,128)(2,1)} %copy-done.10, bf16[96,1024]{1,0:T(8,128)(2,1)} %copy-done.18, bf16[96,1024]{1,0:T(8,128)(2,1)} %copy-done.19, bf16[96,1024]{1,0:T(8,128)(2,1)} %copy-done.20), custom_call_target="tpu_custom_call" | custom-call | bytes 2097152 | tf_op jit(solution)/shard_map/place_down/pallas_call | solution.py:501
  155.0 2.2 %combine.1 = bf16[32,4096]{1,0:T(8,128)(2,1)} custom-call(bf16[192,192]{1,0:T(8,128)(2,1)S(1)} %copy-done.8, bf16[32,24,512]{2,1,0:T(8,128)(2,1)} %all-to-all-done.1.back_ref), custom_call_target="tpu_custom_call" | custom-call | flops 150994944 | bytes 2097152 | tf_op jit(solution)/shard_map/combine/pallas_call | solution.py:252
  (73 shorter events, 5.6 us)
Async XLA Ops:
  0.7 10.2 %copy-start.12 = (s32[3]{0:T(128)}, s32[3]{0:T(128)S(1)}, u32[]{:S(2)}) copy-start(s32[3]{0:T(128)S(1)} %get-tuple-element.67.near_ref.blocks_ref) | copy-start | bytes 40
  0.7 121.9 %copy-start.11 = (s32[3]{0:T(128)}, s32[3]{0:T(128)S(1)}, u32[]{:S(2)}) copy-start(s32[3]{0:T(128)S(1)} %get-tuple-element.130.where_ref) | copy-start | bytes 40
  0.7 1.0 copy-start.9
  1.7 0.7 copy-start.13
  4.6 28.7 %all-to-all-start = ((bf16[8,24,2048]{2,1,0:T(8,128)(2,1)}), bf16[8,24,2048]{2,1,0:T(8,128)(2,1)S(1)}, u32[]{:S(2)}, u32[]{:S(2)}) async-start(bf16[8,24,2048]{2,1,0:T(8,128)(2,1)} %dispatch.1), calls=%async_computation | async-start | bytes 1572864 | tf_op jit(solution)/shard_map/all_to_all | solution.py:531
  18.1 15.0 %collective-permute-start = (bf16[2,384,256]{2,1,0:T(8,128)(2,1)}, bf16[2,384,256]{2,1,0:T(8,128)(2,1)S(1)}, u32[]{:S(2)}, u32[]{:S(2)}) collective-permute-start(bf16[2,384,256]{2,1,0:T(8,128)(2,1)} %get-tuple-element.73), channel_id=1, source_target_pairs={{0,4},{1,5},{2,6},{3,7},{4,8},{5,9},{6,10},{7,11},{8,12},{9,13},{1... | collective-permute-start | bytes 1179656 | tf_op jit(solution)/shard_map/ppermute | solution.py:52
  19.8 13.4 %collective-permute-start.1 = (bf16[2,384,256]{2,1,0:T(8,128)(2,1)}, bf16[2,384,256]{2,1,0:T(8,128)(2,1)S(1)}, u32[]{:S(2)}, u32[]{:S(2)}) collective-permute-start(bf16[2,384,256]{2,1,0:T(8,128)(2,1)} %get-tuple-element.74), channel_id=1, source_target_pairs={{0,12},{1,13},{2,14},{3,15},{4,0},{5,1},{6,2},{7,3},{8,4},{9,5},{1... | collective-permute-start | bytes 1179656 | tf_op jit(solution)/shard_map/ppermute | solution.py:52
  21.4 11.9 %collective-permute-start.2 = (bf16[2,384,256]{2,1,0:T(8,128)(2,1)}, bf16[2,384,256]{2,1,0:T(8,128)(2,1)S(1)}, u32[]{:S(2)}, u32[]{:S(2)}) collective-permute-start(bf16[2,384,256]{2,1,0:T(8,128)(2,1)} %get-tuple-element.75), channel_id=1, source_target_pairs={{0,2},{1,3},{2,0},{3,1},{4,6},{5,7},{6,4},{7,5},{8,10},{9,11},{10,... | collective-permute-start | bytes 1179656 | tf_op jit(solution)/shard_map/ppermute | solution.py:52
  28.0 5.4 %copy-start.21 = (bf16[2,384,256]{2,1,0:T(8,128)(2,1)S(1)}, bf16[2,384,256]{2,1,0:T(8,128)(2,1)}, u32[]{:S(2)}) copy-start(bf16[2,384,256]{2,1,0:T(8,128)(2,1)} %get-tuple-element.77) | copy-start | bytes 1179652
  28.0 15.0 %copy-start.17 = (bf16[2,384,256]{2,1,0:T(8,128)(2,1)S(1)}, bf16[2,384,256]{2,1,0:T(8,128)(2,1)}, u32[]{:S(2)}) copy-start(bf16[2,384,256]{2,1,0:T(8,128)(2,1)} %get-tuple-element.75) | copy-start | bytes 1179652
  33.3 13.6 %collective-permute-start.3 = (bf16[2,384,256]{2,1,0:T(8,128)(2,1)S(1)}, bf16[2,384,256]{2,1,0:T(8,128)(2,1)S(1)}, u32[]{:S(2)}, u32[]{:S(2)}) collective-permute-start(bf16[2,384,256]{2,1,0:T(8,128)(2,1)S(1)} %copy-done.21), channel_id=1, source_target_pairs={{0,8},{1,9},{2,10},{3,11},{4,12},{5,13},{6,14},{7,15},{8,0},{9,1},... | collective-permute-start | bytes 1179656 | tf_op jit(solution)/shard_map/ppermute | solution.py:52
  35.3 13.6 %collective-permute-start.6 = (bf16[2,384,256]{2,1,0:T(8,128)(2,1)S(1)}, bf16[2,384,256]{2,1,0:T(8,128)(2,1)S(1)}, u32[]{:S(2)}, u32[]{:S(2)}) collective-permute-start(bf16[2,384,256]{2,1,0:T(8,128)(2,1)S(1)} %collective-permute-done), channel_id=1, source_target_pairs={{0,2},{1,3},{2,0},{3,1},{4,6},{5,7},{6,4},{7,5},{8,10},{9,11},{10,... | collective-permute-start | bytes 1179656 | tf_op jit(solution)/shard_map/ppermute | solution.py:52
  37.9 16.8 %collective-permute-start.7 = (bf16[2,384,256]{2,1,0:T(8,128)(2,1)S(1)}, bf16[2,384,256]{2,1,0:T(8,128)(2,1)S(1)}, u32[]{:S(2)}, u32[]{:S(2)}) collective-permute-start(bf16[2,384,256]{2,1,0:T(8,128)(2,1)S(1)} %collective-permute-done.1), channel_id=1, source_target_pairs={{0,2},{1,3},{2,0},{3,1},{4,6},{5,7},{6,4},{7,5},{8,10},{9,11},{10,... | collective-permute-start | bytes 1179656 | tf_op jit(solution)/shard_map/ppermute | solution.py:52
  39.7 14.9 %collective-permute-start.4 = (bf16[48,4096]{1,0:T(8,128)(2,1)S(1)}, bf16[48,4096]{1,0:T(8,128)(2,1)S(1)}, u32[]{:S(2)}, u32[]{:S(2)}) collective-permute-start(bf16[48,4096]{1,0:T(8,128)(2,1)S(1)} %get-tuple-element.97.refs_0_), channel_id=1, source_target_pairs={{0,4},{1,5},{2,6},{3,7},{4,8},{5,9},{6,10},{7,11},{8,12},{9,13},{1... | collective-permute-start | bytes 1179656 | tf_op jit(solution)/shard_map/ppermute | solution.py:52
  40.5 14.2 %copy-start.16 = (bf16[1,1536,256]{2,1,0:T(8,128)(2,1)S(1)}, bf16[1,1536,256]{2,1,0:T(8,128)(2,1)}, u32[]{:S(2)}) copy-start(bf16[1,1536,256]{2,1,0:T(8,128)(2,1)} %get-tuple-element.76) | copy-start | bytes 2359300
  40.5 14.2 %collective-permute-start.5 = (bf16[48,4096]{1,0:T(8,128)(2,1)S(1)}, bf16[48,4096]{1,0:T(8,128)(2,1)S(1)}, u32[]{:S(2)}, u32[]{:S(2)}) collective-permute-start(bf16[48,4096]{1,0:T(8,128)(2,1)S(1)} %get-tuple-element.98.refs_1_), channel_id=1, source_target_pairs={{0,12},{1,13},{2,14},{3,15},{4,0},{5,1},{6,2},{7,3},{8,4},{9,5},{1... | collective-permute-start | bytes 1179656 | tf_op jit(solution)/shard_map/ppermute | solution.py:52
  54.8 20.8 %collective-permute-start.12 = (bf16[4,384,256]{2,1,0:T(8,128)(2,1)S(1)}, bf16[4,384,256]{2,1,0:T(8,128)(2,1)S(1)}, u32[]{:S(2)}, u32[]{:S(2)}) collective-permute-start(bf16[4,384,256]{2,1,0:T(8,128)(2,1)S(1)} %pad_maximum_fusion.2), channel_id=1, source_target_pairs={{0,2},{1,3},{2,0},{3,1},{4,6},{5,7},{6,4},{7,5},{8,10},{9,11},{10,... | collective-permute-start | bytes 2359304 | tf_op jit(solution)/shard_map/ppermute | solution.py:52
  56.8 12.0 %collective-permute-start.9 = (bf16[48,4096]{1,0:T(8,128)(2,1)S(1)}, bf16[48,4096]{1,0:T(8,128)(2,1)S(1)}, u32[]{:S(2)}, u32[]{:S(2)}) collective-permute-start(bf16[48,4096]{1,0:T(8,128)(2,1)S(1)} %get-tuple-element.97.refs_0_), channel_id=1, source_target_pairs={{0,12},{1,13},{2,14},{3,15},{4,0},{5,1},{6,2},{7,3},{8,4},{9,5},{1... | collective-permute-start | bytes 1179656 | tf_op jit(solution)/shard_map/ppermute | solution.py:52
  57.9 13.3 %collective-permute-start.8 = (bf16[48,4096]{1,0:T(8,128)(2,1)S(1)}, bf16[48,4096]{1,0:T(8,128)(2,1)S(1)}, u32[]{:S(2)}, u32[]{:S(2)}) collective-permute-start(bf16[48,4096]{1,0:T(8,128)(2,1)S(1)} %get-tuple-element.98.refs_1_), channel_id=1, source_target_pairs={{0,4},{1,5},{2,6},{3,7},{4,8},{5,9},{6,10},{7,11},{8,12},{9,13},{1... | collective-permute-start | bytes 1179656 | tf_op jit(solution)/shard_map/ppermute | solution.py:52
  58.9 16.7 %collective-permute-start.10 = (bf16[48,4096]{1,0:T(8,128)(2,1)S(1)}, bf16[48,4096]{1,0:T(8,128)(2,1)S(1)}, u32[]{:S(2)}, u32[]{:S(2)}) collective-permute-start(bf16[48,4096]{1,0:T(8,128)(2,1)S(1)} %collective-permute-done.4.refs_2_), channel_id=1, source_target_pairs={{0,4},{1,5},{2,6},{3,7},{4,8},{5,9},{6,10},{7,11},{8,12},{9,13},{1... | collective-permute-start | bytes 1179656 | tf_op jit(solution)/shard_map/ppermute | solution.py:52
  59.6 16.0 %collective-permute-start.11 = (bf16[48,4096]{1,0:T(8,128)(2,1)S(1)}, bf16[48,4096]{1,0:T(8,128)(2,1)S(1)}, u32[]{:S(2)}, u32[]{:S(2)}) collective-permute-start(bf16[48,4096]{1,0:T(8,128)(2,1)S(1)} %collective-permute-done.5.refs_5_), channel_id=1, source_target_pairs={{0,12},{1,13},{2,14},{3,15},{4,0},{5,1},{6,2},{7,3},{8,4},{9,5},{1... | collective-permute-start | bytes 1179656 | tf_op jit(solution)/shard_map/ppermute | solution.py:52
  75.6 17.0 %copy-start = (bf16[4,384,256]{2,1,0:T(8,128)(2,1)}, bf16[4,384,256]{2,1,0:T(8,128)(2,1)S(1)}, u32[]{:S(2)}) copy-start(bf16[4,384,256]{2,1,0:T(8,128)(2,1)S(1)} %collective-permute-done.12.refs_2_.refs_10_.refs_1_) | copy-start | bytes 2359300
  75.6 7.2 %collective-permute-start.13 = (bf16[8,384,256]{2,1,0:T(8,128)(2,1)S(1)}, bf16[8,384,256]{2,1,0:T(8,128)(2,1)S(1)}, u32[]{:S(2)}, u32[]{:S(2)}) collective-permute-start(bf16[8,384,256]{2,1,0:T(8,128)(2,1)S(1)} %pad_maximum_fusion.refs_0_.refs_8_), channel_id=1, source_target_pairs={{0,1},{1,0},{2,3},{3,2},{4,5},{5,4},{6,7},{7,6},{8,9},{9,8},{10,11... | collective-permute-start | bytes 4718600 | tf_op jit(solution)/shard_map/ppermute | solution.py:52
  75.7 7.1 %collective-permute-start.14 = (bf16[6,384,256]{2,1,0:T(8,128)(2,1)S(1)}, bf16[6,384,256]{2,1,0:T(8,128)(2,1)S(1)}, u32[]{:S(2)}, u32[]{:S(2)}) collective-permute-start(bf16[6,384,256]{2,1,0:T(8,128)(2,1)S(1)} %pad_maximum_fusion.1.refs_1_.refs_9_), channel_id=1, source_target_pairs={{0,1},{1,0},{2,3},{3,2},{4,5},{5,4},{6,7},{7,6},{8,9},{9,8},{10,11... | collective-permute-start | bytes 3538952 | tf_op jit(solution)/shard_map/ppermute | solution.py:52
  76.2 6.6 %collective-permute-start.15 = (bf16[4,384,256]{2,1,0:T(8,128)(2,1)S(1)}, bf16[4,384,256]{2,1,0:T(8,128)(2,1)S(1)}, u32[]{:S(2)}, u32[]{:S(2)}) collective-permute-start(bf16[4,384,256]{2,1,0:T(8,128)(2,1)S(1)} %collective-permute-done.12.refs_2_.refs_10_.refs_1_), channel_id=1, source_target_pairs={{0,1},{1,0},{2,3},{3,2},{4,5},{5,4},{6,7},{7,6},{8,9},{9,8},{10,11... | collective-permute-start | bytes 2359304 | tf_op jit(solution)/shard_map/ppermute | solution.py:52
  76.3 13.2 %collective-permute-start.20 = (bf16[768,256]{1,0:T(8,128)(2,1)S(1)}, bf16[768,256]{1,0:T(8,128)(2,1)S(1)}, u32[]{:S(2)}, u32[]{:S(2)}) collective-permute-start(bf16[768,256]{1,0:T(8,128)(2,1)S(1)} %slice.15), channel_id=1, source_target_pairs={{0,2},{1,3},{2,0},{3,1},{4,6},{5,7},{6,4},{7,5},{8,10},{9,11},{10,... | collective-permute-start | bytes 1179656 | tf_op jit(solution)/shard_map/ppermute | solution.py:52
  82.8 3.2 %copy-start.4 = (bf16[6,384,256]{2,1,0:T(8,128)(2,1)}, bf16[6,384,256]{2,1,0:T(8,128)(2,1)S(1)}, u32[]{:S(2)}) copy-start(bf16[6,384,256]{2,1,0:T(8,128)(2,1)S(1)} %collective-permute-done.14.refs_4_.refs_1_) | copy-start | bytes 3538948
  82.8 3.2 %copy-start.2 = (bf16[8,384,256]{2,1,0:T(8,128)(2,1)}, bf16[8,384,256]{2,1,0:T(8,128)(2,1)S(1)}, u32[]{:S(2)}) copy-start(bf16[8,384,256]{2,1,0:T(8,128)(2,1)S(1)} %collective-permute-done.13.refs_3_.refs_0_) | copy-start | bytes 4718596
  89.6 2.9 %collective-permute-start.21 = (bf16[2304,256]{1,0:T(8,128)(2,1)S(1)}, bf16[2304,256]{1,0:T(8,128)(2,1)S(1)}, u32[]{:S(2)}, u32[]{:S(2)}) collective-permute-start(bf16[2304,256]{1,0:T(8,128)(2,1)S(1)} %constant_dynamic-update-slice_fusion.refs_0_), channel_id=1, source_target_pairs={{0,1},{1,0},{2,3},{3,2},{4,5},{5,4},{6,7},{7,6},{8,9},{9,8},{10,11... | collective-permute-start | bytes 3538952 | tf_op jit(solution)/shard_map/ppermute | solution.py:52
  89.7 9.9 %collective-permute-start.17 = (bf16[384,384]{1,0:T(8,128)(2,1)S(1)}, bf16[384,384]{1,0:T(8,128)(2,1)S(1)}, u32[]{:S(2)}, u32[]{:S(2)}) collective-permute-start(bf16[384,384]{1,0:T(8,128)(2,1)S(1)} %last_half.1.refs_0_), channel_id=1, source_target_pairs={{0,12},{1,13},{2,14},{3,15},{4,0},{5,1},{6,2},{7,3},{8,4},{9,5},{1... | collective-permute-start | bytes 884744 | tf_op jit(solution)/shard_map/ppermute | solution.py:52
  90.0 11.1 %collective-permute-start.16 = (bf16[384,384]{1,0:T(8,128)(2,1)S(1)}, bf16[384,384]{1,0:T(8,128)(2,1)S(1)}, u32[]{:S(2)}, u32[]{:S(2)}) collective-permute-start(bf16[384,384]{1,0:T(8,128)(2,1)S(1)} %last_half.1.refs_0_), channel_id=1, source_target_pairs={{0,4},{1,5},{2,6},{3,7},{4,8},{5,9},{6,10},{7,11},{8,12},{9,13},{1... | collective-permute-start | bytes 884744 | tf_op jit(solution)/shard_map/ppermute | solution.py:52
  94.7 17.3 %copy-start.10 = (bf16[96,1024]{1,0:T(8,128)(2,1)}, bf16[96,1024]{1,0:T(8,128)(2,1)S(1)}, u32[]{:S(2)}) copy-start(bf16[96,1024]{1,0:T(8,128)(2,1)S(1)} %get-tuple-element.124.refs_0_) | copy-start | bytes 589828
  94.7 17.2 %collective-permute-start.22 = (bf16[96,1024]{1,0:T(8,128)(2,1)S(1)}, bf16[96,1024]{1,0:T(8,128)(2,1)S(1)}, u32[]{:S(2)}, u32[]{:S(2)}) collective-permute-start(bf16[96,1024]{1,0:T(8,128)(2,1)S(1)} %get-tuple-element.111), channel_id=1, source_target_pairs={{0,12},{1,13},{2,14},{3,15},{4,0},{5,1},{6,2},{7,3},{8,4},{9,5},{1... | collective-permute-start | bytes 589832 | tf_op jit(solution)/shard_map/ppermute | solution.py:52
  95.5 16.5 %collective-permute-start.23 = (bf16[96,1024]{1,0:T(8,128)(2,1)S(1)}, bf16[96,1024]{1,0:T(8,128)(2,1)S(1)}, u32[]{:S(2)}, u32[]{:S(2)}) collective-permute-start(bf16[96,1024]{1,0:T(8,128)(2,1)S(1)} %get-tuple-element.112), channel_id=1, source_target_pairs={{0,4},{1,5},{2,6},{3,7},{4,8},{5,9},{6,10},{7,11},{8,12},{9,13},{1... | collective-permute-start | bytes 589832 | tf_op jit(solution)/shard_map/ppermute | solution.py:52
  96.8 15.1 %collective-permute-start.24 = (bf16[96,1024]{1,0:T(8,128)(2,1)S(1)}, bf16[96,1024]{1,0:T(8,128)(2,1)S(1)}, u32[]{:S(2)}, u32[]{:S(2)}) collective-permute-start(bf16[96,1024]{1,0:T(8,128)(2,1)S(1)} %get-tuple-element.113), channel_id=1, source_target_pairs={{0,8},{1,9},{2,10},{3,11},{4,12},{5,13},{6,14},{7,15},{8,0},{9,1},... | collective-permute-start | bytes 589832 | tf_op jit(solution)/shard_map/ppermute | solution.py:52
  99.6 11.2 %collective-permute-start.19 = (bf16[192,384]{1,0:T(8,128)(2,1)S(1)}, bf16[192,384]{1,0:T(8,128)(2,1)S(1)}, u32[]{:S(2)}, u32[]{:S(2)}) collective-permute-start(bf16[192,384]{1,0:T(8,128)(2,1)S(1)} %slice.17), channel_id=1, source_target_pairs={{0,12},{1,13},{2,14},{3,15},{4,0},{5,1},{6,2},{7,3},{8,4},{9,5},{1... | collective-permute-start | bytes 442376 | tf_op jit(solution)/shard_map/ppermute | solution.py:52
  101.1 10.8 %collective-permute-start.18 = (bf16[192,384]{1,0:T(8,128)(2,1)S(1)}, bf16[192,384]{1,0:T(8,128)(2,1)S(1)}, u32[]{:S(2)}, u32[]{:S(2)}) collective-permute-start(bf16[192,384]{1,0:T(8,128)(2,1)S(1)} %slice.16), channel_id=1, source_target_pairs={{0,4},{1,5},{2,6},{3,7},{4,8},{5,9},{6,10},{7,11},{8,12},{9,13},{1... | collective-permute-start | bytes 442376 | tf_op jit(solution)/shard_map/ppermute | solution.py:52
  111.9 0.7 copy-start.18
  111.9 0.8 copy-start.19
  112.0 0.7 copy-start.20
  115.6 0.9 copy-start.6
  116.4 5.3 %copy-start.14 = (s32[32,2]{0,1:T(2,128)S(1)}, s32[32,2]{0,1:T(2,128)}, u32[]{:S(2)}) copy-start(s32[32,2]{0,1:T(2,128)} %param.20) | copy-start | bytes 772
  116.4 5.3 %copy-start.15 = (f32[32,2]{0,1:T(2,128)S(1)}, f32[32,2]{0,1:T(2,128)}, u32[]{:S(2)}) copy-start(f32[32,2]{0,1:T(2,128)} %param.21) | copy-start | bytes 772
  116.4 38.5 %all-to-all-start.1 = ((bf16[32,24,512]{2,1,0:T(8,128)(2,1)}), bf16[32,24,512]{2,1,0:T(8,128)(2,1)}, u32[]{:S(2)}, u32[]{:S(2)}) async-start(bf16[32,24,512]{2,1,0:T(8,128)(2,1)} %copy-done.6), calls=%async_computation.1 | async-start | bytes 1572864 | tf_op jit(solution)/shard_map/all_to_all | solution.py:578
  123.3 1.1 copy-start.1
  124.4 1.4 copy-start.3
  125.8 1.3 copy-start.5
  129.2 25.8 %copy-start.8 = (bf16[192,192]{1,0:T(8,128)(2,1)S(1)}, bf16[192,192]{1,0:T(8,128)(2,1)}, u32[]{:S(2)}) copy-start(bf16[192,192]{1,0:T(8,128)(2,1)} %copy-done.7) | copy-start | bytes 221188
  (1 other events, 0.7 us)

commit v4 on v3

--- a/solution.py
+++ b/solution.py
@@ -505,7 +505,7 @@
         out_shape=jax.ShapeDtypeStruct((1, 96, 4096), BF16),
         scratch_shapes=[pltpu.SemaphoreType.DMA((4,))],
         cost_estimate=cost(0, 2 << 20),
-        compiler_params=params(56),
+        compiler_params=params(),
         name="place_down",
     )(where, *parts)
 
@@ -573,10 +573,10 @@
     downs = [rest, groups[2], rest_crossed, crossed[2]]
     downs, *slices = spread_down(where, downs)
     slices = [slices[0]] + [move_y(part, shift) for part, shift in zip(slices[1:], SHIFTS[1:])]
-    hiddens, slices = staged((hiddens, slices))
+    rollout_down = place_down(where, slices)
+    hiddens, rollout_down = staged((hiddens, rollout_down))
     result = second_matmul(where, hiddens, downs)
     back = lax.all_to_all(result, ("xl", "z", "y"), split_axis=0, concat_axis=0, tiled=True)
-    rollout_down = place_down(where, after(slices, result))
     rollout_gate_up = place_gate_up(where, groups + crossed)
     moe_out = combine(mixing, back)
     return (new_master_gate_up, new_master_down, rollout_gate_up, rollout_down, moe_out)

time: 158 us -> 139 us (0.88)
  Pallas kernels: 62.9 us -> 38.6 us
  waiting for transfers between devices: 41.9 us -> 46.7 us
    pallas_call x1, Pallas kernels: 25.8 us -> 1.45 us  [place_down(): pl.pallas_call(place_kernel, in_specs=[SMEM] + [ANY] * 4, out_specs=ANY,...]
    all_to_all x1, waiting for transfers between devices: 0.01 us -> 6.31 us  [body(): lax.all_to_all(result, ('xl', 'z', 'y'), split_axis=0, concat_axis=0, til...]
    unnamed x45 -> x35, local copies, waits for them, and re-layouts: 7.85 us -> 7.98 us
  transfers between devices with their start and end apart: 27 -> 27, of which waited for: 12 -> 14; matrix products, arithmetic and copies ran while one was open for 0% -> 0% of each run, Pallas kernels for 35% -> 23%
where the time goes in v4:
time: 139 us; the launch traced here: 138 us
  waiting for transfers between devices  46.7 us (34%)
  starting transfers between devices  43.3 us (31%)
  Pallas kernels  38.6 us (28%)
  local copies, waits for them, and re-layouts  8.09 us (6%)
    ppermute x25, waiting for transfers between devices, move(): return lax.ppermute(array, AXES, pairs)  40.4 us
    ppermute x25, starting transfers between devices, move(): return lax.ppermute(array, AXES, pairs)  31.3 us
    pallas_call x3, Pallas kernels, adam(): pl.pallas_call(functools.partial(adam_kernel, count, parts, rows), in_spe...  16.1 us
    unnamed x35, local copies, waits for them, and re-layouts  7.98 us
    all_to_all x1, starting transfers between devices, body(): lax.all_to_all(dispatched, ('xl', 'z'), split_axis=0, concat_axis=0, tile...  6.32 us
    all_to_all x1, waiting for transfers between devices, body(): lax.all_to_all(result, ('xl', 'z', 'y'), split_axis=0, concat_axis=0, til...  6.31 us
    all_to_all x1, starting transfers between devices, body(): lax.all_to_all(result, ('xl', 'z', 'y'), split_axis=0, concat_axis=0, til...  5.65 us
    pallas_call x1, Pallas kernels, first_half(): pl.pallas_call(first_half_kernel, in_specs=[SMEM] + [ANY] * 11, out_specs...  4.67 us
  transfers between devices with their start and end apart: 27, of which 14 were waited for; matrix products, arithmetic and copies ran while one was open for 0% of the time, Pallas kernels for 23%

profile of v4, /device:TPU:0, one launch (start us, length us, event | category | flops | bytes accessed | tf_op | source)
XLA Modules:
  0.0 138.1 jit_solution(13881170699983164392)
XLA Ops:
  0.7 1.0 copy-done.9
  2.4 2.2 %dispatch.1 = bf16[8,24,2048]{2,1,0:T(8,128)(2,1)} custom-call(s32[3]{0:T(128)S(1)} %get-tuple-element.116.where_ref, s32[3]{0:T(128)S(1)} %get-tuple-element.60.near_ref.blocks_ref, s32[2,32]{1,0:T(2,128)S(1)} %bitcast.15, bf16[32,4096]{1,0:T(8,128)(2,1)S(1)} %copy-done.9), custom_call_target="tpu_custom_call" | custom-call | flops 50331648 | bytes 2097152 | tf_op jit(solution)/shard_map/dispatch/pallas_call | solution.py:170
  4.6 6.3 %all-to-all-start = ((bf16[8,24,2048]{2,1,0:T(8,128)(2,1)}), bf16[8,24,2048]{2,1,0:T(8,128)(2,1)S(1)}, u32[]{:S(2)}, u32[]{:S(2)}) async-start(bf16[8,24,2048]{2,1,0:T(8,128)(2,1)} %dispatch.1), calls=%async_computation | async-start | bytes 1572864 | tf_op jit(solution)/shard_map/all_to_all | solution.py:531
  10.9 7.2 %adam.3 = (f32[1,2,1536,256]{3,2,1,0:T(8,128)}, bf16[2,384,256]{2,1,0:T(8,128)(2,1)}, bf16[2,384,256]{2,1,0:T(8,128)(2,1)}, bf16[2,384,256]{2,1,0:T(8,128)(2,1)}) custom-call(s32[3]{0:T(128)} %copy-done.10, f32[1,2,1536,256]{3,2,1,0:T(8,128)} %refs_0_.3, f32[1,2,1536,256]{3,2,1,0:T(8,128)} %refs_1_.3, f32[1,2,1536,256]{3,2,1,0:T(8,128)} %refs_2_.3, ...), custom_call_target="tpu_custom_call" | custom-call | bytes 12976128 | tf_op jit(solution)/shard_map/adam/pallas_call | solution.py:120
  18.1 1.6 %collective-permute-start = (bf16[2,384,256]{2,1,0:T(8,128)(2,1)}, bf16[2,384,256]{2,1,0:T(8,128)(2,1)S(1)}, u32[]{:S(2)}, u32[]{:S(2)}) collective-permute-start(bf16[2,384,256]{2,1,0:T(8,128)(2,1)} %get-tuple-element.66), channel_id=1, source_target_pairs={{0,4},{1,5},{2,6},{3,7},{4,8},{5,9},{6,10},{7,11},{8,12},{9,13},{1... | collective-permute-start | bytes 1179656 | tf_op jit(solution)/shard_map/ppermute | solution.py:52
  19.7 1.7 %collective-permute-start.1 = (bf16[2,384,256]{2,1,0:T(8,128)(2,1)}, bf16[2,384,256]{2,1,0:T(8,128)(2,1)S(1)}, u32[]{:S(2)}, u32[]{:S(2)}) collective-permute-start(bf16[2,384,256]{2,1,0:T(8,128)(2,1)} %get-tuple-element.67), channel_id=1, source_target_pairs={{0,12},{1,13},{2,14},{3,15},{4,0},{5,1},{6,2},{7,3},{8,4},{9,5},{1... | collective-permute-start | bytes 1179656 | tf_op jit(solution)/shard_map/ppermute | solution.py:52
  21.4 2.7 %collective-permute-start.2 = (bf16[2,384,256]{2,1,0:T(8,128)(2,1)}, bf16[2,384,256]{2,1,0:T(8,128)(2,1)S(1)}, u32[]{:S(2)}, u32[]{:S(2)}) collective-permute-start(bf16[2,384,256]{2,1,0:T(8,128)(2,1)} %get-tuple-element.68), channel_id=1, source_target_pairs={{0,2},{1,3},{2,0},{3,1},{4,6},{5,7},{6,4},{7,5},{8,10},{9,11},{10,... | collective-permute-start | bytes 1179656 | tf_op jit(solution)/shard_map/ppermute | solution.py:52
  24.1 3.8 %adam.4 = (f32[1,2,1536,256]{3,2,1,0:T(8,128)}, bf16[2,384,256]{2,1,0:T(8,128)(2,1)}) custom-call(s32[1]{0:T(128)} %bitcast.blocks_ref, f32[1,2,1536,256]{3,2,1,0:T(8,128)} %refs_0_.3, f32[1,2,1536,256]{3,2,1,0:T(8,128)} %refs_1_.3, f32[1,2,1536,256]{3,2,1,0:T(8,128)} %refs_2_.3, f32[1,2,1536,256]{3,2,1,0:T(8,128)} %refs_3_.3, ...), custom_call_target="tpu_custom_call", output_to_operand_aliasing={{0}: (5, {})} | custom-call | bytes 4325376 | tf_op jit(solution)/shard_map/adam/pallas_call | solution.py:120
  28.0 5.2 %adam.5 = (f32[1,1,1536,256]{3,2,1,0:T(8,128)}, bf16[1,1536,256]{2,1,0:T(8,128)(2,1)}) custom-call(s32[1]{0:T(128)} %constant.38.clone.1.blocks_ref, f32[1,1,1536,256]{3,2,1,0:T(8,128)} %bitcast.22, f32[1,1,1536,256]{3,2,1,0:T(8,128)} %bitcast.23, f32[1,1,1536,256]{3,2,1,0:T(8,128)} %bitcast.24, f32[1,1,1536,256]{3,2,1,0:T(8,128)} %bitcast.25), custom_call_target="tpu_custom_call" | custom-call | bytes 8650752 | tf_op jit(solution)/shard_map/adam/pallas_call | solution.py:120
  33.3 2.0 %collective-permute-start.3 = (bf16[2,384,256]{2,1,0:T(8,128)(2,1)S(1)}, bf16[2,384,256]{2,1,0:T(8,128)(2,1)S(1)}, u32[]{:S(2)}, u32[]{:S(2)}) collective-permute-start(bf16[2,384,256]{2,1,0:T(8,128)(2,1)S(1)} %copy-done.16), channel_id=1, source_target_pairs={{0,8},{1,9},{2,10},{3,11},{4,12},{5,13},{6,14},{7,15},{8,0},{9,1},... | collective-permute-start | bytes 1179656 | tf_op jit(solution)/shard_map/ppermute | solution.py:52
  35.3 2.6 %collective-permute-start.6 = (bf16[2,384,256]{2,1,0:T(8,128)(2,1)S(1)}, bf16[2,384,256]{2,1,0:T(8,128)(2,1)S(1)}, u32[]{:S(2)}, u32[]{:S(2)}) collective-permute-start(bf16[2,384,256]{2,1,0:T(8,128)(2,1)S(1)} %collective-permute-done), channel_id=1, source_target_pairs={{0,2},{1,3},{2,0},{3,1},{4,6},{5,7},{6,4},{7,5},{8,10},{9,11},{10,... | collective-permute-start | bytes 1179656 | tf_op jit(solution)/shard_map/ppermute | solution.py:52
  37.9 0.9 collective-permute-start.7
  38.8 0.9 unpack.1
  40.5 2.6 %collective-permute-start.5 = (bf16[48,4096]{1,0:T(8,128)(2,1)S(1)}, bf16[48,4096]{1,0:T(8,128)(2,1)S(1)}, u32[]{:S(2)}, u32[]{:S(2)}) collective-permute-start(bf16[48,4096]{1,0:T(8,128)(2,1)S(1)} %get-tuple-element.91.refs_1_), channel_id=1, source_target_pairs={{0,12},{1,13},{2,14},{3,15},{4,0},{5,1},{6,2},{7,3},{8,4},{9,5},{1... | collective-permute-start | bytes 1179656 | tf_op jit(solution)/shard_map/ppermute | solution.py:52
  43.2 3.6 %collective-permute-done.3 = bf16[2,384,256]{2,1,0:T(8,128)(2,1)S(1)} collective-permute-done((bf16[2,384,256]{2,1,0:T(8,128)(2,1)S(1)}, bf16[2,384,256]{2,1,0:T(8,128)(2,1)S(1)}, u32[]{:S(2)}, u32[]{:S(2)}) %collective-permute-start.3) | collective-permute-done | bytes 393248 | tf_op jit(solution)/shard_map/ppermute | solution.py:52
  46.9 2.0 %collective-permute-done.6 = bf16[2,384,256]{2,1,0:T(8,128)(2,1)S(1)} collective-permute-done((bf16[2,384,256]{2,1,0:T(8,128)(2,1)S(1)}, bf16[2,384,256]{2,1,0:T(8,128)(2,1)S(1)}, u32[]{:S(2)}, u32[]{:S(2)}) %collective-permute-start.6) | collective-permute-done | bytes 393248 | tf_op jit(solution)/shard_map/ppermute | solution.py:52
  48.8 5.8 %collective-permute-done.7 = bf16[2,384,256]{2,1,0:T(8,128)(2,1)S(1)} collective-permute-done((bf16[2,384,256]{2,1,0:T(8,128)(2,1)S(1)}, bf16[2,384,256]{2,1,0:T(8,128)(2,1)S(1)}, u32[]{:S(2)}, u32[]{:S(2)}) %collective-permute-start.7) | collective-permute-done | bytes 393248 | tf_op jit(solution)/shard_map/ppermute | solution.py:52
  54.8 2.0 %collective-permute-start.12 = (bf16[4,384,256]{2,1,0:T(8,128)(2,1)S(1)}, bf16[4,384,256]{2,1,0:T(8,128)(2,1)S(1)}, u32[]{:S(2)}, u32[]{:S(2)}) collective-permute-start(bf16[4,384,256]{2,1,0:T(8,128)(2,1)S(1)} %pad_maximum_fusion.2), channel_id=1, source_target_pairs={{0,2},{1,3},{2,0},{3,1},{4,6},{5,7},{6,4},{7,5},{8,10},{9,11},{10,... | collective-permute-start | bytes 2359304 | tf_op jit(solution)/shard_map/ppermute | solution.py:52
  56.8 1.0 collective-permute-start.9
  57.9 1.0 collective-permute-start.8
  59.5 2.6 %collective-permute-start.11 = (bf16[48,4096]{1,0:T(8,128)(2,1)S(1)}, bf16[48,4096]{1,0:T(8,128)(2,1)S(1)}, u32[]{:S(2)}, u32[]{:S(2)}) collective-permute-start(bf16[48,4096]{1,0:T(8,128)(2,1)S(1)} %collective-permute-done.5.refs_5_), channel_id=1, source_target_pairs={{0,12},{1,13},{2,14},{3,15},{4,0},{5,1},{6,2},{7,3},{8,4},{9,5},{1... | collective-permute-start | bytes 1179656 | tf_op jit(solution)/shard_map/ppermute | solution.py:52
  62.2 6.6 %collective-permute-done.9.refs_4_ = bf16[48,4096]{1,0:T(8,128)(2,1)S(1)} collective-permute-done((bf16[48,4096]{1,0:T(8,128)(2,1)S(1)}, bf16[48,4096]{1,0:T(8,128)(2,1)S(1)}, u32[]{:S(2)}, u32[]{:S(2)}) %collective-permute-start.9) | collective-permute-done | bytes 393248 | tf_op jit(solution)/shard_map/ppermute | solution.py:52
  68.8 2.4 %collective-permute-done.8.refs_3_ = bf16[48,4096]{1,0:T(8,128)(2,1)S(1)} collective-permute-done((bf16[48,4096]{1,0:T(8,128)(2,1)S(1)}, bf16[48,4096]{1,0:T(8,128)(2,1)S(1)}, u32[]{:S(2)}, u32[]{:S(2)}) %collective-permute-start.8) | collective-permute-done | bytes 393248 | tf_op jit(solution)/shard_map/ppermute | solution.py:52
  71.1 4.4 %collective-permute-done.10.refs_6_ = bf16[48,4096]{1,0:T(8,128)(2,1)S(1)} collective-permute-done((bf16[48,4096]{1,0:T(8,128)(2,1)S(1)}, bf16[48,4096]{1,0:T(8,128)(2,1)S(1)}, u32[]{:S(2)}, u32[]{:S(2)}) %collective-permute-start.10) | collective-permute-done | bytes 393248 | tf_op jit(solution)/shard_map/ppermute | solution.py:52
  76.3 1.8 %collective-permute-start.20 = (bf16[768,256]{1,0:T(8,128)(2,1)S(1)}, bf16[768,256]{1,0:T(8,128)(2,1)S(1)}, u32[]{:S(2)}, u32[]{:S(2)}) collective-permute-start(bf16[768,256]{1,0:T(8,128)(2,1)S(1)} %slice.15), channel_id=1, source_target_pairs={{0,2},{1,3},{2,0},{3,1},{4,6},{5,7},{6,4},{7,5},{8,10},{9,11},{10,... | collective-permute-start | bytes 1179656 | tf_op jit(solution)/shard_map/ppermute | solution.py:52
  78.1 4.7 %first_half.1 = (bf16[384,4096]{1,0:T(8,128)(2,1)S(1)}, f32[2,384,384]{2,1,0:T(8,128)S(1)}) custom-call(s32[3]{0:T(128)S(1)} %get-tuple-element.116.where_ref, bf16[48,4096]{1,0:T(8,128)(2,1)S(1)} %get-tuple-element.90.refs_0_, bf16[48,4096]{1,0:T(8,128)(2,1)S(1)} %get-tuple-element.91.refs_1_, bf16[48,4096]{1,0:T(8,128)(2,1)S(1)} %collective-permute-done.4.refs_2_, ...), custom_call_target="tpu_custom_call" | custom-call | flops 1207959552 | bytes 8388608 | tf_op jit(solution)/shard_map/first_half/pallas_call | solution.py:322
  82.9 3.1 %last_half.1.refs_0_ = bf16[384,384]{1,0:T(8,128)(2,1)S(1)} custom-call(s32[3]{0:T(128)S(1)} %get-tuple-element.116.where_ref, bf16[384,4096]{1,0:T(8,128)(2,1)S(1)} %get-tuple-element.98.x_ref, f32[2,384,384]{2,1,0:T(8,128)S(1)} %get-tuple-element.99.acc_ref, bf16[8,384,256]{2,1,0:T(8,128)(2,1)S(1)} %collective-permute-done.13.refs_3_.refs_0_, ...), custom_call_target="tpu_custom_call" | custom-call | flops 1207959552 | bytes 8388608 | tf_op jit(solution)/shard_map/last_half/pallas_call | solution.py:339
  86.0 3.5 %collective-permute-done.20 = bf16[768,256]{1,0:T(8,128)(2,1)S(1)} collective-permute-done((bf16[768,256]{1,0:T(8,128)(2,1)S(1)}, bf16[768,256]{1,0:T(8,128)(2,1)S(1)}, u32[]{:S(2)}, u32[]{:S(2)}) %collective-permute-start.20) | collective-permute-done | bytes 393248 | tf_op jit(solution)/shard_map/ppermute | solution.py:52
  89.9 1.8 %collective-permute-start.16 = (bf16[384,384]{1,0:T(8,128)(2,1)S(1)}, bf16[384,384]{1,0:T(8,128)(2,1)S(1)}, u32[]{:S(2)}, u32[]{:S(2)}) collective-permute-start(bf16[384,384]{1,0:T(8,128)(2,1)S(1)} %last_half.1.refs_0_), channel_id=1, source_target_pairs={{0,4},{1,5},{2,6},{3,7},{4,8},{5,9},{6,10},{7,11},{8,12},{9,13},{1... | collective-permute-start | bytes 884744 | tf_op jit(solution)/shard_map/ppermute | solution.py:52
  92.5 2.2 %spread_down.1 = (bf16[1536,1024]{1,0:T(8,128)(2,1)S(1)}, bf16[96,1024]{1,0:T(8,128)(2,1)S(1)}, bf16[96,1024]{1,0:T(8,128)(2,1)S(1)}, bf16[96,1024]{1,0:T(8,128)(2,1)S(1)}, bf16[96,1024]{1,0:T(8,128)(2,1)S(1)}) custom-call(s32[3]{0:T(128)S(1)} %get-tuple-element.116.where_ref, bf16[2304,256]{1,0:T(8,128)(2,1)S(1)} %constant_dynamic-update-slice_fusion.refs_0_, ...), custom_call_target="tpu_custom_call" | custom-call | bytes 8388608 | tf_op jit(solution)/shard_map/spread_down/pallas_call | solution.py:417
  95.4 1.4 collective-permute-start.23
  97.0 2.6 %collective-permute-done.17.refs_2_ = bf16[384,384]{1,0:T(8,128)(2,1)S(1)} collective-permute-done((bf16[384,384]{1,0:T(8,128)(2,1)S(1)}, bf16[384,384]{1,0:T(8,128)(2,1)S(1)}, u32[]{:S(2)}, u32[]{:S(2)}) %collective-permute-start.17) | collective-permute-done | bytes 294944 | tf_op jit(solution)/shard_map/ppermute | solution.py:52
  99.6 1.5 %collective-permute-start.19 = (bf16[192,384]{1,0:T(8,128)(2,1)S(1)}, bf16[192,384]{1,0:T(8,128)(2,1)S(1)}, u32[]{:S(2)}, u32[]{:S(2)}) collective-permute-start(bf16[192,384]{1,0:T(8,128)(2,1)S(1)} %slice.17), channel_id=1, source_target_pairs={{0,12},{1,13},{2,14},{3,15},{4,0},{5,1},{6,2},{7,3},{8,4},{9,5},{1... | collective-permute-start | bytes 442376 | tf_op jit(solution)/shard_map/ppermute | solution.py:52
  101.8 2.0 %collective-permute-done.22.refs_1_ = bf16[96,1024]{1,0:T(8,128)(2,1)S(1)} collective-permute-done((bf16[96,1024]{1,0:T(8,128)(2,1)S(1)}, bf16[96,1024]{1,0:T(8,128)(2,1)S(1)}, u32[]{:S(2)}, u32[]{:S(2)}) %collective-permute-start.22) | collective-permute-done | bytes 196640 | tf_op jit(solution)/shard_map/ppermute | solution.py:52
  103.8 5.6 %collective-permute-done.23.refs_2_ = bf16[96,1024]{1,0:T(8,128)(2,1)S(1)} collective-permute-done((bf16[96,1024]{1,0:T(8,128)(2,1)S(1)}, bf16[96,1024]{1,0:T(8,128)(2,1)S(1)}, u32[]{:S(2)}, u32[]{:S(2)}) %collective-permute-start.23) | collective-permute-done | bytes 196640 | tf_op jit(solution)/shard_map/ppermute | solution.py:52
  109.4 1.5 %place_down.1 = bf16[1,96,4096]{2,1,0:T(8,128)(2,1)} custom-call(s32[3]{0:T(128)S(1)} %get-tuple-element.116.where_ref, bf16[96,1024]{1,0:T(8,128)(2,1)S(1)} %get-tuple-element.103.refs_0_, bf16[96,1024]{1,0:T(8,128)(2,1)S(1)} %collective-permute-done.22.refs_1_, bf16[96,1024]{1,0:T(8,128)(2,1)S(1)} %collective-permute-done.23.refs_2_, ...), custom_call_target="tpu_custom_call" | custom-call | bytes 2097152 | tf_op jit(solution)/shard_map/place_down/pallas_call | solution.py:501
  110.9 1.0 collective-permute-done.18.refs_3_
  111.9 2.8 %second_matmul.1 = bf16[32,24,512]{2,1,0:T(8,128)(2,1)S(1)} custom-call(s32[3]{0:T(128)S(1)} %get-tuple-element.116.where_ref, bf16[384,384]{1,0:T(8,128)(2,1)S(1)} %last_half.1.refs_0_, bf16[384,384]{1,0:T(8,128)(2,1)S(1)} %collective-permute-done.16.refs_1_, bf16[384,384]{1,0:T(8,128)(2,1)S(1)} %collective-permute-done.17.refs_2_, ...), custom_call_target="tpu_custom_call" | custom-call | flops 1207959552 | bytes 6291456 | tf_op jit(solution)/shard_map/second_matmul/pallas_call | solution.py:471
  114.7 0.9 copy-done.6
  115.6 5.7 %all-to-all-start.1 = ((bf16[32,24,512]{2,1,0:T(8,128)(2,1)}), bf16[32,24,512]{2,1,0:T(8,128)(2,1)}, u32[]{:S(2)}, u32[]{:S(2)}) async-start(bf16[32,24,512]{2,1,0:T(8,128)(2,1)} %copy-done.6), calls=%async_computation.1 | async-start | bytes 1572864 | tf_op jit(solution)/shard_map/all_to_all | solution.py:579
  121.3 0.8 mix.1.mixing_ref
  122.7 1.1 copy-done.1
  123.9 1.4 %copy-done.3 = bf16[8,384,256]{2,1,0:T(8,128)(2,1)S(1)} copy-done((bf16[8,384,256]{2,1,0:T(8,128)(2,1)S(1)}, bf16[8,384,256]{2,1,0:T(8,128)(2,1)}, u32[]{:S(2)}) %copy-start.3) | copy-done | bytes 1572888
  125.3 1.3 copy-done.5
  126.6 2.1 %place_gate_up.1 = bf16[1,2,96,4096]{3,2,1,0:T(8,128)(2,1)} custom-call(s32[3]{0:T(128)S(1)} %get-tuple-element.116.where_ref, bf16[8,384,256]{2,1,0:T(8,128)(2,1)S(1)} %pad_maximum_fusion.refs_0_.refs_8_, bf16[6,384,256]{2,1,0:T(8,128)(2,1)S(1)} %pad_maximum_fusion.1.refs_1_.refs_9_, bf16[4,384,256]{2,1,0:T(8,128)(2,1)S(1)} %copy-done.1, ...), custom_call_target="tpu_custom_call" | custom-call | bytes 4194304 | tf_op jit(solution)/shard_map/place_gate_up/pallas_call | solution.py:371
  128.7 6.3 %all-to-all-done.1.back_ref = bf16[32,24,512]{2,1,0:T(8,128)(2,1)} async-done(((bf16[32,24,512]{2,1,0:T(8,128)(2,1)}), bf16[32,24,512]{2,1,0:T(8,128)(2,1)}, u32[]{:S(2)}, u32[]{:S(2)}) %all-to-all-start.1) | async-done | bytes 786464 | tf_op jit(solution)/shard_map/all_to_all | solution.py:579
  135.0 0.9 copy-done.8
  135.9 2.2 %combine.1 = bf16[32,4096]{1,0:T(8,128)(2,1)} custom-call(bf16[192,192]{1,0:T(8,128)(2,1)S(1)} %copy-done.8, bf16[32,24,512]{2,1,0:T(8,128)(2,1)} %all-to-all-done.1.back_ref), custom_call_target="tpu_custom_call" | custom-call | flops 150994944 | bytes 2097152 | tf_op jit(solution)/shard_map/combine/pallas_call | solution.py:252
  (63 shorter events, 7.0 us)
Async XLA Ops:
  0.7 10.2 %copy-start.10 = (s32[3]{0:T(128)}, s32[3]{0:T(128)S(1)}, u32[]{:S(2)}) copy-start(s32[3]{0:T(128)S(1)} %get-tuple-element.60.near_ref.blocks_ref) | copy-start | bytes 40
  0.7 1.0 copy-start.9
  1.7 0.7 copy-start.11
  4.6 28.7 %all-to-all-start = ((bf16[8,24,2048]{2,1,0:T(8,128)(2,1)}), bf16[8,24,2048]{2,1,0:T(8,128)(2,1)S(1)}, u32[]{:S(2)}, u32[]{:S(2)}) async-start(bf16[8,24,2048]{2,1,0:T(8,128)(2,1)} %dispatch.1), calls=%async_computation | async-start | bytes 1572864 | tf_op jit(solution)/shard_map/all_to_all | solution.py:531
  18.1 15.0 %collective-permute-start = (bf16[2,384,256]{2,1,0:T(8,128)(2,1)}, bf16[2,384,256]{2,1,0:T(8,128)(2,1)S(1)}, u32[]{:S(2)}, u32[]{:S(2)}) collective-permute-start(bf16[2,384,256]{2,1,0:T(8,128)(2,1)} %get-tuple-element.66), channel_id=1, source_target_pairs={{0,4},{1,5},{2,6},{3,7},{4,8},{5,9},{6,10},{7,11},{8,12},{9,13},{1... | collective-permute-start | bytes 1179656 | tf_op jit(solution)/shard_map/ppermute | solution.py:52
  19.7 13.4 %collective-permute-start.1 = (bf16[2,384,256]{2,1,0:T(8,128)(2,1)}, bf16[2,384,256]{2,1,0:T(8,128)(2,1)S(1)}, u32[]{:S(2)}, u32[]{:S(2)}) collective-permute-start(bf16[2,384,256]{2,1,0:T(8,128)(2,1)} %get-tuple-element.67), channel_id=1, source_target_pairs={{0,12},{1,13},{2,14},{3,15},{4,0},{5,1},{6,2},{7,3},{8,4},{9,5},{1... | collective-permute-start | bytes 1179656 | tf_op jit(solution)/shard_map/ppermute | solution.py:52
  21.4 11.9 %collective-permute-start.2 = (bf16[2,384,256]{2,1,0:T(8,128)(2,1)}, bf16[2,384,256]{2,1,0:T(8,128)(2,1)S(1)}, u32[]{:S(2)}, u32[]{:S(2)}) collective-permute-start(bf16[2,384,256]{2,1,0:T(8,128)(2,1)} %get-tuple-element.68), channel_id=1, source_target_pairs={{0,2},{1,3},{2,0},{3,1},{4,6},{5,7},{6,4},{7,5},{8,10},{9,11},{10,... | collective-permute-start | bytes 1179656 | tf_op jit(solution)/shard_map/ppermute | solution.py:52
  28.0 5.3 %copy-start.16 = (bf16[2,384,256]{2,1,0:T(8,128)(2,1)S(1)}, bf16[2,384,256]{2,1,0:T(8,128)(2,1)}, u32[]{:S(2)}) copy-start(bf16[2,384,256]{2,1,0:T(8,128)(2,1)} %get-tuple-element.70) | copy-start | bytes 1179652
  28.0 15.0 %copy-start.15 = (bf16[2,384,256]{2,1,0:T(8,128)(2,1)S(1)}, bf16[2,384,256]{2,1,0:T(8,128)(2,1)}, u32[]{:S(2)}) copy-start(bf16[2,384,256]{2,1,0:T(8,128)(2,1)} %get-tuple-element.68) | copy-start | bytes 1179652
  33.3 13.6 %collective-permute-start.3 = (bf16[2,384,256]{2,1,0:T(8,128)(2,1)S(1)}, bf16[2,384,256]{2,1,0:T(8,128)(2,1)S(1)}, u32[]{:S(2)}, u32[]{:S(2)}) collective-permute-start(bf16[2,384,256]{2,1,0:T(8,128)(2,1)S(1)} %copy-done.16), channel_id=1, source_target_pairs={{0,8},{1,9},{2,10},{3,11},{4,12},{5,13},{6,14},{7,15},{8,0},{9,1},... | collective-permute-start | bytes 1179656 | tf_op jit(solution)/shard_map/ppermute | solution.py:52
  35.3 13.6 %collective-permute-start.6 = (bf16[2,384,256]{2,1,0:T(8,128)(2,1)S(1)}, bf16[2,384,256]{2,1,0:T(8,128)(2,1)S(1)}, u32[]{:S(2)}, u32[]{:S(2)}) collective-permute-start(bf16[2,384,256]{2,1,0:T(8,128)(2,1)S(1)} %collective-permute-done), channel_id=1, source_target_pairs={{0,2},{1,3},{2,0},{3,1},{4,6},{5,7},{6,4},{7,5},{8,10},{9,11},{10,... | collective-permute-start | bytes 1179656 | tf_op jit(solution)/shard_map/ppermute | solution.py:52
  37.9 16.8 %collective-permute-start.7 = (bf16[2,384,256]{2,1,0:T(8,128)(2,1)S(1)}, bf16[2,384,256]{2,1,0:T(8,128)(2,1)S(1)}, u32[]{:S(2)}, u32[]{:S(2)}) collective-permute-start(bf16[2,384,256]{2,1,0:T(8,128)(2,1)S(1)} %collective-permute-done.1), channel_id=1, source_target_pairs={{0,2},{1,3},{2,0},{3,1},{4,6},{5,7},{6,4},{7,5},{8,10},{9,11},{10,... | collective-permute-start | bytes 1179656 | tf_op jit(solution)/shard_map/ppermute | solution.py:52
  39.7 14.9 %collective-permute-start.4 = (bf16[48,4096]{1,0:T(8,128)(2,1)S(1)}, bf16[48,4096]{1,0:T(8,128)(2,1)S(1)}, u32[]{:S(2)}, u32[]{:S(2)}) collective-permute-start(bf16[48,4096]{1,0:T(8,128)(2,1)S(1)} %get-tuple-element.90.refs_0_), channel_id=1, source_target_pairs={{0,4},{1,5},{2,6},{3,7},{4,8},{5,9},{6,10},{7,11},{8,12},{9,13},{1... | collective-permute-start | bytes 1179656 | tf_op jit(solution)/shard_map/ppermute | solution.py:52
  40.5 14.2 %copy-start.14 = (bf16[1,1536,256]{2,1,0:T(8,128)(2,1)S(1)}, bf16[1,1536,256]{2,1,0:T(8,128)(2,1)}, u32[]{:S(2)}) copy-start(bf16[1,1536,256]{2,1,0:T(8,128)(2,1)} %get-tuple-element.69) | copy-start | bytes 2359300
  40.5 14.2 %collective-permute-start.5 = (bf16[48,4096]{1,0:T(8,128)(2,1)S(1)}, bf16[48,4096]{1,0:T(8,128)(2,1)S(1)}, u32[]{:S(2)}, u32[]{:S(2)}) collective-permute-start(bf16[48,4096]{1,0:T(8,128)(2,1)S(1)} %get-tuple-element.91.refs_1_), channel_id=1, source_target_pairs={{0,12},{1,13},{2,14},{3,15},{4,0},{5,1},{6,2},{7,3},{8,4},{9,5},{1... | collective-permute-start | bytes 1179656 | tf_op jit(solution)/shard_map/ppermute | solution.py:52
  54.8 20.8 %collective-permute-start.12 = (bf16[4,384,256]{2,1,0:T(8,128)(2,1)S(1)}, bf16[4,384,256]{2,1,0:T(8,128)(2,1)S(1)}, u32[]{:S(2)}, u32[]{:S(2)}) collective-permute-start(bf16[4,384,256]{2,1,0:T(8,128)(2,1)S(1)} %pad_maximum_fusion.2), channel_id=1, source_target_pairs={{0,2},{1,3},{2,0},{3,1},{4,6},{5,7},{6,4},{7,5},{8,10},{9,11},{10,... | collective-permute-start | bytes 2359304 | tf_op jit(solution)/shard_map/ppermute | solution.py:52
  56.8 11.9 %collective-permute-start.9 = (bf16[48,4096]{1,0:T(8,128)(2,1)S(1)}, bf16[48,4096]{1,0:T(8,128)(2,1)S(1)}, u32[]{:S(2)}, u32[]{:S(2)}) collective-permute-start(bf16[48,4096]{1,0:T(8,128)(2,1)S(1)} %get-tuple-element.90.refs_0_), channel_id=1, source_target_pairs={{0,12},{1,13},{2,14},{3,15},{4,0},{5,1},{6,2},{7,3},{8,4},{9,5},{1... | collective-permute-start | bytes 1179656 | tf_op jit(solution)/shard_map/ppermute | solution.py:52
  57.9 13.3 %collective-permute-start.8 = (bf16[48,4096]{1,0:T(8,128)(2,1)S(1)}, bf16[48,4096]{1,0:T(8,128)(2,1)S(1)}, u32[]{:S(2)}, u32[]{:S(2)}) collective-permute-start(bf16[48,4096]{1,0:T(8,128)(2,1)S(1)} %get-tuple-element.91.refs_1_), channel_id=1, source_target_pairs={{0,4},{1,5},{2,6},{3,7},{4,8},{5,9},{6,10},{7,11},{8,12},{9,13},{1... | collective-permute-start | bytes 1179656 | tf_op jit(solution)/shard_map/ppermute | solution.py:52
  58.8 16.7 %collective-permute-start.10 = (bf16[48,4096]{1,0:T(8,128)(2,1)S(1)}, bf16[48,4096]{1,0:T(8,128)(2,1)S(1)}, u32[]{:S(2)}, u32[]{:S(2)}) collective-permute-start(bf16[48,4096]{1,0:T(8,128)(2,1)S(1)} %collective-permute-done.4.refs_2_), channel_id=1, source_target_pairs={{0,4},{1,5},{2,6},{3,7},{4,8},{5,9},{6,10},{7,11},{8,12},{9,13},{1... | collective-permute-start | bytes 1179656 | tf_op jit(solution)/shard_map/ppermute | solution.py:52
  59.5 16.0 %collective-permute-start.11 = (bf16[48,4096]{1,0:T(8,128)(2,1)S(1)}, bf16[48,4096]{1,0:T(8,128)(2,1)S(1)}, u32[]{:S(2)}, u32[]{:S(2)}) collective-permute-start(bf16[48,4096]{1,0:T(8,128)(2,1)S(1)} %collective-permute-done.5.refs_5_), channel_id=1, source_target_pairs={{0,12},{1,13},{2,14},{3,15},{4,0},{5,1},{6,2},{7,3},{8,4},{9,5},{1... | collective-permute-start | bytes 1179656 | tf_op jit(solution)/shard_map/ppermute | solution.py:52
  75.6 17.0 %copy-start = (bf16[4,384,256]{2,1,0:T(8,128)(2,1)}, bf16[4,384,256]{2,1,0:T(8,128)(2,1)S(1)}, u32[]{:S(2)}) copy-start(bf16[4,384,256]{2,1,0:T(8,128)(2,1)S(1)} %collective-permute-done.12.refs_2_.refs_10_.refs_1_) | copy-start | bytes 2359300
  75.6 7.3 %collective-permute-start.13 = (bf16[8,384,256]{2,1,0:T(8,128)(2,1)S(1)}, bf16[8,384,256]{2,1,0:T(8,128)(2,1)S(1)}, u32[]{:S(2)}, u32[]{:S(2)}) collective-permute-start(bf16[8,384,256]{2,1,0:T(8,128)(2,1)S(1)} %pad_maximum_fusion.refs_0_.refs_8_), channel_id=1, source_target_pairs={{0,1},{1,0},{2,3},{3,2},{4,5},{5,4},{6,7},{7,6},{8,9},{9,8},{10,11... | collective-permute-start | bytes 4718600 | tf_op jit(solution)/shard_map/ppermute | solution.py:52
  75.7 7.2 %collective-permute-start.14 = (bf16[6,384,256]{2,1,0:T(8,128)(2,1)S(1)}, bf16[6,384,256]{2,1,0:T(8,128)(2,1)S(1)}, u32[]{:S(2)}, u32[]{:S(2)}) collective-permute-start(bf16[6,384,256]{2,1,0:T(8,128)(2,1)S(1)} %pad_maximum_fusion.1.refs_1_.refs_9_), channel_id=1, source_target_pairs={{0,1},{1,0},{2,3},{3,2},{4,5},{5,4},{6,7},{7,6},{8,9},{9,8},{10,11... | collective-permute-start | bytes 3538952 | tf_op jit(solution)/shard_map/ppermute | solution.py:52
  76.2 6.6 %collective-permute-start.15 = (bf16[4,384,256]{2,1,0:T(8,128)(2,1)S(1)}, bf16[4,384,256]{2,1,0:T(8,128)(2,1)S(1)}, u32[]{:S(2)}, u32[]{:S(2)}) collective-permute-start(bf16[4,384,256]{2,1,0:T(8,128)(2,1)S(1)} %collective-permute-done.12.refs_2_.refs_10_.refs_1_), channel_id=1, source_target_pairs={{0,1},{1,0},{2,3},{3,2},{4,5},{5,4},{6,7},{7,6},{8,9},{9,8},{10,11... | collective-permute-start | bytes 2359304 | tf_op jit(solution)/shard_map/ppermute | solution.py:52
  76.3 13.2 %collective-permute-start.20 = (bf16[768,256]{1,0:T(8,128)(2,1)S(1)}, bf16[768,256]{1,0:T(8,128)(2,1)S(1)}, u32[]{:S(2)}, u32[]{:S(2)}) collective-permute-start(bf16[768,256]{1,0:T(8,128)(2,1)S(1)} %slice.15), channel_id=1, source_target_pairs={{0,2},{1,3},{2,0},{3,1},{4,6},{5,7},{6,4},{7,5},{8,10},{9,11},{10,... | collective-permute-start | bytes 1179656 | tf_op jit(solution)/shard_map/ppermute | solution.py:52
  82.8 3.2 %copy-start.4 = (bf16[6,384,256]{2,1,0:T(8,128)(2,1)}, bf16[6,384,256]{2,1,0:T(8,128)(2,1)S(1)}, u32[]{:S(2)}) copy-start(bf16[6,384,256]{2,1,0:T(8,128)(2,1)S(1)} %collective-permute-done.14.refs_4_.refs_1_) | copy-start | bytes 3538948
  82.8 3.2 %copy-start.2 = (bf16[8,384,256]{2,1,0:T(8,128)(2,1)}, bf16[8,384,256]{2,1,0:T(8,128)(2,1)S(1)}, u32[]{:S(2)}) copy-start(bf16[8,384,256]{2,1,0:T(8,128)(2,1)S(1)} %collective-permute-done.13.refs_3_.refs_0_) | copy-start | bytes 4718596
  89.6 2.9 %collective-permute-start.21 = (bf16[2304,256]{1,0:T(8,128)(2,1)S(1)}, bf16[2304,256]{1,0:T(8,128)(2,1)S(1)}, u32[]{:S(2)}, u32[]{:S(2)}) collective-permute-start(bf16[2304,256]{1,0:T(8,128)(2,1)S(1)} %constant_dynamic-update-slice_fusion.refs_0_), channel_id=1, source_target_pairs={{0,1},{1,0},{2,3},{3,2},{4,5},{5,4},{6,7},{7,6},{8,9},{9,8},{10,11... | collective-permute-start | bytes 3538952 | tf_op jit(solution)/shard_map/ppermute | solution.py:52
  89.7 9.9 %collective-permute-start.17 = (bf16[384,384]{1,0:T(8,128)(2,1)S(1)}, bf16[384,384]{1,0:T(8,128)(2,1)S(1)}, u32[]{:S(2)}, u32[]{:S(2)}) collective-permute-start(bf16[384,384]{1,0:T(8,128)(2,1)S(1)} %last_half.1.refs_0_), channel_id=1, source_target_pairs={{0,12},{1,13},{2,14},{3,15},{4,0},{5,1},{6,2},{7,3},{8,4},{9,5},{1... | collective-permute-start | bytes 884744 | tf_op jit(solution)/shard_map/ppermute | solution.py:52
  89.9 11.1 %collective-permute-start.16 = (bf16[384,384]{1,0:T(8,128)(2,1)S(1)}, bf16[384,384]{1,0:T(8,128)(2,1)S(1)}, u32[]{:S(2)}, u32[]{:S(2)}) collective-permute-start(bf16[384,384]{1,0:T(8,128)(2,1)S(1)} %last_half.1.refs_0_), channel_id=1, source_target_pairs={{0,4},{1,5},{2,6},{3,7},{4,8},{5,9},{6,10},{7,11},{8,12},{9,13},{1... | collective-permute-start | bytes 884744 | tf_op jit(solution)/shard_map/ppermute | solution.py:52
  94.7 9.1 %collective-permute-start.22 = (bf16[96,1024]{1,0:T(8,128)(2,1)S(1)}, bf16[96,1024]{1,0:T(8,128)(2,1)S(1)}, u32[]{:S(2)}, u32[]{:S(2)}) collective-permute-start(bf16[96,1024]{1,0:T(8,128)(2,1)S(1)} %get-tuple-element.104), channel_id=1, source_target_pairs={{0,12},{1,13},{2,14},{3,15},{4,0},{5,1},{6,2},{7,3},{8,4},{9,5},{1... | collective-permute-start | bytes 589832 | tf_op jit(solution)/shard_map/ppermute | solution.py:52
  95.4 14.0 %collective-permute-start.23 = (bf16[96,1024]{1,0:T(8,128)(2,1)S(1)}, bf16[96,1024]{1,0:T(8,128)(2,1)S(1)}, u32[]{:S(2)}, u32[]{:S(2)}) collective-permute-start(bf16[96,1024]{1,0:T(8,128)(2,1)S(1)} %get-tuple-element.105), channel_id=1, source_target_pairs={{0,4},{1,5},{2,6},{3,7},{4,8},{5,9},{6,10},{7,11},{8,12},{9,13},{1... | collective-permute-start | bytes 589832 | tf_op jit(solution)/shard_map/ppermute | solution.py:52
  96.8 12.7 %collective-permute-start.24 = (bf16[96,1024]{1,0:T(8,128)(2,1)S(1)}, bf16[96,1024]{1,0:T(8,128)(2,1)S(1)}, u32[]{:S(2)}, u32[]{:S(2)}) collective-permute-start(bf16[96,1024]{1,0:T(8,128)(2,1)S(1)} %get-tuple-element.106), channel_id=1, source_target_pairs={{0,8},{1,9},{2,10},{3,11},{4,12},{5,13},{6,14},{7,15},{8,0},{9,1},... | collective-permute-start | bytes 589832 | tf_op jit(solution)/shard_map/ppermute | solution.py:52
  99.6 11.3 %collective-permute-start.19 = (bf16[192,384]{1,0:T(8,128)(2,1)S(1)}, bf16[192,384]{1,0:T(8,128)(2,1)S(1)}, u32[]{:S(2)}, u32[]{:S(2)}) collective-permute-start(bf16[192,384]{1,0:T(8,128)(2,1)S(1)} %slice.17), channel_id=1, source_target_pairs={{0,12},{1,13},{2,14},{3,15},{4,0},{5,1},{6,2},{7,3},{8,4},{9,5},{1... | collective-permute-start | bytes 442376 | tf_op jit(solution)/shard_map/ppermute | solution.py:52
  101.1 10.8 %collective-permute-start.18 = (bf16[192,384]{1,0:T(8,128)(2,1)S(1)}, bf16[192,384]{1,0:T(8,128)(2,1)S(1)}, u32[]{:S(2)}, u32[]{:S(2)}) collective-permute-start(bf16[192,384]{1,0:T(8,128)(2,1)S(1)} %slice.16), channel_id=1, source_target_pairs={{0,4},{1,5},{2,6},{3,7},{4,8},{5,9},{6,10},{7,11},{8,12},{9,13},{1... | collective-permute-start | bytes 442376 | tf_op jit(solution)/shard_map/ppermute | solution.py:52
  114.7 0.9 copy-start.6
  115.6 5.7 %copy-start.12 = (s32[32,2]{0,1:T(2,128)S(1)}, s32[32,2]{0,1:T(2,128)}, u32[]{:S(2)}) copy-start(s32[32,2]{0,1:T(2,128)} %param.20) | copy-start | bytes 772
  115.6 5.7 %copy-start.13 = (f32[32,2]{0,1:T(2,128)S(1)}, f32[32,2]{0,1:T(2,128)}, u32[]{:S(2)}) copy-start(f32[32,2]{0,1:T(2,128)} %param.21) | copy-start | bytes 772
  115.6 19.4 %all-to-all-start.1 = ((bf16[32,24,512]{2,1,0:T(8,128)(2,1)}), bf16[32,24,512]{2,1,0:T(8,128)(2,1)}, u32[]{:S(2)}, u32[]{:S(2)}) async-start(bf16[32,24,512]{2,1,0:T(8,128)(2,1)} %copy-done.6), calls=%async_computation.1 | async-start | bytes 1572864 | tf_op jit(solution)/shard_map/all_to_all | solution.py:579
  122.1 0.7 copy-start.7
  122.7 1.1 copy-start.1
  123.9 1.4 %copy-start.3 = (bf16[8,384,256]{2,1,0:T(8,128)(2,1)S(1)}, bf16[8,384,256]{2,1,0:T(8,128)(2,1)}, u32[]{:S(2)}) copy-start(bf16[8,384,256]{2,1,0:T(8,128)(2,1)} %copy-done.2) | copy-start | bytes 4718596
  125.3 1.3 copy-start.5
  135.0 0.9 copy-start.8
